TPU v7x, 32 devices: a whole 2x2x4 slice. The times are simulated.
32 devices in a mesh: seq: 2 (over x), ctx: 8 (over z, y), wsh: 2 (over core).
Axes of the slice: x: 2, y: 2, z: 4, core: 2. Of those that a mesh axis runs over, the one named last changes fastest.
Arguments:
- hidden_in: bfloat16 [2048, 4, 1024], P('ctx', ('seq', 'wsh')), may hold values from -6 to 6
- cotangent: bfloat16 [2048, 4, 1024], P('ctx', ('seq', 'wsh')), may hold values from -6 to 6
- query_key_value_weight: bfloat16 [1024, 2048], P('wsh'), may hold values from -0.1875 to 0.1875
- w_o: bfloat16 [1024, 1024], P('wsh'), may hold values from -3 to 3
- w_gu: bfloat16 [1024, 9216], P('wsh'), may hold values from -0.1875 to 0.1875
- w_down: bfloat16 [4608, 1024], P('wsh'), may hold values from -0.09375 to 0.09375
- g_attn: bfloat16 [1024], replicated, may hold values from 0.5 to 1.5
- g_ffn: bfloat16 [1024], replicated, may hold values from 0.5 to 1.5
- g_q: bfloat16 [64], replicated, may hold values from 0.5 to 1.5
- key_norm_gain: bfloat16 [64], replicated, may hold values from 0.5 to 1.5
- a_qkv: bfloat16 [8, 1024, 48], replicated, may hold values from -0.1875 to 0.1875
- b_q: bfloat16 [8, 16, 1024], replicated, may hold values from -0.75 to 0.75
- key_up_weight: bfloat16 [8, 16, 512], replicated, may hold values from -0.75 to 0.75
- value_up_weight: bfloat16 [8, 16, 512], replicated, may hold values from -0.75 to 0.75
- a_o: bfloat16 [8, 1024, 16], replicated, may hold values from -0.1875 to 0.1875
- b_o: bfloat16 [8, 16, 1024], replicated, may hold values from -6 to 6
- a_gu: bfloat16 [8, 1024, 32], replicated, may hold values from -0.1875 to 0.1875
- b_gu: bfloat16 [8, 2, 16, 4608], replicated, may hold values from -0.75 to 0.75
- a_down: bfloat16 [8, 4608, 16], replicated, may hold values from -0.09375 to 0.09375
- b_down: bfloat16 [8, 16, 1024], replicated, may hold values from -0.75 to 0.75
- set_index: int32 [4], replicated, may hold values from 0 to 7
- stretch_order: int32 [4, 16], P(('seq', 'wsh')), may hold values from 0 to 15, as said below
Outputs:
- layer_out: float32 [2048, 4, 1024], P('ctx', ('seq', 'wsh'))
- input_grad: float32 [2048, 4, 1024], P('ctx', ('seq', 'wsh'))
- grad_a_qkv: float32 [8, 1024, 48], replicated
- grad_b_q: float32 [8, 16, 1024], replicated
- grad_b_k: float32 [8, 16, 512], replicated
- grad_b_v: float32 [8, 16, 512], replicated
- grad_a_o: float32 [8, 1024, 16], replicated
- grad_b_o: float32 [8, 16, 1024], replicated
- grad_a_gu: float32 [8, 1024, 32], replicated
- grad_b_gu: float32 [8, 2, 16, 4608], replicated
- grad_a_down: float32 [8, 4608, 16], replicated
- grad_b_down: float32 [8, 16, 1024], replicated
Inputs may be any that keep to these rules, and one draw needn't show every extreme that they name: `stretch_order`: in each row, slots 2 j and 2 j + 1 hold stretches c and 15 - c, where c over j = 0 to 7 is a permutation of 0 to 7 drawn for each sequence.
All inputs are finite; a program needn't handle non-finite values.
Results may differ from a plain program's by a relative error of at most 0.023.
Values may be sent and summed in bfloat16 or wider, within the bound.
No kernel may reach another device: no remote copies, remote signals or barrier semaphores. Data moves between devices by JAX's collectives and lax.ppermute only.
A program may use at most 384 MiB of HBM per device.

v0:
```python
import math

import jax
import jax.numpy as jnp
from jax import lax
from jax.sharding import PartitionSpec as P

QUERY_HEADS = 16
KEY_VALUE_HEADS = 8
HEAD_SIZE = 64
FF = 4608
ADAPTER_RANK = 16
ADAPTER_SETS = 8
CH = 128


epsilon = 1e-05
rope_base = 1000000.0
masked = -1e30
precise = lax.Precision.HIGHEST


def norm_forward(inputs, gain_vec):
    inverse = lax.rsqrt(jnp.mean(inputs * inputs, axis=-1, keepdims=True) + epsilon)
    return (inputs * inverse * gain_vec, inverse)


def norm_backward(inputs, inverse, gain_vec, upstream):
    weighted = upstream * gain_vec
    return inverse * weighted - inputs * inverse**3 * jnp.mean(
        inputs * weighted, axis=-1, keepdims=True
    )


def rope_tables(positions):
    half_width = HEAD_SIZE // 2
    frequency = jnp.exp(
        -math.log(rope_base) * 2.0 * jnp.arange(half_width, dtype=jnp.float32) / HEAD_SIZE
    )
    angle_grid = positions.astype(jnp.float32)[..., None] * frequency
    return (jnp.cos(angle_grid)[:, :, None, :], jnp.sin(angle_grid)[:, :, None, :])


def rotary_apply(inputs, cosine_table, sine_table):
    half_width = inputs.shape[-1] // 2
    lower_half = inputs[..., :half_width]
    upper_half = inputs[..., half_width:]
    return jnp.concatenate(
        [
            lower_half * cosine_table - upper_half * sine_table,
            upper_half * cosine_table + lower_half * sine_table,
        ],
        axis=-1,
    )


def stretch_positions(order_table, first_row, row_total):
    row_ids = first_row + jnp.arange(row_total, dtype=jnp.int32)
    slot_ids = row_ids // CH
    onehot = slot_ids[:, None] == jnp.arange(order_table.shape[1], dtype=jnp.int32)[None, :]
    stretch_ids = jnp.sum(jnp.where(onehot[:, None, :], order_table[None, :, :], 0), axis=-1)
    return stretch_ids * CH + (row_ids % CH)[:, None]


def contract(form, left, right):
    return jnp.einsum(form, left, right, preferred_element_type=jnp.float32)


def per_device(
    hidden_in,
    cotangent,
    query_key_value_weight,
    w_o,
    w_gu,
    w_down,
    g_attn,
    g_ffn,
    g_q,
    key_norm_gain,
    a_qkv,
    b_q,
    key_up_weight,
    value_up_weight,
    a_o,
    b_o,
    a_gu,
    b_gu,
    a_down,
    b_down,
    set_index,
    stretch_order,
):
    count_of_rows, sequence_count, model_width = hidden_in.shape
    token_count = count_of_rows * sequence_count
    q_width = QUERY_HEADS * HEAD_SIZE
    key_total_width = KEY_VALUE_HEADS * HEAD_SIZE
    heads_per_group = QUERY_HEADS // KEY_VALUE_HEADS
    score_scale = 1.0 / math.sqrt(HEAD_SIZE)
    cycle_size = lax.axis_size("ctx")
    ctx_index = lax.axis_index("ctx")
    group_index = lax.axis_index(("seq", "wsh"))
    own_sets = lax.dynamic_slice_in_dim(set_index, group_index * sequence_count, sequence_count)
    set_ids = jnp.arange(ADAPTER_SETS, dtype=jnp.int32)
    own_onehot = own_sets[:, None] == set_ids[None, :]
    selector = own_onehot.astype(jnp.bfloat16)

    def select(table):
        return contract("bs,s...->b...", selector, table).astype(jnp.bfloat16)

    pick_a_qkv = select(a_qkv)
    pick_b_q = select(b_q)
    pick_b_k = select(key_up_weight)
    pick_b_v = select(value_up_weight)
    pick_a_o = select(a_o)
    pick_b_o = select(b_o)
    pick_a_gu = select(a_gu)
    pick_b_gu = select(b_gu)
    pick_a_down = select(a_down)
    pick_b_down = select(b_down)
    gain_attn = g_attn.astype(jnp.float32)
    gain_ffn = g_ffn.astype(jnp.float32)
    gain_query = g_q.astype(jnp.float32)
    gain_key = key_norm_gain.astype(jnp.float32)
    full_qkv, full_o, full_gu, full_down = (
        lax.all_gather(query_key_value_weight, "wsh", axis=0, tiled=True),
        lax.all_gather(w_o, "wsh", axis=0, tiled=True),
        lax.all_gather(w_gu, "wsh", axis=0, tiled=True),
        lax.all_gather(w_down, "wsh", axis=0, tiled=True),
    )
    query_pos = stretch_positions(stretch_order, ctx_index * count_of_rows, count_of_rows)
    cosine_table, sine_table = rope_tables(query_pos)
    inputs = hidden_in.astype(jnp.float32)
    normed_attn, inverse_attn = norm_forward(inputs, gain_attn)
    low_attn = normed_attn.astype(jnp.bfloat16)
    rank_qkv = contract("rbd,bdk->rbk", low_attn, pick_a_qkv).astype(jnp.bfloat16)
    joined = jnp.dot(
        low_attn.reshape(token_count, model_width), full_qkv, preferred_element_type=jnp.float32
    ).reshape(count_of_rows, sequence_count, -1)
    q_raw = joined[..., :q_width] + contract("rbk,bkn->rbn", rank_qkv[..., :ADAPTER_RANK], pick_b_q)
    key_unnormed = joined[..., q_width : q_width + key_total_width] + contract(
        "rbk,bkn->rbn", rank_qkv[..., ADAPTER_RANK : 2 * ADAPTER_RANK], pick_b_k
    )
    value_unnormed = joined[..., q_width + key_total_width :] + contract(
        "rbk,bkn->rbn", rank_qkv[..., 2 * ADAPTER_RANK :], pick_b_v
    )
    q_heads_raw = q_raw.reshape(count_of_rows, sequence_count, QUERY_HEADS, HEAD_SIZE)
    key_heads_unnormed = key_unnormed.reshape(
        count_of_rows, sequence_count, KEY_VALUE_HEADS, HEAD_SIZE
    )
    q_normed, q_inverse = norm_forward(q_heads_raw, gain_query)
    k_normed, k_inverse = norm_forward(key_heads_unnormed, gain_key)
    query_low = (
        rotary_apply(q_normed, cosine_table, sine_table)
        .astype(jnp.bfloat16)
        .reshape(count_of_rows, sequence_count, KEY_VALUE_HEADS, heads_per_group, HEAD_SIZE)
    )
    key_low = (
        rotary_apply(k_normed, cosine_table, sine_table)
        .astype(jnp.bfloat16)
        .reshape(count_of_rows, sequence_count, key_total_width)
    )
    value_low = value_unnormed.astype(jnp.bfloat16)
    kv_local = jnp.stack([key_low, value_low])

    def visible(key_pos):
        return (key_pos.T[:, None, :] <= query_pos.T[:, :, None])[:, None, None, :, :]

    statistic_shape = (sequence_count, KEY_VALUE_HEADS, heads_per_group, count_of_rows)
    initial = (
        jnp.full(statistic_shape, masked, jnp.float32),
        jnp.zeros(statistic_shape, jnp.float32),
        jnp.zeros(statistic_shape + (HEAD_SIZE,), jnp.float32),
    )
    key_value_piece = lax.all_gather(kv_local, "ctx", axis=1, tiled=True)
    rows_per_piece = key_value_piece.shape[1]
    allowed = visible(stretch_positions(stretch_order, jnp.int32(0), rows_per_piece))
    block_of_keys = key_value_piece[0].reshape(
        rows_per_piece, sequence_count, KEY_VALUE_HEADS, HEAD_SIZE
    )
    block_of_values = key_value_piece[1].reshape(
        rows_per_piece, sequence_count, KEY_VALUE_HEADS, HEAD_SIZE
    )

    def accumulate(state_in):
        run_max, run_sum, run_out = state_in
        scores = jnp.where(
            allowed, contract("rbgjd,kbgd->bgjrk", query_low, block_of_keys) * score_scale, masked
        )
        new_max = jnp.maximum(run_max, jnp.max(scores, axis=-1))
        weights = jnp.where(allowed, jnp.exp(scores - new_max[..., None]), 0.0)
        run_sum = jnp.sum(weights, axis=-1)
        run_out = contract("bgjrk,kbgd->bgjrd", weights.astype(jnp.bfloat16), block_of_values)
        return (new_max, run_sum, run_out)

    run_max, run_sum, run_out = lax.cond(
        jnp.any(allowed), accumulate, lambda state_in: state_in, initial
    )
    log_sum = run_max + jnp.log(run_sum)
    attn_out = run_out / run_sum[..., None]
    attn_low = (
        jnp.transpose(attn_out, (3, 0, 1, 2, 4))
        .reshape(count_of_rows, sequence_count, q_width)
        .astype(jnp.bfloat16)
    )
    rank_o = contract("rbm,bmk->rbk", attn_low, pick_a_o).astype(jnp.bfloat16)
    mixed = jnp.dot(
        attn_low.reshape(token_count, q_width), full_o, preferred_element_type=jnp.float32
    ).reshape(count_of_rows, sequence_count, model_width) + contract(
        "rbk,bkn->rbn", rank_o, pick_b_o
    )
    residual = inputs + mixed
    normed_ffn, inverse_ffn = norm_forward(residual, gain_ffn)
    low_ffn = normed_ffn.astype(jnp.bfloat16)
    rank_gu = contract("rbd,bdk->rbk", low_ffn, pick_a_gu).astype(jnp.bfloat16)
    joined_ffn = jnp.dot(
        low_ffn.reshape(token_count, model_width), full_gu, preferred_element_type=jnp.float32
    ).reshape(count_of_rows, sequence_count, 2 * FF)
    gate_pre = joined_ffn[..., :FF] + contract(
        "rbk,bkn->rbn", rank_gu[..., :ADAPTER_RANK], pick_b_gu[:, 0]
    )
    up_pre = joined_ffn[..., FF:] + contract(
        "rbk,bkn->rbn", rank_gu[..., ADAPTER_RANK:], pick_b_gu[:, 1]
    )
    sigmoid_gate = jax.nn.sigmoid(gate_pre)
    silu_gate = gate_pre * sigmoid_gate
    hidden_low = (silu_gate * up_pre).astype(jnp.bfloat16)
    rank_down = contract("rbf,bfk->rbk", hidden_low, pick_a_down).astype(jnp.bfloat16)
    down_out = jnp.dot(
        hidden_low.reshape(token_count, FF), full_down, preferred_element_type=jnp.float32
    ).reshape(count_of_rows, sequence_count, model_width) + contract(
        "rbk,bkn->rbn", rank_down, pick_b_down
    )
    layer_out = residual + down_out
    back_qkv, back_o, back_gu, back_down = (full_qkv, full_o, full_gu, full_down)
    upstream = cotangent.astype(jnp.float32)
    rank_down_grad = contract("rbn,bkn->rbk", cotangent, pick_b_down).astype(jnp.bfloat16)
    grad_b_down = contract("rbk,rbn->bkn", rank_down, cotangent)
    grad_a_down = contract("rbf,rbk->bfk", hidden_low, rank_down_grad)
    hidden_grad = contract(
        "tn,fn->tf", cotangent.reshape(token_count, model_width), back_down
    ).reshape(count_of_rows, sequence_count, FF) + contract(
        "rbk,bfk->rbf", rank_down_grad, pick_a_down
    )
    gate_grad = (
        hidden_grad * up_pre * sigmoid_gate * (1.0 + gate_pre * (1.0 - sigmoid_gate))
    ).astype(jnp.bfloat16)
    up_grad = (hidden_grad * silu_gate).astype(jnp.bfloat16)
    rank_gu_grad = jnp.concatenate(
        [
            contract("rbn,bkn->rbk", gate_grad, pick_b_gu[:, 0]),
            contract("rbn,bkn->rbk", up_grad, pick_b_gu[:, 1]),
        ],
        axis=-1,
    ).astype(jnp.bfloat16)
    grad_b_gu = jnp.stack(
        [
            contract("rbk,rbn->bkn", rank_gu[..., :ADAPTER_RANK], gate_grad),
            contract("rbk,rbn->bkn", rank_gu[..., ADAPTER_RANK:], up_grad),
        ],
        axis=1,
    )
    grad_a_gu = contract("rbd,rbk->bdk", low_ffn, rank_gu_grad)
    joined_grad = jnp.concatenate([gate_grad, up_grad], axis=-1).reshape(token_count, 2 * FF)
    ffn_in_grad = contract("tf,df->td", joined_grad, back_gu).reshape(
        count_of_rows, sequence_count, model_width
    ) + contract("rbk,bdk->rbd", rank_gu_grad, pick_a_gu)
    residual_grad = upstream + norm_backward(residual, inverse_ffn, gain_ffn, ffn_in_grad)
    mixed_grad = residual_grad.astype(jnp.bfloat16)
    rank_o_grad = contract("rbn,bkn->rbk", mixed_grad, pick_b_o).astype(jnp.bfloat16)
    grad_b_o = contract("rbk,rbn->bkn", rank_o, mixed_grad)
    grad_a_o = contract("rbm,rbk->bmk", attn_low, rank_o_grad)
    attention_gradient = (
        contract("tn,mn->tm", mixed_grad.reshape(token_count, model_width), back_o).reshape(
            count_of_rows, sequence_count, q_width
        )
        + contract("rbk,bmk->rbm", rank_o_grad, pick_a_o)
    ).astype(jnp.bfloat16)
    output_gradient = attention_gradient.reshape(
        count_of_rows, sequence_count, KEY_VALUE_HEADS, heads_per_group, HEAD_SIZE
    )
    delta = jnp.sum(
        jnp.transpose(output_gradient.astype(jnp.float32), (1, 2, 3, 0, 4)) * attn_out, axis=-1
    )

    def key_grads(key_value_piece, first_row, q_grad):
        rows_per_piece = key_value_piece.shape[1]
        allowed = visible(stretch_positions(stretch_order, first_row, rows_per_piece))
        block_of_keys = key_value_piece[0].reshape(
            rows_per_piece, sequence_count, KEY_VALUE_HEADS, HEAD_SIZE
        )
        block_of_values = key_value_piece[1].reshape(
            rows_per_piece, sequence_count, KEY_VALUE_HEADS, HEAD_SIZE
        )

        def compute(q_in):
            scores = contract("rbgjd,kbgd->bgjrk", query_low, block_of_keys) * score_scale
            probs = jnp.where(allowed, jnp.exp(scores - log_sum[..., None]), 0.0)
            prob_grad = contract("rbgjd,kbgd->bgjrk", output_gradient, block_of_values)
            score_grad = (probs * (prob_grad - delta[..., None])).astype(jnp.bfloat16)
            value_grad = contract("bgjrk,rbgjd->kbgd", probs.astype(jnp.bfloat16), output_gradient)
            key_grad = contract("bgjrk,rbgjd->kbgd", score_grad, query_low) * score_scale
            q_out = q_in + contract("bgjrk,kbgd->bgjrd", score_grad, block_of_keys) * score_scale
            paired_gradient = jnp.stack(
                [
                    key_grad.reshape(rows_per_piece, sequence_count, key_total_width),
                    value_grad.reshape(rows_per_piece, sequence_count, key_total_width),
                ]
            )
            return (q_out, paired_gradient)

        def skip(q_in):
            return (
                q_in,
                jnp.zeros((2, rows_per_piece, sequence_count, key_total_width), jnp.float32),
            )

        return lax.cond(jnp.any(allowed), compute, skip, q_grad)

    q_zero = jnp.zeros(statistic_shape + (HEAD_SIZE,), jnp.float32)
    span = math.gcd(cycle_size, max(1, 512 // count_of_rows))
    whole = lax.all_gather(kv_local, "ctx", axis=1, tiled=True)

    def visit(step_index, state_now):
        q_grad, all_grad = state_now
        block_row = step_index * (span * count_of_rows)
        block = lax.dynamic_slice_in_dim(whole, block_row, span * count_of_rows, 1)
        q_grad, fresh = key_grads(block, block_row, q_grad)
        all_grad = lax.dynamic_update_slice_in_dim(all_grad, fresh, block_row, 1)
        return (q_grad, all_grad)

    q_grad, all_grad = lax.fori_loop(
        0, cycle_size // span, visit, (q_zero, jnp.zeros(whole.shape, jnp.float32))
    )
    paired_gradient = lax.psum_scatter(
        all_grad.astype(jnp.bfloat16), "ctx", scatter_dimension=1, tiled=True
    ).astype(jnp.float32)
    q_grad_rows = jnp.transpose(q_grad, (3, 0, 1, 2, 4)).reshape(
        count_of_rows, sequence_count, QUERY_HEADS, HEAD_SIZE
    )
    q_pre_grad = (
        norm_backward(
            q_heads_raw, q_inverse, gain_query, rotary_apply(q_grad_rows, cosine_table, -sine_table)
        )
        .astype(jnp.bfloat16)
        .reshape(count_of_rows, sequence_count, q_width)
    )
    k_pre_grad = (
        norm_backward(
            key_heads_unnormed,
            k_inverse,
            gain_key,
            rotary_apply(
                paired_gradient[0].reshape(
                    count_of_rows, sequence_count, KEY_VALUE_HEADS, HEAD_SIZE
                ),
                cosine_table,
                -sine_table,
            ),
        )
        .astype(jnp.bfloat16)
        .reshape(count_of_rows, sequence_count, key_total_width)
    )
    v_pre_grad = paired_gradient[1].astype(jnp.bfloat16)
    rank_qkv_grad = jnp.concatenate(
        [
            contract("rbn,bkn->rbk", q_pre_grad, pick_b_q),
            contract("rbn,bkn->rbk", k_pre_grad, pick_b_k),
            contract("rbn,bkn->rbk", v_pre_grad, pick_b_v),
        ],
        axis=-1,
    ).astype(jnp.bfloat16)
    grad_b_q = contract("rbk,rbn->bkn", rank_qkv[..., :ADAPTER_RANK], q_pre_grad)
    grad_b_k = contract("rbk,rbn->bkn", rank_qkv[..., ADAPTER_RANK : 2 * ADAPTER_RANK], k_pre_grad)
    grad_b_v = contract("rbk,rbn->bkn", rank_qkv[..., 2 * ADAPTER_RANK :], v_pre_grad)
    grad_a_qkv = contract("rbd,rbk->bdk", low_attn, rank_qkv_grad)
    qkv_grad = jnp.concatenate([q_pre_grad, k_pre_grad, v_pre_grad], axis=-1).reshape(
        token_count, -1
    )
    attn_in_grad = contract("tn,dn->td", qkv_grad, back_qkv).reshape(
        count_of_rows, sequence_count, model_width
    ) + contract("rbk,bdk->rbd", rank_qkv_grad, pick_a_qkv)
    input_grad = residual_grad + norm_backward(inputs, inverse_attn, gain_attn, attn_in_grad)
    seq_grads = [
        grad_a_qkv,
        grad_b_q,
        grad_b_k,
        grad_b_v,
        grad_a_o,
        grad_b_o,
        grad_a_gu,
        grad_b_gu,
        grad_a_down,
        grad_b_down,
    ]
    own_weights = own_onehot.astype(jnp.float32)
    set_terms = [
        jnp.tensordot(own_weights, term, axes=(0, 0), precision=precise) for term in seq_grads
    ]
    totals = lax.psum(
        (
            set_terms[0],
            set_terms[1],
            set_terms[2],
            set_terms[3],
            set_terms[4],
            set_terms[5],
            set_terms[6],
            set_terms[7],
            set_terms[8],
            set_terms[9],
        ),
        ("seq", "ctx", "wsh"),
    )
    return (
        layer_out,
        input_grad,
        totals[0],
        totals[1],
        totals[2],
        totals[3],
        totals[4],
        totals[5],
        totals[6],
        totals[7],
        totals[8],
        totals[9],
    )


def solution(mesh):
    in_specs = (
        P("ctx", ("seq", "wsh"), None),
        P("ctx", ("seq", "wsh"), None),
        P("wsh", None),
        P("wsh", None),
        P("wsh", None),
        P("wsh", None),
        P(),
        P(),
        P(),
        P(),
        P(),
        P(),
        P(),
        P(),
        P(),
        P(),
        P(),
        P(),
        P(),
        P(),
        P(),
        P(("seq", "wsh"), None),
    )
    out_specs = (
        P("ctx", ("seq", "wsh"), None),
        P("ctx", ("seq", "wsh"), None),
        P(),
        P(),
        P(),
        P(),
        P(),
        P(),
        P(),
        P(),
        P(),
        P(),
    )
    return jax.shard_map(
        per_device, mesh=mesh, in_specs=in_specs, out_specs=out_specs, check_vma=False
    )
```

profile of v0, /device:TPU:1, one launch (start us, length us, event | category | flops | bytes accessed | tf_op | source)
XLA Modules:
  0.0 684.9 jit_solution(10754608495025306522)
XLA Ops:
  9.4 2.3 fusion.105
  18.4 7.3 %all-gather.6.cloned.1.call-done = bf16[1024,2048]{1,0:T(8,128)(2,1)} async-done(((bf16[512,2048]{1,0:T(8,128)(2,1)}), bf16[1024,2048]{1,0:T(8,128)(2,1)}) %all-gather.6.cloned.1.call-update) | async-done | bytes 4194320 | tf_op jit(solution)/shard_map/all_gather | solution.py:125
  25.8 3.5 convolution_bitcast_fusion.8
  34.0 1.8 copy.100
  37.3 1.9 pad_maximum_fusion.2
  43.7 2.5 fusion.132
  48.4 2.7 fusion.120
  51.1 1.8 copy.156
  52.8 3.4 fusion.53
  57.0 11.0 %fusion.69 = bf16[1,4608,16]{0,1,2:T(8,128)(2,1)} fusion(bf16[8,4608,16]{1,2,0:T(8,128)(2,1)S(1)} %copy-done.30, s32[]{:T(128)} %bitcast.47), kind=kOutput, calls=%fused_computation.121 | convolution fusion | flops 1179656 | bytes 1327108 | tf_op jit(solution)/shard_map/bs,s...->b.../dot_general | solution.py:66
  67.9 15.1 %copy.162 = bf16[1,4608,16]{1,2,0:T(8,128)(2,1)S(1)} copy(bf16[1,4608,16]{0,1,2:T(8,128)(2,1)} %fusion.69) | data formatting | bytes 294912 | tf_op jit(solution)/shard_map/bs,s...->b.../dot_general | solution.py:66
  87.7 1.8 fusion.58
  92.6 11.5 %convolution_bitcast_fusion.5 = f32[256,1,4608]{2,0,1:T(8,128)} fusion(bf16[4608,1024]{1,0:T(8,128)(2,1)} %all-gather.14.cloned.1.call-done, bf16[256,1,1024]{2,0,1:T(8,128)(2,1)S(1)} %copy-done.26), kind=kOutput, calls=%fused_computation.63 | convolution fusion | flops 2415919104 | bytes 14680064 | tf_op jit(solution)/shard_map/tn,fn->tf/dot_general | solution.py:66
  104.2 22.2 %all-gather.8.cloned.1.call-done = bf16[2,2048,1,512]{3,1,2,0:T(8,128)(2,1)} async-done(((bf16[2,256,1,512]{3,1,2,0:T(8,128)(2,1)}), bf16[2,2048,1,512]{3,1,2,0:T(8,128)(2,1)}) %all-gather.8.cloned.1.call-update) | async-done | bytes 4194320 | tf_op jit(solution)/shard_map/all_gather | solution.py:174
  126.4 63.5 %conditional.2 = (f32[1,8,2,256]{3,2,1,0:T(2,128)}, f32[1,8,2,256,64]{3,4,2,1,0:T(8,128)S(1)}, f32[1,8,2,256]{3,2,1,0:T(2,128)}) conditional(s32[]{:T(128)} %convert_element_type.271, () %tuple.55, (s32[2048]{0:T(1024)S(1)}, s32[256]{0:T(256)S(1)}, bf16[2,2048,1,512]{3,1,2,0:T(8,128)(2,1)}, bf16[256,1,8,2,64]{0,4,3,2,1:T(8,128)(2,1)}) %tuple.139), branch_computations={%region_6.7_spmd.clone, %region_7.10_spmd.clone} | conditional | flops 2257063936 | bytes 125461528 | solution.py:195
  127.4 6.3 copy.168
  133.7 3.0 fusion.194
  136.7 19.1 %fusion.24 = (f32[8,2,256]{2,1,0:T(2,128)S(1)}, f32[8,2048,256,2]{2,1,3,0:T(8,128)}) fusion(pred[256,2048]{0,1:T(8,128)(4,1)S(1)} %broadcast_compare_fusion.1, bf16[2048,8,64,1]{0,2,3,1:T(8,128)(2,1)S(1)} %bitcast.564, bf16[256,1,8,2,64]{0,4,3,2,1:T(8,128)(2,1)} %get-tuple-element.435), kind=kOutput, calls=%fused_computation.44 | convolution fusion | flops 1098903552 | bytes 36716544 | tf_op jit(solution)/shard_map/cond/branch_1_fun/rbgjd,kbgd->bgjrk/dot_general | solution.py:66
  155.8 18.4 %fusion.26 = f32[8,2,256]{2,1,0:T(2,128)} fusion(f32[8,2048,256,2]{2,1,3,0:T(8,128)} %get-tuple-element.476, f32[8,2,256]{2,1,0:T(2,128)S(1)} %broadcast_maximum_fusion, pred[256,2048]{0,1:T(8,128)(4,1)S(1)} %broadcast_compare_fusion.1), kind=kLoop, calls=%fused_computation.46 | loop fusion | flops 41938944 | bytes 34111488 | tf_op jit(solution)/shard_map/cond/branch_1_fun/reduce_sum | solution.py:191
  175.5 14.2 %fusion.31 = f32[1,8,2,256,64]{3,4,2,1,0:T(8,128)S(1)} fusion(bf16[2048,8,64,1]{0,2,3,1:T(8,128)(2,1)S(1)} %bitcast.576, f32[8,2048,256,2]{2,1,3,0:T(8,128)} %get-tuple-element.476, f32[8,2,256]{2,1,0:T(2,128)S(1)} %broadcast_maximum_fusion, pred[256,2048]{0,1:T(8,128)(4,1)S(1)} %broadcast_compare_fusion.1), kind=kOutput, calls=%fused_computation.50 | convolution fusion | flops 1115684864 | bytes 37240832 | tf_op jit(solution)/shard_map/cond/branch_1_fun/bgjrk,kbgd->bgjrd/dot_general | solution.py:66
  189.9 6.3 copy.112
  198.0 2.3 convolution_bitcast_fusion.10
  204.6 9.0 %convolution_bitcast_fusion.1 = f32[256,1,9216]{2,0,1:T(8,128)S(1)} fusion(bf16[256,1024]{1,0:T(8,128)(2,1)S(1)} %fusion.107, bf16[1024,9216]{1,0:T(8,128)(2,1)} %all-gather.12.cloned.1.call-done), kind=kOutput, calls=%fused_computation.59 | convolution fusion | flops 4831838208 | bytes 28835840 | tf_op jit(solution)/shard_map/dot_general | solution.py:215
  215.3 5.6 multiply_convert_fusion.1
  224.3 11.4 %multiply_reduce_fusion.1 = (f32[256]{0:T(256)S(1)}, f32[256,1,1024]{2,0,1:T(8,128)}) fusion(f32[256,1,1024]{2,0,1:T(8,128)S(1)} %get-tuple-element.510, f32[1024]{0:T(1024)S(1)} %copy-done.85, f32[256,1,1024]{2,0,1:T(8,128)} %convolution_bitcast_fusion.14, bf16[1024,9216]{1,0:T(8,128)(2,1)} %all-gather.12.cloned.1.call-done, ...), kind=kOutput, calls=%fused_computation.165 | convolution fusion | flops 4842323968 | bytes 26743808 | tf_op jit(solution)/shard_map/tf,df->td/dot_general | solution.py:66
  235.8 1.8 subtract_add_fusion
  239.8 2.0 copy.111
  243.1 2.3 broadcast_in_dim.147.clone
  245.5 68.6 %while.20 = (s32[]{:T(128)}, f32[1,8,2,256,64]{3,4,2,1,0:T(8,128)S(1)}, bf16[2,2048,1,512]{3,1,2,0:T(8,128)(2,1)}, s32[1,16]{1,0:T(1,128)S(1)}, s32[256,1]{0,1:T...) while((s32[]{:T(128)}, ...), condition=%wide.region_18.19_spmd, body=%wide.region_13.18_spmd.sunk | while | flops 1365154304 | bytes 53412716 | solution.py:331
  247.3 13.9 %conditional.4 = (f32[1,8,2,256,64]{3,4,2,1,0:T(8,128)S(1)}, bf16[2,512,1,512]{1,3,2,0:T(8,128)(2,1)S(1)}) conditional(s32[]{:T(128)} %convert_element_type.457, f32[1,8,2,256,64]{3,4,2,1,0:T(8,128)S(1)} %get-tuple-element.605, (s32[512]{0:T(512)S(1)}, s32[256]{0:T(256)S(1)}, bf16[2,2048,1,512]{1,3,2,0:T(8,128)(2,1)}, s32[]{:T(128)}, ...), branch_computations={%region_16.16_spmd, %region_17.17_spmd} | conditional | flops 1364852736 | bytes 49204260 | solution.py:317
  248.6 2.3 fusion.16
  251.1 3.9 fusion.6
  255.1 2.4 fusion.12
  257.5 2.8 fusion.7
  264.4 13.9 %conditional.4 = (f32[1,8,2,256,64]{3,4,2,1,0:T(8,128)S(1)}, bf16[2,512,1,512]{1,3,2,0:T(8,128)(2,1)S(1)}) conditional(s32[]{:T(128)} %convert_element_type.457, f32[1,8,2,256,64]{3,4,2,1,0:T(8,128)S(1)} %get-tuple-element.605, (s32[512]{0:T(512)S(1)}, s32[256]{0:T(256)S(1)}, bf16[2,2048,1,512]{1,3,2,0:T(8,128)(2,1)}, s32[]{:T(128)}, ...), branch_computations={%region_16.16_spmd, %region_17.17_spmd} | conditional | flops 1364852736 | bytes 49204260 | solution.py:317
  265.7 2.3 fusion.16
  268.2 3.9 fusion.6
  272.2 2.4 fusion.12
  274.6 2.8 fusion.7
  281.6 13.9 %conditional.4 = (f32[1,8,2,256,64]{3,4,2,1,0:T(8,128)S(1)}, bf16[2,512,1,512]{1,3,2,0:T(8,128)(2,1)S(1)}) conditional(s32[]{:T(128)} %convert_element_type.457, f32[1,8,2,256,64]{3,4,2,1,0:T(8,128)S(1)} %get-tuple-element.605, (s32[512]{0:T(512)S(1)}, s32[256]{0:T(256)S(1)}, bf16[2,2048,1,512]{1,3,2,0:T(8,128)(2,1)}, s32[]{:T(128)}, ...), branch_computations={%region_16.16_spmd, %region_17.17_spmd} | conditional | flops 1364852736 | bytes 49204260 | solution.py:317
  282.9 2.3 fusion.16
  285.4 3.9 fusion.6
  289.3 2.4 fusion.12
  291.7 2.8 fusion.7
  298.7 13.9 %conditional.4 = (f32[1,8,2,256,64]{3,4,2,1,0:T(8,128)S(1)}, bf16[2,512,1,512]{1,3,2,0:T(8,128)(2,1)S(1)}) conditional(s32[]{:T(128)} %convert_element_type.457, f32[1,8,2,256,64]{3,4,2,1,0:T(8,128)S(1)} %get-tuple-element.605, (s32[512]{0:T(512)S(1)}, s32[256]{0:T(256)S(1)}, bf16[2,2048,1,512]{1,3,2,0:T(8,128)(2,1)}, s32[]{:T(128)}, ...), branch_computations={%region_16.16_spmd, %region_17.17_spmd} | conditional | flops 1364852736 | bytes 49204260 | solution.py:317
  300.0 2.3 fusion.16
  302.5 3.9 fusion.6
  306.4 2.4 fusion.12
  308.8 2.8 fusion.7
  324.6 2.2 convolution_bitcast_fusion.6
  326.8 2.2 convolution_bitcast_fusion.7
  329.1 2.3 subtract_convert_fusion
  339.6 2.8 broadcast_multiply_fusion
  342.3 59.8 %reduce-scatter.2.cloned.1.call-done = bf16[2,256,1,512]{3,1,2,0:T(8,128)(2,1)} async-done(((bf16[2,2048,1,512]{3,1,2,0:T(8,128)(2,1)}), bf16[2,256,1,512]{3,1,2,0:T(8,128)(2,1)}) %reduce-scatter.2.cloned.1.call-update) | async-done | bytes 524304 | tf_op jit(solution)/shard_map/reduce_scatter | solution.py:334
  407.7 2.0 copy.122
  409.7 2.0 copy.119
  411.8 1.8 subtract_convert_fusion.1
  420.0 6.2 convolution_bitcast_fusion.16
  426.6 2.0 copy.124
  431.4 2.0 copy.125
  433.5 228.8 %all-reduce.3.cloned.1.call-done = (f32[8,1024,48]{1,2,0:T(8,128)}, f32[8,16,1024]{2,1,0:T(8,128)}, f32[8,16,512]{2,1,0:T(8,128)}, f32[8,16,512]{2,1,0:T(8,128)}...) async-done(((f32[8,1024,48]{1,2,0:T(8,128)}, ...) | async-done | bytes 12320784 | tf_op jit(solution)/shard_map/psum | solution.py:399
  662.3 2.9 copy.253
  665.2 2.1 copy.254
  672.2 2.4 copy.260
  (389 shorter events, 106.4 us)
Async XLA Ops:
  7.2 45.6 %copy-start = (bf16[8,2,16,4608]{3,2,1,0:T(8,128)(2,1)S(1)}, bf16[8,2,16,4608]{3,2,1,0:T(8,128)(2,1)}, u32[]{:S(2)}) copy-start(bf16[8,2,16,4608]{3,2,1,0:T(8,128)(2,1)} %param.45) | copy-start | bytes 7077892
  7.3 18.5 %all-gather.6.cloned.1.call-start = ((), (), s32[]{:S(2)}) async-start(), calls=%async_computation.1 | async-start | bytes 6291456 | tf_op jit(solution)/shard_map/all_gather | solution.py:125
  8.0 84.6 %all-gather.14.cloned.1.call-start = ((), (), s32[]{:S(2)}) async-start(), calls=%async_computation.5 | async-start | bytes 14155776 | tf_op jit(solution)/shard_map/all_gather | solution.py:128
  8.7 117.7 %all-gather.8.cloned.1.call-start = ((), (), s32[]{:S(2)}) async-start(), calls=%async_computation.2 | async-start | bytes 4718592 | tf_op jit(solution)/shard_map/all_gather | solution.py:174
  11.8 14.0 %copy-start.39 = (bf16[1,1024,48]{2,1,0:T(8,128)(2,1)}, bf16[1,1024,48]{2,1,0:T(8,128)(2,1)S(1)}, u32[]{:S(2)}) copy-start(bf16[1,1024,48]{2,1,0:T(8,128)(2,1)S(1)} %copy.139) | copy-start | bytes 294916
  11.8 14.0 %copy-start.83 = (f32[1024]{0:T(1024)}, f32[1024]{0:T(1024)S(1)}, u32[]{:S(2)}) copy-start(f32[1024]{0:T(1024)S(1)} %convert_element_type.272) | copy-start | bytes 12292
  11.9 20.7 %copy-start.95 = (f32[64]{0:T(128)}, f32[64]{0:T(128)S(1)}, u32[]{:S(2)}) copy-start(f32[64]{0:T(128)S(1)} %convert_element_type.279) | copy-start | bytes 772
  12.8 13.0 %copy-start.92 = (f32[256]{0:T(256)}, f32[256]{0:T(256)S(1)}, u32[]{:S(2)}) copy-start(f32[256]{0:T(256)S(1)} %get-tuple-element.500) | copy-start | bytes 3076
  14.3 27.1 %copy-start.86 = (s32[256]{0:T(256)}, s32[256]{0:T(256)S(1)}, u32[]{:S(2)}) copy-start(s32[256]{0:T(256)S(1)} %get-tuple-element.470) | copy-start | bytes 3076
  15.1 18.1 %copy-start.41 = (f32[256,32]{0,1:T(8,128)}, f32[256,32]{0,1:T(8,128)S(1)}, u32[]{:S(2)}) copy-start(f32[256,32]{0,1:T(8,128)S(1)} %get-tuple-element.498) | copy-start | bytes 98308
  15.1 18.1 %copy-start.50 = (f32[256,32]{0,1:T(8,128)}, f32[256,32]{0,1:T(8,128)S(1)}, u32[]{:S(2)}) copy-start(f32[256,32]{0,1:T(8,128)S(1)} %get-tuple-element.497) | copy-start | bytes 98308
  16.7 15.2 %copy-start.65 = (bf16[1,16,512]{2,0,1:T(2,128)(2,1)}, bf16[1,16,512]{2,0,1:T(2,128)(2,1)S(1)}, u32[]{:S(2)}) copy-start(bf16[1,16,512]{2,0,1:T(2,128)(2,1)S(1)} %fusion.140) | copy-start | bytes 49156
  18.4 17.4 %copy-start.67 = (bf16[1,16,512]{2,0,1:T(2,128)(2,1)}, bf16[1,16,512]{2,0,1:T(2,128)(2,1)S(1)}, u32[]{:S(2)}) copy-start(bf16[1,16,512]{2,0,1:T(2,128)(2,1)S(1)} %fusion.138) | copy-start | bytes 49156
  31.6 8.7 %copy-start.23 = (f32[256,1,512]{2,0,1:T(8,128)}, f32[256,1,512]{2,0,1:T(8,128)S(1)}, u32[]{:S(2)}) copy-start(f32[256,1,512]{2,0,1:T(8,128)S(1)} %fusion.66) | copy-start | bytes 1572868
  31.8 8.5 %copy-start.18 = (f32[256,1,512]{0,2,1:T(8,128)}, f32[256,1,512]{0,2,1:T(8,128)S(1)}, u32[]{:S(2)}) copy-start(f32[256,1,512]{0,2,1:T(8,128)S(1)} %copy.98) | copy-start | bytes 1572868
  39.1 158.8 %all-gather.10.cloned.1.call-start = ((), (), s32[]{:S(2)}) async-start(), calls=%async_computation.3 | async-start | bytes 3145728 | tf_op jit(solution)/shard_map/all_gather | solution.py:126
  39.7 8.1 %copy-start.97 = (bf16[1024]{0:T(1024)(128)(2,1)S(1)}, bf16[1024]{0:T(1024)(128)(2,1)}, u32[]{:S(2)}) copy-start(bf16[1024]{0:T(1024)(128)(2,1)} %param.35) | copy-start | bytes 6148
  39.7 164.8 %all-gather.12.cloned.1.call-start = ((), (), s32[]{:S(2)}) async-start(), calls=%async_computation.4 | async-start | bytes 28311552 | tf_op jit(solution)/shard_map/all_gather | solution.py:127
  40.3 361.8 %reduce-scatter.2.cloned.1.call-start = ((), (), s32[]{:S(2)}) async-start(), calls=%async_computation.6 | async-start | bytes 4718592 | tf_op jit(solution)/shard_map/reduce_scatter | solution.py:334
  40.7 16.3 %copy-start.30 = (bf16[8,4608,16]{1,2,0:T(8,128)(2,1)S(1)}, bf16[8,4608,16]{1,2,0:T(8,128)(2,1)}, u32[]{:S(2)}) copy-start(bf16[8,4608,16]{1,2,0:T(8,128)(2,1)} %param.46) | copy-start | bytes 3538948
  67.9 15.2 %copy-start.90 = (s32[256]{0:T(256)S(1)}, s32[256]{0:T(256)}, u32[]{:S(2)}) copy-start(s32[256]{0:T(256)} %get-tuple-element.501) | copy-start | bytes 3076
  67.9 15.8 %copy-start.57 = (bf16[8,16,1024]{2,1,0:T(8,128)(2,1)S(1)}, bf16[8,16,1024]{2,1,0:T(8,128)(2,1)}, u32[]{:S(2)}) copy-start(bf16[8,16,1024]{2,1,0:T(8,128)(2,1)} %param.39) | copy-start | bytes 786436
  67.9 16.6 %copy-start.58 = (bf16[8,16,1024]{2,1,0:T(8,128)(2,1)S(1)}, bf16[8,16,1024]{2,1,0:T(8,128)(2,1)}, u32[]{:S(2)}) copy-start(bf16[8,16,1024]{2,1,0:T(8,128)(2,1)} %param.43) | copy-start | bytes 786436
  67.9 18.1 %copy-start.59 = (bf16[8,16,1024]{2,1,0:T(8,128)(2,1)S(1)}, bf16[8,16,1024]{2,1,0:T(8,128)(2,1)}, u32[]{:S(2)}) copy-start(bf16[8,16,1024]{2,1,0:T(8,128)(2,1)} %param.47) | copy-start | bytes 786436
  67.9 18.9 %copy-start.26 = (bf16[256,1,1024]{2,0,1:T(8,128)(2,1)S(1)}, bf16[256,1,1024]{2,0,1:T(8,128)(2,1)}, u32[]{:S(2)}) copy-start(bf16[256,1,1024]{2,0,1:T(8,128)(2,1)} %param.29) | copy-start | bytes 1572868
  83.1 132.2 %copy-start.44 = (bf16[1,4608,16]{1,2,0:T(8,128)(2,1)}, bf16[1,4608,16]{1,2,0:T(8,128)(2,1)S(1)}, u32[]{:S(2)}) copy-start(bf16[1,4608,16]{1,2,0:T(8,128)(2,1)S(1)} %copy.162) | copy-start | bytes 442372
  83.1 8.3 %copy-start.98 = (f32[64]{0:T(128)S(1)}, f32[64]{0:T(128)}, u32[]{:S(2)}) copy-start(f32[64]{0:T(128)} %convert_element_type.285) | copy-start | bytes 772
  83.1 8.5 %copy-start.42 = (f32[256,32]{0,1:T(8,128)S(1)}, f32[256,32]{0,1:T(8,128)}, u32[]{:S(2)}) copy-start(f32[256,32]{0,1:T(8,128)} %copy-done.41) | copy-start | bytes 98308
  83.1 8.5 %copy-start.51 = (f32[256,32]{0,1:T(8,128)S(1)}, f32[256,32]{0,1:T(8,128)}, u32[]{:S(2)}) copy-start(f32[256,32]{0,1:T(8,128)} %copy-done.50) | copy-start | bytes 98308
  84.5 6.2 copy-start.54
  89.5 14.7 %copy-start.8 = (f32[256,1,1024]{2,0,1:T(8,128)}, f32[256,1,1024]{2,0,1:T(8,128)S(1)}, u32[]{:S(2)}) copy-start(f32[256,1,1024]{2,0,1:T(8,128)S(1)} %fusion.58) | copy-start | bytes 3145732
  89.8 14.3 %copy-start.6 = (f32[256,1,1024]{0,2,1:T(8,128)}, f32[256,1,1024]{0,2,1:T(8,128)S(1)}, u32[]{:S(2)}) copy-start(f32[256,1,1024]{0,2,1:T(8,128)S(1)} %copy.102) | copy-start | bytes 3145732
  92.6 33.8 %copy-start.74 = (s32[2048]{0:T(1024)S(1)}, s32[2048]{0:T(1024)}, u32[]{:S(2)}) copy-start(s32[2048]{0:T(1024)} %copy-done.73) | copy-start | bytes 24580
  92.6 33.8 %copy-start.87 = (s32[256]{0:T(256)S(1)}, s32[256]{0:T(256)}, u32[]{:S(2)}) copy-start(s32[256]{0:T(256)} %copy-done.86) | copy-start | bytes 3076
  189.9 7.2 %copy-start.34 = (bf16[1,1024,16]{2,1,0:T(8,128)(2,1)S(1)}, bf16[1,1024,16]{2,1,0:T(8,128)(2,1)}, u32[]{:S(2)}) copy-start(bf16[1,1024,16]{2,1,0:T(8,128)(2,1)} %copy.150) | copy-start | bytes 98308
  201.6 34.2 %copy-start.4 = (f32[256,1,1024]{2,0,1:T(8,128)}, f32[256,1,1024]{2,0,1:T(8,128)S(1)}, u32[]{:S(2)}) copy-start(f32[256,1,1024]{2,0,1:T(8,128)S(1)} %get-tuple-element.510) | copy-start | bytes 3145732
  203.1 10.5 %copy-start.13 = (bf16[256,1024]{1,0:T(8,128)(2,1)}, bf16[256,1024]{1,0:T(8,128)(2,1)S(1)}, u32[]{:S(2)}) copy-start(bf16[256,1024]{1,0:T(8,128)(2,1)S(1)} %fusion.107) | copy-start | bytes 1572868
  204.5 9.9 %copy-start.63 = (bf16[256,1,32]{0,2,1:T(8,128)(2,1)}, bf16[256,1,32]{0,2,1:T(8,128)(2,1)S(1)}, u32[]{:S(2)}) copy-start(bf16[256,1,32]{0,2,1:T(8,128)(2,1)S(1)} %fusion.73) | copy-start | bytes 49156
  204.5 9.1 %copy-start.33 = (bf16[1,2,16,4608]{3,2,1,0:T(8,128)(2,1)S(1)}, bf16[1,2,16,4608]{3,2,1,0:T(8,128)(2,1)}, u32[]{:S(2)}) copy-start(bf16[1,2,16,4608]{3,2,1,0:T(8,128)(2,1)} %copy.220) | copy-start | bytes 884740
  224.3 11.4 %copy-start.89 = (f32[256]{0:T(256)S(1)}, f32[256]{0:T(256)}, u32[]{:S(2)}) copy-start(f32[256]{0:T(256)} %copy-done.88) | copy-start | bytes 3076
  224.3 11.4 %copy-start.94 = (f32[256]{0:T(256)S(1)}, f32[256]{0:T(256)}, u32[]{:S(2)}) copy-start(f32[256]{0:T(256)} %get-tuple-element.502) | copy-start | bytes 3076
  224.3 13.2 %copy-start.56 = (bf16[1,16,1024]{2,0,1:T(2,128)(2,1)S(1)}, bf16[1,16,1024]{2,0,1:T(2,128)(2,1)}, u32[]{:S(2)}) copy-start(bf16[1,16,1024]{2,0,1:T(2,128)(2,1)} %fusion.134) | copy-start | bytes 98308
  238.7 6.8 copy-start.69
  238.7 6.8 copy-start.80
  245.5 69.0 %copy-start.101 = (bf16[64]{0:T(256)(128)(2,1)S(1)}, bf16[64]{0:T(256)(128)(2,1)}, u32[]{:S(2)}) copy-start(bf16[64]{0:T(256)(128)(2,1)} %param.37) | copy-start | bytes 388
  245.5 69.6 %copy-start.103 = (bf16[64]{0:T(256)(128)(2,1)S(1)}, bf16[64]{0:T(256)(128)(2,1)}, u32[]{:S(2)}) copy-start(bf16[64]{0:T(256)(128)(2,1)} %param.36) | copy-start | bytes 388
  245.5 70.8 %copy-start.72 = (f32[256,8]{0,1:T(8,128)S(1)}, f32[256,8]{0,1:T(8,128)}, u32[]{:S(2)}) copy-start(f32[256,8]{0,1:T(8,128)} %copy-done.71) | copy-start | bytes 24580
  314.2 348.1 %all-reduce.3.cloned.1.call-start = ((), (), s32[]{:S(2)}) async-start(), calls=%async_computation.7 | async-start | bytes 24641536 | tf_op jit(solution)/shard_map/psum | solution.py:399
  316.4 21.5 %copy-start.81 = (f32[8]{0:T(128)}, f32[8]{0:T(128)S(1)}, u32[]{:S(2)}) copy-start(f32[8]{0:T(128)S(1)} %fusion.168) | copy-start | bytes 100
  321.9 7.1 %copy-start.9 = (f32[256,1,1024]{2,0,1:T(8,128)S(1)}, f32[256,1,1024]{2,0,1:T(8,128)}, u32[]{:S(2)}) copy-start(f32[256,1,1024]{2,0,1:T(8,128)} %copy-done.8) | copy-start | bytes 3145732
  339.6 65.8 %copy-start.19 = (f32[256,1,512]{0,2,1:T(8,128)S(1)}, f32[256,1,512]{0,2,1:T(8,128)}, u32[]{:S(2)}) copy-start(f32[256,1,512]{0,2,1:T(8,128)} %copy-done.18) | copy-start | bytes 1572868
  342.3 69.4 %copy-start.24 = (f32[256,1,512]{2,0,1:T(8,128)S(1)}, f32[256,1,512]{2,0,1:T(8,128)}, u32[]{:S(2)}) copy-start(f32[256,1,512]{2,0,1:T(8,128)} %copy-done.23) | copy-start | bytes 1572868
  403.2 11.3 %copy-start.66 = (bf16[1,16,512]{2,0,1:T(2,128)(2,1)S(1)}, bf16[1,16,512]{2,0,1:T(2,128)(2,1)}, u32[]{:S(2)}) copy-start(bf16[1,16,512]{2,0,1:T(2,128)(2,1)} %copy-done.65) | copy-start | bytes 49156
  403.2 11.4 %copy-start.68 = (bf16[1,16,512]{2,0,1:T(2,128)(2,1)S(1)}, bf16[1,16,512]{2,0,1:T(2,128)(2,1)}, u32[]{:S(2)}) copy-start(bf16[1,16,512]{2,0,1:T(2,128)(2,1)} %copy-done.67) | copy-start | bytes 49156
  404.2 11.5 %copy-start.22 = (bf16[256,1,1024]{2,0,1:T(8,128)(2,1)S(1)}, bf16[256,1,1024]{2,0,1:T(8,128)(2,1)}, u32[]{:S(2)}) copy-start(bf16[256,1,1024]{2,0,1:T(8,128)(2,1)} %param.28) | copy-start | bytes 1572868
  405.4 11.4 %copy-start.82 = (f32[8]{0:T(128)S(1)}, f32[8]{0:T(128)}, u32[]{:S(2)}) copy-start(f32[8]{0:T(128)} %copy-done.81) | copy-start | bytes 100
  406.9 11.3 %copy-start.31 = (bf16[2,256,1,512]{3,1,2,0:T(8,128)(2,1)S(1)}, bf16[2,256,1,512]{3,1,2,0:T(8,128)(2,1)}, u32[]{:S(2)}) copy-start(bf16[2,256,1,512]{3,1,2,0:T(8,128)(2,1)} %reduce-scatter.2.cloned.1.call-done) | copy-start | bytes 1572868
  419.9 6.3 copy-start.5
  420.0 6.3 copy-start.53
  662.3 6.6 copy-start.60
  662.3 7.4 %copy-start.48 = (f32[8,1024,16]{1,2,0:T(8,128)S(1)}, f32[8,1024,16]{1,2,0:T(8,128)}, u32[]{:S(2)}) copy-start(f32[8,1024,16]{1,2,0:T(8,128)} %get-tuple-element.638) | copy-start | bytes 1572868
  662.3 8.1 %copy-start.47 = (f32[8,16,1024]{2,1,0:T(8,128)S(1)}, f32[8,16,1024]{2,1,0:T(8,128)}, u32[]{:S(2)}) copy-start(f32[8,16,1024]{2,1,0:T(8,128)} %get-tuple-element.639) | copy-start | bytes 1572868
  662.3 8.9 %copy-start.38 = (f32[8,1024,32]{1,2,0:T(8,128)S(1)}, f32[8,1024,32]{1,2,0:T(8,128)}, u32[]{:S(2)}) copy-start(f32[8,1024,32]{1,2,0:T(8,128)} %get-tuple-element.640) | copy-start | bytes 3145732
  662.3 9.9 %copy-start.25 = (f32[8,2,16,4608]{3,2,1,0:T(8,128)S(1)}, f32[8,2,16,4608]{3,2,1,0:T(8,128)}, u32[]{:S(2)}) copy-start(f32[8,2,16,4608]{3,2,1,0:T(8,128)} %get-tuple-element.641) | copy-start | bytes 14155780
  (49 other events, 173.9 us)
Sparse Core Ops, SparseCore 0:
  9.6 16.1 all-gather.5
  27.3 23.0 all-gather.13
  53.2 73.1 all-gather.7
  127.8 10.3 all-gather.9
  139.6 34.9 all-gather.11
  314.3 87.8 reduce-scatter.1
  420.1 242.1 all-reduce.2
where the time goes:
time: 693 us; the launch traced here: 685 us
  waiting for transfers between devices  321 us (46%)
  matrix products  190 us (27%)
  local copies, waits for them, and re-layouts  93.8 us (14%)
  other arithmetic  59.5 us (9%)
  between operations  16.5 us (2%)
    psum x1, waiting for transfers between devices, per_device(): lax.psum((set_terms[0], set_terms[1], set_terms[2], set_terms[3], set_ter...  229 us
    dot_general x69, matrix products, contract(): return jnp.einsum(form, left, right, preferred_element_type=jnp.float32)  169 us
    reduce_scatter x1, waiting for transfers between devices, per_device(): lax.psum_scatter(all_grad.astype(jnp.bfloat16), 'ctx', scatter_dimension=...  59.8 us
    unnamed x224, local copies, waits for them, and re-layouts  24.4 us
    all_gather x1, waiting for transfers between devices, per_device(): key_value_piece = lax.all_gather(kv_local, 'ctx', axis=1, tiled=True)  22.2 us
    dot_general x5, local copies, waits for them, and re-layouts, contract(): return jnp.einsum(form, left, right, preferred_element_type=jnp.float32)  19.5 us
    reduce_sum x1, other arithmetic, accumulate(): run_sum = jnp.sum(weights, axis=-1)  18.4 us
  transfers between devices with their start and end apart: 7, of which 4 were waited for; matrix products, arithmetic and copies ran while one was open for 29% of the time, Pallas kernels for 0%

commit v1 on v0

v1 whole, which is shorter than its diff:
```python
import functools
import math

import jax
import jax.numpy as jnp
import numpy as np
from jax import lax
from jax.experimental import pallas as pl
from jax.experimental.pallas import tpu as pltpu
from jax.sharding import PartitionSpec as P

QUERY_HEADS = 16
KEY_VALUE_HEADS = 8
HEAD_SIZE = 64
FF = 4608
ADAPTER_RANK = 16
ADAPTER_SETS = 8
CH = 128

epsilon = 1e-05
rope_base = 1000000.0

TOK = 4 * CH
PAIR = 2 * HEAD_SIZE
QW = QUERY_HEADS * HEAD_SIZE // 2
KW = KEY_VALUE_HEADS * HEAD_SIZE // 2
EW = QW + 2 * KW
GROUPS = KEY_VALUE_HEADS // 2
HF = FF // 2
TF = 256
NT = HF // TF
R = ADAPTER_RANK
VMEM = 56 * 1024 * 1024
f32 = jnp.float32
bf16 = jnp.bfloat16


def mm(a, b):
    return lax.dot_general(a, b, (((1,), (0,)), ((), ())), preferred_element_type=f32)


def mm_nt(a, b):
    return lax.dot_general(a, b, (((1,), (1,)), ((), ())), preferred_element_type=f32)


def params(sem=("arbitrary",)):
    return pltpu.CompilerParams(dimension_semantics=sem, vmem_limit_bytes=VMEM)


def cost(flops, nbytes):
    return pl.CostEstimate(flops=int(flops), bytes_accessed=int(nbytes), transcendentals=0)


def whole(shape):
    return pl.BlockSpec(shape, lambda *_: (0,) * len(shape))


def split_dot(x, ones):
    hi = x.astype(bf16)
    lo = (x - hi.astype(f32)).astype(bf16)
    return mm(hi, ones) + mm(lo, ones)


def head_mean(x, ones):
    width = ones.shape[0]
    parts = [
        split_dot(x[:, i : i + width], ones) for i in range(0, x.shape[1], width)
    ]
    return jnp.concatenate(parts, axis=1) * (1.0 / HEAD_SIZE)


def lane_iota(shape):
    return lax.broadcasted_iota(jnp.int32, shape, len(shape) - 1)


def half_turn(x):
    width = x.shape[1]
    near = pltpu.roll(x, HEAD_SIZE // 2, 1)
    far = pltpu.roll(x, width - HEAD_SIZE // 2, 1)
    return jnp.where(lane_iota(x.shape) % HEAD_SIZE < HEAD_SIZE // 2, far, near)


def widen(table, width):
    return jnp.concatenate([table] * (width // table.shape[1]), axis=1)


def put_masked(x, ref, index):
    left = lane_iota((x.shape[0], PAIR)) < HEAD_SIZE
    for g in range(GROUPS):
        tile = x[:, g * PAIR : (g + 1) * PAIR]
        turned = pltpu.roll(tile, HEAD_SIZE, 1)
        if g % 2 == 0:
            pair = (jnp.where(left, tile, 0.0), jnp.where(left, turned, 0.0))
        else:
            pair = (jnp.where(left, 0.0, turned), jnp.where(left, 0.0, tile))
        for j in range(2):
            index(ref, g, j, pair[j].astype(bf16))


def qkv_kernel(
    sc, mine, other, cos, sin, w_own, w_rec, gain, a_t, b_q, b_k, b_v, g_qk, ones,
    x_out, u_out, raw_out, qm_out, kv_out, u_s, b_s,
):
    core = sc[0]
    blk = pl.program_id(0)
    x = jnp.where(blk == core, mine[...], other[...])
    half = x.shape[0] // 2
    x_out[0, 0] = x[:half]
    x_out[1, 0] = x[half:]
    x = x.astype(f32)
    inv = lax.rsqrt(jnp.mean(x * x, axis=1, keepdims=True) + epsilon)
    u = (x * inv * gain[...]).astype(bf16)
    u_s[...] = u
    u_out[0, 0] = u[:half]
    u_out[1, 0] = u[half:]
    b_s[...] = jnp.zeros_like(b_s)
    b_s[0:R, 0:QW] = b_q[0]
    b_s[R : 2 * R, QW : QW + KW] = b_k[0]
    b_s[2 * R : 3 * R, QW + KW : EW] = b_v[0]
    depth = w_own.shape[0]
    rank = mm_nt(u, a_t[0]).astype(bf16)
    raw = mm(u_s[:, pl.ds(pl.multiple_of(core * depth, depth), depth)], w_own[...])
    raw += mm(u_s[:, pl.ds(pl.multiple_of((1 - core) * depth, depth), depth)], w_rec[...])
    raw += mm(rank, b_s[...])
    qk = raw[:, : QW + KW]
    raw_out[0, 0] = qk[:half]
    raw_out[1, 0] = qk[half:]
    normed = qk * lax.rsqrt(head_mean(qk * qk, ones[...]) + epsilon) * g_qk[...]
    c = jnp.concatenate([cos[0, 0], cos[1, 0]], axis=0)
    s = jnp.concatenate([sin[0, 0], sin[1, 0]], axis=0)
    turned = normed * widen(c, QW + KW) + half_turn(normed) * widen(s, QW + KW)

    def put(ref, g, j, value):
        ref[g, j, 0, 0] = value[:half]
        ref[g, j, 1, 0] = value[half:]

    put_masked(turned[:, :QW] * (1.0 / math.sqrt(HEAD_SIZE)), qm_out, put)
    kv = jnp.concatenate([turned[:, QW:], raw[:, QW + KW :]], axis=1).astype(bf16)
    kv_out[0, 0] = kv[:half]
    kv_out[1, 0] = kv[half:]


def qkv_call(sc, mine, other, cos, sin, w_own, w_rec, gain, a_t, b_q, b_k, b_v, g_qk, ones):
    rows, width = mine.shape
    depth = w_own.shape[0]

    def out(n, dtype):
        return jax.ShapeDtypeStruct((2, 2, CH, n), dtype)

    def out_spec(n):
        return pl.BlockSpec((2, 1, CH, n), lambda i, s: (0, i, 0, 0))

    return pl.pallas_call(
        qkv_kernel,
        grid_spec=pltpu.PrefetchScalarGridSpec(
            num_scalar_prefetch=1,
            grid=(2,),
            in_specs=[
                whole((rows, width)), whole((rows, width)),
                out_spec(PAIR), out_spec(PAIR),
                whole((depth, EW)), whole((depth, EW)),
                whole((1, width)),
                pl.BlockSpec((1, 3 * R, width), lambda i, s: (s[1], 0, 0)),
                pl.BlockSpec((1, R, QW), lambda i, s: (s[1], 0, s[0])),
                pl.BlockSpec((1, R, KW), lambda i, s: (s[1], 0, s[0])),
                pl.BlockSpec((1, R, KW), lambda i, s: (s[1], 0, s[0])),
                whole((1, QW + KW)), whole(ones.shape),
            ],
            out_specs=[
                out_spec(width), out_spec(width), out_spec(QW + KW),
                pl.BlockSpec((GROUPS, 2, 2, 1, CH, PAIR), lambda i, s: (0, 0, 0, i, 0, 0)),
                out_spec(2 * KW),
            ],
            scratch_shapes=[pltpu.VMEM((rows, width), bf16), pltpu.VMEM((3 * R, EW), bf16)],
        ),
        out_shape=[
            out(width, bf16), out(width, bf16), out(QW + KW, f32),
            jax.ShapeDtypeStruct((GROUPS, 2, 2, 2, CH, PAIR), bf16), out(2 * KW, bf16),
        ],
        compiler_params=params(),
        cost_estimate=cost(2 * TOK * width * EW, 8e6),
        name="qkv",
    )(sc, mine, other, cos, sin, w_own, w_rec, gain, a_t, b_q, b_k, b_v, g_qk, ones)


def sub_blocks(sc, base, first):
    out = []
    for qb in range(2):
        for kb in range(2):
            if first and qb == kb:
                out.append((qb * CH, kb * CH, True))
                out.append(((2 + qb) * CH, (2 + kb) * CH, True))
            else:
                flag = sc[base + qb * 2 + kb]
                q_at = pl.multiple_of((1 - flag) * (2 * CH) + qb * CH, CH)
                k_at = pl.multiple_of((1 - flag) * (2 * CH) + kb * CH, CH)
                out.append((q_at, k_at, False))
    return out


def attend_kernel(base, first, sc, qm, k, v, *rest):
    if first:
        acc_out, acc, vx = rest
    else:
        acc_in, acc_out, acc, vx = rest
    g = pl.program_id(0)
    acc[...] = jnp.zeros_like(acc)
    vx[:, :PAIR] = v[...]
    vx[:, PAIR:] = jnp.ones_like(v[...])
    high = 2 * CH

    def part(q_at, q_n, k_at, k_n, diagonal):
        rows = pl.ds(q_at, q_n)
        keys = pl.ds(k_at, k_n)
        q2 = jnp.concatenate([qm[0, 0, rows, :], qm[0, 1, rows, :]], axis=0)
        p = jnp.exp(mm_nt(q2, k[keys, :]))
        if diagonal:
            t = lax.broadcasted_iota(jnp.int32, p.shape, 0) % q_n
            p = jnp.where(lane_iota(p.shape) <= t, p, 0.0)
        o = mm(p.astype(bf16), vx[keys, :])
        acc[0, rows, :] += o[:q_n]
        acc[1, rows, :] += o[q_n:]

    part(high, 2 * CH, 0, 2 * CH, False)
    for q_at, k_at, diagonal in sub_blocks(sc, base, first):
        part(q_at, CH, k_at, CH, diagonal)
    left = lane_iota((TOK, PAIR)) < HEAD_SIZE
    even = g % 2 == 0
    o0, o1 = acc[0, :, :PAIR], acc[1, :, :PAIR]
    o0 = jnp.where(even, o0, pltpu.roll(o0, HEAD_SIZE, 1))
    o1 = jnp.where(even, pltpu.roll(o1, HEAD_SIZE, 1), o1)
    o = jnp.where(left, o0, o1)
    norm = jnp.where(left, acc[0, :, PAIR:], acc[1, :, PAIR:])
    if not first:
        o += acc_in[0, :, :PAIR]
        norm += acc_in[0, :, PAIR:]
    acc_out[0, :, :PAIR] = o
    acc_out[0, :, PAIR:] = norm


def attend_call(base, sc, qm, kv, acc):
    first = acc is None
    acc_spec = pl.BlockSpec((1, TOK, 2 * PAIR), lambda g, s: (g, 0, 0))
    return pl.pallas_call(
        functools.partial(attend_kernel, base, first),
        grid_spec=pltpu.PrefetchScalarGridSpec(
            num_scalar_prefetch=1,
            grid=(GROUPS,),
            in_specs=[
                pl.BlockSpec((1, 2, TOK, PAIR), lambda g, s: (g, 0, 0, 0)),
                pl.BlockSpec((TOK, PAIR), lambda g, s: (0, g // 2)),
                pl.BlockSpec((TOK, PAIR), lambda g, s: (0, GROUPS // 2 + g // 2)),
            ]
            + ([] if first else [acc_spec]),
            out_specs=acc_spec,
            scratch_shapes=[
                pltpu.VMEM((2, TOK, 2 * PAIR), f32),
                pltpu.VMEM((TOK, 2 * PAIR), bf16),
            ],
        ),
        out_shape=jax.ShapeDtypeStruct((GROUPS, TOK, 2 * PAIR), f32),
        input_output_aliases={} if first else {4: 0},
        compiler_params=params(),
        cost_estimate=cost(2.4e9, 5e6),
        name="attend",
    )(sc, qm, kv, kv, *([] if first else [acc]))


def project_kernel(sc, acc, w_o, a_o, b_o, pick, ob_out, mix_out, lse_out):
    o = jnp.concatenate([acc[g, :, :PAIR] / acc[g, :, PAIR:] for g in range(GROUPS)], axis=1)
    ob = o.astype(bf16)
    ob_out[...] = ob
    norm = jnp.concatenate([acc[g, :, PAIR:] for g in range(GROUPS)], axis=1)
    lse_out[...] = lax.dot_general(
        pick[...], jnp.log(norm), (((1,), (1,)), ((), ())),
        precision=lax.Precision.HIGHEST, preferred_element_type=f32,
    )
    rank = mm_nt(ob, a_o[0]).astype(bf16)
    mix_out[...] = (mm(ob, w_o[...]) + mm(rank, b_o[0])).astype(bf16)


def project_call(sc, acc, w_o, a_o, b_o, pick):
    width = w_o.shape[1]
    return pl.pallas_call(
        project_kernel,
        grid_spec=pltpu.PrefetchScalarGridSpec(
            num_scalar_prefetch=1,
            grid=(1,),
            in_specs=[
                whole(acc.shape), whole(w_o.shape),
                pl.BlockSpec((1, R, QW), lambda i, s: (s[1], 0, s[0])),
                pl.BlockSpec((1, R, width), lambda i, s: (s[1], 0, 0)),
                whole(pick.shape),
            ],
            out_specs=[whole((TOK, QW)), whole((TOK, width)), whole((2 * GROUPS, TOK))],
        ),
        out_shape=[
            jax.ShapeDtypeStruct((TOK, QW), bf16),
            jax.ShapeDtypeStruct((TOK, width), bf16),
            jax.ShapeDtypeStruct((2 * GROUPS, TOK), f32),
        ],
        compiler_params=params(),
        cost_estimate=cost(2 * TOK * QW * width, 6e6),
        name="project",
    )(sc, acc, w_o, a_o, b_o, pick)


def ffn_kernel(
    sc, x, mix_a, mix_b, ed, gain, wg_own, wu_own, wg_rec, wu_rec, w_d, a_gu, b_gu, a_d, b_d,
    h_out, down_out, du_out, gb_gu, ga_d, gb_d, ga_gu,
    u_s, down_s, du_s, rgu_s, rguT_s, drd_s, drdT_s, rd_s, drgu_s,
):
    i = pl.program_id(0)
    core = sc[0]
    depth = wg_own.shape[0]
    own = pl.ds(pl.multiple_of(core * depth, depth), depth)
    rec = pl.ds(pl.multiple_of((1 - core) * depth, depth), depth)

    @pl.when(i == 0)
    def _():
        h = x[...].astype(f32) + (mix_a[...].astype(f32) + mix_b[...].astype(f32))
        h_out[...] = h
        inv = lax.rsqrt(jnp.mean(h * h, axis=1, keepdims=True) + epsilon)
        u = (h * inv * gain[...]).astype(bf16)
        u_s[...] = u
        rgu_s[...] = mm_nt(u, a_gu[0]).astype(bf16)
        rguT_s[...] = mm_nt(a_gu[0], u).astype(bf16)
        drd_s[...] = mm_nt(ed[...], b_d[0]).astype(bf16)
        drdT_s[...] = mm_nt(b_d[0], ed[...]).astype(bf16)
        down_s[...] = jnp.zeros_like(down_s)
        du_s[...] = jnp.zeros_like(du_s)
        rd_s[...] = jnp.zeros_like(rd_s)
        drgu_s[...] = jnp.zeros_like(drgu_s)

    u_own, u_rec = u_s[:, own], u_s[:, rec]
    gate = mm(u_own, wg_own[...]) + mm(u_rec, wg_rec[...]) + mm(rgu_s[:, :R], b_gu[0, 0])
    up = mm(u_own, wu_own[...]) + mm(u_rec, wu_rec[...]) + mm(rgu_s[:, R:], b_gu[0, 1])
    d_hid = mm_nt(ed[...], w_d[...]) + mm(drd_s[...], a_d[0])
    sig = jax.nn.sigmoid(gate)
    silu = gate * sig
    hid = (silu * up).astype(bf16)
    e_g = (d_hid * up * (sig * (1.0 + gate * (1.0 - sig)))).astype(bf16)
    e_u = (d_hid * silu).astype(bf16)
    down_s[...] += mm(hid, w_d[...])
    rd_s[...] += mm_nt(hid, a_d[0])
    du_s[:, own] += mm_nt(e_g, wg_own[...]) + mm_nt(e_u, wu_own[...])
    du_s[:, rec] += mm_nt(e_g, wg_rec[...]) + mm_nt(e_u, wu_rec[...])
    drgu_s[:, :R] += mm_nt(e_g, b_gu[0, 0])
    drgu_s[:, R:] += mm_nt(e_u, b_gu[0, 1])
    gb_gu[0] = mm(rguT_s[:R], e_g).astype(bf16)
    gb_gu[1] = mm(rguT_s[R:], e_u).astype(bf16)
    ga_d[...] = mm(drdT_s[...], hid).astype(bf16)

    @pl.when(i == pl.num_programs(0) - 1)
    def _():
        rd = rd_s[...].astype(bf16)
        down_out[...] = (down_s[...] + mm(rd, b_d[0])).astype(bf16)
        gb_d[...] = mm(rd_s[...].T.astype(bf16), ed[...]).astype(bf16)
        dr = drgu_s[...].astype(bf16)
        du_out[...] = (du_s[...] + mm(dr, a_gu[0])).astype(bf16)
        ga_gu[...] = mm(drgu_s[...].T.astype(bf16), u_s[...]).astype(bf16)


def ffn_call(sc, x, mix_a, mix_b, ed, gain, w_gu, w_rec, w_d, a_gu, b_gu, a_d, b_d):
    width = x.shape[1]
    depth = w_gu.shape[0]
    return pl.pallas_call(
        ffn_kernel,
        grid_spec=pltpu.PrefetchScalarGridSpec(
            num_scalar_prefetch=1,
            grid=(NT,),
            in_specs=[
                whole((TOK, width)), whole((TOK, width)), whole((TOK, width)), whole((TOK, width)),
                whole((1, width)),
                pl.BlockSpec((depth, TF), lambda i, s: (0, s[0] * NT + i)),
                pl.BlockSpec((depth, TF), lambda i, s: (0, 2 * NT + s[0] * NT + i)),
                pl.BlockSpec((depth, TF), lambda i, s: (0, i)),
                pl.BlockSpec((depth, TF), lambda i, s: (0, NT + i)),
                pl.BlockSpec((TF, width), lambda i, s: (i, 0)),
                pl.BlockSpec((1, 2 * R, width), lambda i, s: (s[1], 0, 0)),
                pl.BlockSpec((1, 2, R, TF), lambda i, s: (s[1], 0, 0, s[0] * NT + i)),
                pl.BlockSpec((1, R, TF), lambda i, s: (s[1], 0, s[0] * NT + i)),
                pl.BlockSpec((1, R, width), lambda i, s: (s[1], 0, 0)),
            ],
            out_specs=[
                whole((TOK, width)), whole((TOK, width)), whole((TOK, width)),
                pl.BlockSpec((2, R, TF), lambda i, s: (0, 0, i)),
                pl.BlockSpec((R, TF), lambda i, s: (0, i)),
                whole((R, width)), whole((2 * R, width)),
            ],
            scratch_shapes=[
                pltpu.VMEM((TOK, width), bf16),
                pltpu.VMEM((TOK, width), f32),
                pltpu.VMEM((TOK, width), f32),
                pltpu.VMEM((TOK, 2 * R), bf16),
                pltpu.VMEM((2 * R, TOK), bf16),
                pltpu.VMEM((TOK, R), bf16),
                pltpu.VMEM((R, TOK), bf16),
                pltpu.VMEM((TOK, R), f32),
                pltpu.VMEM((TOK, 2 * R), f32),
            ],
        ),
        out_shape=[
            jax.ShapeDtypeStruct((TOK, width), f32),
            jax.ShapeDtypeStruct((TOK, width), bf16),
            jax.ShapeDtypeStruct((TOK, width), bf16),
            jax.ShapeDtypeStruct((2, R, HF), bf16),
            jax.ShapeDtypeStruct((R, HF), bf16),
            jax.ShapeDtypeStruct((R, width), bf16),
            jax.ShapeDtypeStruct((2 * R, width), bf16),
        ],
        compiler_params=params(),
        cost_estimate=cost(2 * TOK * HF * width * 6, 2.5e7),
        name="ffn",
    )(sc, x, mix_a, mix_b, ed, gain, w_gu, w_gu, w_rec, w_rec, w_d, a_gu, b_gu, a_d, b_d)


def back_mix_kernel(
    sc, h, ed, du_a, du_b, gain, w_o, a_o, b_o, acc, ob, pick,
    dh_out, dom_out, delta_out, gb_o, ga_o,
):
    hv = h[...]
    inv = lax.rsqrt(jnp.mean(hv * hv, axis=1, keepdims=True) + epsilon)
    w = gain[...] * (du_a[...].astype(f32) + du_b[...].astype(f32))
    dh = ed[...].astype(f32) + inv * w - hv * (
        inv * inv * inv * jnp.mean(hv * w, axis=1, keepdims=True)
    )
    dh_out[...] = dh
    e_o = dh.astype(bf16)
    dr = mm_nt(e_o, b_o[0]).astype(bf16)
    drT = mm_nt(b_o[0], e_o).astype(bf16)
    rT = mm_nt(a_o[0], ob[...]).astype(bf16)
    gb_o[...] = mm(rT, e_o).astype(bf16)
    ga_o[...] = mm(drT, ob[...]).astype(bf16)
    d_o = (mm_nt(e_o, w_o[...]) + mm(dr, a_o[0])).astype(bf16).astype(f32)
    o = jnp.concatenate([acc[g, :, :PAIR] / acc[g, :, PAIR:] for g in range(GROUPS)], axis=1)
    delta_out[...] = lax.dot_general(
        pick[...], d_o * o, (((1,), (1,)), ((), ())),
        precision=lax.Precision.HIGHEST, preferred_element_type=f32,
    )

    def put(ref, g, j, value):
        ref[g, j] = value

    put_masked(d_o, dom_out, put)


def back_mix_call(sc, h, ed, du_a, du_b, gain, w_o, a_o, b_o, acc, ob, pick):
    width = h.shape[1]
    return pl.pallas_call(
        back_mix_kernel,
        grid_spec=pltpu.PrefetchScalarGridSpec(
            num_scalar_prefetch=1,
            grid=(1,),
            in_specs=[
                whole((TOK, width)), whole((TOK, width)), whole((TOK, width)), whole((TOK, width)),
                whole((1, width)), whole(w_o.shape),
                pl.BlockSpec((1, R, QW), lambda i, s: (s[1], 0, s[0])),
                pl.BlockSpec((1, R, width), lambda i, s: (s[1], 0, 0)),
                whole(acc.shape), whole(ob.shape), whole(pick.shape),
            ],
            out_specs=[
                whole((TOK, width)), whole((GROUPS, 2, TOK, PAIR)), whole((2 * GROUPS, TOK)),
                whole((R, width)), whole((R, QW)),
            ],
        ),
        out_shape=[
            jax.ShapeDtypeStruct((TOK, width), f32),
            jax.ShapeDtypeStruct((GROUPS, 2, TOK, PAIR), bf16),
            jax.ShapeDtypeStruct((2 * GROUPS, TOK), f32),
            jax.ShapeDtypeStruct((R, width), bf16),
            jax.ShapeDtypeStruct((R, QW), bf16),
        ],
        compiler_params=params(),
        cost_estimate=cost(2 * TOK * QW * width, 1.2e7),
        name="back_mix",
    )(sc, h, ed, du_a, du_b, gain, w_o, a_o, b_o, acc, ob, pick)


def attend_back_kernel(base, first, has_dq, sc, qm, dom, k, v, lse, delta, *rest):
    if has_dq:
        dq_in, dq_out, dk_out, dv_out, dq, dk, dv, kt = rest
    else:
        dq_out, dk_out, dv_out, dq, dk, dv, kt = rest
    g = pl.program_id(0)
    side = g % 2
    dq[...] = jnp.zeros_like(dq)

    @pl.when(side == 0)
    def _():
        dk[...] = jnp.zeros_like(dk)
        dv[...] = jnp.zeros_like(dv)
        kt[...] = k[...].astype(f32).T.astype(bf16)

    kth = kt.at[pl.ds(pl.multiple_of(side * HEAD_SIZE, HEAD_SIZE), HEAD_SIZE), :]

    def part(q_at, q_n, k_at, k_n, diagonal):
        rows = pl.ds(q_at, q_n)
        keys = pl.ds(k_at, k_n)

        def both(ref):
            return jnp.concatenate([ref[0, 0, rows, :], ref[0, 1, rows, :]], axis=0)

        def line(ref):
            return jnp.concatenate([ref[0, 0:1, rows], ref[0, 1:2, rows]], axis=1)

        q2, do2 = both(qm), both(dom)
        s = mm_nt(k[keys, :], q2)
        p = jnp.exp(s - line(lse))
        if diagonal:
            t = lane_iota(p.shape) % q_n
            p = jnp.where(lax.broadcasted_iota(jnp.int32, p.shape, 0) <= t, p, 0.0)
        dp = mm_nt(v[keys, :], do2)
        ds = (p * (dp - line(delta))).astype(bf16)
        dv[keys, :] += mm(p.astype(bf16), do2)
        dk[keys, :] += mm(ds, q2)
        dqp = mm(kth[:, keys], ds)
        dq[0, :, rows] += dqp[:, :q_n]
        dq[1, :, rows] += dqp[:, q_n:]

    part(2 * CH, 2 * CH, 0, 2 * CH, False)
    for q_at, k_at, diagonal in sub_blocks(sc, base, first):
        part(q_at, CH, k_at, CH, diagonal)
    if has_dq:
        dq_out[0] = dq_in[0] + dq[...]
    else:
        dq_out[0] = dq[...]

    @pl.when(side == 1)
    def _():
        dk_out[...] = dk[...].astype(dk_out.dtype)
        dv_out[...] = dv[...].astype(dv_out.dtype)


def attend_back_call(base, first, sc, qm, dom, kv, lse, delta, dq):
    has_dq = dq is not None
    kind = f32 if first else bf16
    dq_spec = pl.BlockSpec((1, 2, HEAD_SIZE, TOK), lambda g, s: (g, 0, 0, 0))
    row_spec = pl.BlockSpec((1, 2, TOK), lambda g, s: (g, 0, 0))
    pair_spec = pl.BlockSpec((TOK, PAIR), lambda g, s: (0, g // 2))
    return pl.pallas_call(
        functools.partial(attend_back_kernel, base, first, has_dq),
        grid_spec=pltpu.PrefetchScalarGridSpec(
            num_scalar_prefetch=1,
            grid=(GROUPS,),
            in_specs=[
                pl.BlockSpec((1, 2, TOK, PAIR), lambda g, s: (g, 0, 0, 0)),
                pl.BlockSpec((1, 2, TOK, PAIR), lambda g, s: (g, 0, 0, 0)),
                pair_spec,
                pl.BlockSpec((TOK, PAIR), lambda g, s: (0, GROUPS // 2 + g // 2)),
                row_spec, row_spec,
            ]
            + ([dq_spec] if has_dq else []),
            out_specs=[dq_spec, pair_spec, pair_spec],
            scratch_shapes=[
                pltpu.VMEM((2, HEAD_SIZE, TOK), f32),
                pltpu.VMEM((TOK, PAIR), f32),
                pltpu.VMEM((TOK, PAIR), f32),
                pltpu.VMEM((PAIR, TOK), bf16),
            ],
        ),
        out_shape=[
            jax.ShapeDtypeStruct((GROUPS, 2, HEAD_SIZE, TOK), f32),
            jax.ShapeDtypeStruct((TOK, KW), kind),
            jax.ShapeDtypeStruct((TOK, KW), kind),
        ],
        input_output_aliases={7: 0} if has_dq else {},
        compiler_params=params(),
        cost_estimate=cost(6e9, 6e6),
        name="attend_back",
    )(sc, qm, dom, kv, kv, lse, delta, *([dq] if has_dq else []))


def qkv_back_kernel(
    parts, sc, dq, dk, dv, *rest
):
    got = rest[: 2 * parts]
    (raw, cos, sin, g_qk, ones, u, w_own, w_rec, a_t, b_q, b_k, b_v,
     du_out, ga_out, gb_out, e_s, b_s) = rest[2 * parts :]
    core = sc[0]
    d_q = dq[...].T * (1.0 / math.sqrt(HEAD_SIZE))
    d_k, d_v = dk[...], dv[...]
    for n in range(parts):
        d_k = d_k + got[2 * n][...].astype(f32)
        d_v = d_v + got[2 * n + 1][...].astype(f32)
    grad = jnp.concatenate([d_q, d_k], axis=1)
    width = QW + KW
    grad = grad * widen(cos[...], width) - half_turn(grad) * widen(sin[...], width)
    v = raw[...]
    inv = lax.rsqrt(head_mean(v * v, ones[...]) + epsilon)
    w = grad * g_qk[...]
    grad = inv * w - v * (inv * inv * inv) * head_mean(v * w, ones[...])
    e_s[:, :width] = grad.astype(bf16)
    e_s[:, width:] = d_v.astype(bf16)
    b_s[...] = jnp.zeros_like(b_s)
    b_s[0:R, 0:QW] = b_q[0]
    b_s[R : 2 * R, QW:width] = b_k[0]
    b_s[2 * R : 3 * R, width:EW] = b_v[0]
    e = e_s[...]
    dr = mm_nt(e, b_s[...]).astype(bf16)
    drT = mm_nt(b_s[...], e).astype(bf16)
    rT = mm_nt(a_t[0], u[...]).astype(bf16)
    gb = mm(rT, e).astype(bf16)
    gb_out[...] = jnp.concatenate(
        [gb[0:R, 0:QW], gb[R : 2 * R, QW:width], gb[2 * R : 3 * R, width:EW]], axis=1
    )
    ga_out[...] = mm(drT, u[...]).astype(bf16)
    du_out[...] = mm(dr, a_t[0])
    depth = w_own.shape[0]
    du_out[:, pl.ds(pl.multiple_of(core * depth, depth), depth)] += mm_nt(e, w_own[...])
    du_out[:, pl.ds(pl.multiple_of((1 - core) * depth, depth), depth)] += mm_nt(e, w_rec[...])


def qkv_back_call(sc, dq, dk, dv, got, raw, cos, sin, g_qk, ones, u, w_own, w_rec, a_t, b_q, b_k, b_v):
    width = u.shape[1]
    depth = w_own.shape[0]
    parts = len(got) // 2
    return pl.pallas_call(
        functools.partial(qkv_back_kernel, parts),
        grid_spec=pltpu.PrefetchScalarGridSpec(
            num_scalar_prefetch=1,
            grid=(1,),
            in_specs=[whole(dq.shape), whole(dk.shape), whole(dv.shape)]
            + [whole(dk.shape)] * (2 * parts)
            + [
                whole(raw.shape), whole(cos.shape), whole(sin.shape), whole(g_qk.shape),
                whole(ones.shape), whole(u.shape), whole(w_own.shape), whole(w_rec.shape),
                pl.BlockSpec((1, 3 * R, width), lambda i, s: (s[1], 0, 0)),
                pl.BlockSpec((1, R, QW), lambda i, s: (s[1], 0, s[0])),
                pl.BlockSpec((1, R, KW), lambda i, s: (s[1], 0, s[0])),
                pl.BlockSpec((1, R, KW), lambda i, s: (s[1], 0, s[0])),
            ],
            out_specs=[whole((TOK, width)), whole((3 * R, width)), whole((R, EW))],
            scratch_shapes=[pltpu.VMEM((TOK, EW), bf16), pltpu.VMEM((3 * R, EW), bf16)],
        ),
        out_shape=[
            jax.ShapeDtypeStruct((TOK, width), f32),
            jax.ShapeDtypeStruct((3 * R, width), bf16),
            jax.ShapeDtypeStruct((R, EW), bf16),
        ],
        compiler_params=params(),
        cost_estimate=cost(2 * TOK * EW * width, 1.2e7),
        name="qkv_back",
    )(sc, dq, dk, dv, *got, raw, cos, sin, g_qk, ones, u, w_own, w_rec, a_t, b_q, b_k, b_v)


def rope_parts():
    freq = np.exp(-math.log(rope_base) * 2.0 * np.arange(HEAD_SIZE // 2) / HEAD_SIZE)
    angle = np.arange(CH)[:, None] * freq[None, :]
    return freq, np.cos(angle).astype(np.float32), np.sin(angle).astype(np.float32)


def rope_tables(stretches):
    freq, cos_t, sin_t = rope_parts()
    angle = (stretches.astype(f32) * CH)[:, None] * jnp.asarray(freq.astype(np.float32))[None, :]
    cos_a, sin_a = jnp.cos(angle)[:, None, :], jnp.sin(angle)[:, None, :]
    cos = cos_a * cos_t[None] - sin_a * sin_t[None]
    sin = sin_a * cos_t[None] + cos_a * sin_t[None]
    return (
        jnp.concatenate([cos, cos, cos, cos], axis=-1),
        jnp.concatenate([-sin, sin, -sin, sin], axis=-1),
    )


def per_device(
    hidden_in, cotangent, query_key_value_weight, w_o, w_gu, w_down, g_attn, g_ffn, g_q,
    key_norm_gain, a_qkv, b_q, key_up_weight, value_up_weight, a_o, b_o, a_gu, b_gu, a_down,
    b_down, set_index, stretch_order,
):
    rows, _, width = hidden_in.shape
    n_ctx = lax.axis_size("ctx")
    n_seq = lax.axis_size("seq")
    half = n_ctx // 2
    core = lax.axis_index("wsh")
    ctx = lax.axis_index("ctx")
    side = ctx // half
    place = ctx % half
    stays = core == side

    def line(s, p, c):
        return (s * half + p) * 2 + c

    swap_pairs = [
        (line(s, p, c), line(c, p, s))
        for s in range(2) for p in range(half) for c in range(2) if s != c
    ]
    core_pairs = [(0, 1), (1, 0)]

    def swap(v):
        return lax.ppermute(v, ("ctx", "wsh"), swap_pairs)

    def other_core(v):
        return lax.ppermute(v, "wsh", core_pairs)

    def partner(v, k):
        return lax.ppermute(
            v, "ctx", [(s * half + p, s * half + (p ^ k)) for s in range(2) for p in range(half)]
        )

    hid = hidden_in.reshape(rows, width)
    cot = cotangent.reshape(rows, width)
    mine = jnp.where(stays, hid, swap(hid))
    order = jnp.where(stays, stretch_order[0], swap(stretch_order)[0])
    other = other_core(mine)
    cot_mine = jnp.where(stays, cot, swap(cot))
    cot_other = other_core(cot_mine)

    def cols(w, start, size, which):
        return lax.dynamic_slice_in_dim(w, start + which * size, size, 1)

    q_all, k_all = 2 * QW, 2 * KW

    def qkv_cols(which):
        return jnp.concatenate(
            [
                cols(query_key_value_weight, 0, QW, which),
                cols(query_key_value_weight, q_all, KW, which),
                cols(query_key_value_weight, q_all + k_all, KW, which),
            ],
            axis=1,
        )

    w_own = qkv_cols(core)
    w_rec = other_core(qkv_cols(1 - core))
    gu_rec = other_core(
        jnp.concatenate([cols(w_gu, 0, HF, 1 - core), cols(w_gu, FF, HF, 1 - core)], axis=1)
    )

    own_set = lax.dynamic_index_in_dim(set_index, lax.axis_index("seq") * 2 + side, keepdims=False)
    low = order.reshape(2, half, 2)
    here = lax.dynamic_index_in_dim(low, place, 1, keepdims=False)
    flags = []
    for k in range(half):
        there = lax.dynamic_index_in_dim(low, place ^ k, 1, keepdims=False)
        flags.append((there[None, :, 0] < here[:, None, 0]).astype(jnp.int32).reshape(4))
    sc = jnp.concatenate([jnp.stack([core, own_set]).astype(jnp.int32)] + flags)
    cos, sin = rope_tables(here.T.reshape(4))
    ones = jnp.asarray(np.kron(np.eye(4), np.ones((HEAD_SIZE, HEAD_SIZE))), bf16)
    pick_one = np.zeros((2 * GROUPS, QW), np.float32)
    pick_sum = np.zeros((2 * GROUPS, QW), np.float32)
    for head in range(2 * GROUPS):
        pick_one[head, head * HEAD_SIZE] = 1.0
        pick_sum[head, head * HEAD_SIZE : (head + 1) * HEAD_SIZE] = 1.0
    gain_a = g_attn.astype(f32)[None]
    gain_f = g_ffn.astype(f32)[None]
    g_qk = jnp.concatenate(
        [jnp.tile(g_q, QW // HEAD_SIZE), jnp.tile(key_norm_gain, KW // HEAD_SIZE)]
    ).astype(f32)[None]
    a_qkv_t = jnp.swapaxes(a_qkv, 1, 2)
    a_o_t = jnp.swapaxes(a_o, 1, 2)
    a_gu_t = jnp.swapaxes(a_gu, 1, 2)
    a_down_t = jnp.swapaxes(a_down, 1, 2)

    four = (2, 2, CH)
    x4, u4, raw4, qm6, kv4 = qkv_call(
        sc, mine, other, cos.reshape(four + (PAIR,)), sin.reshape(four + (PAIR,)), w_own, w_rec,
        gain_a, a_qkv_t, b_q, key_up_weight, value_up_weight, g_qk, ones,
    )
    x = x4.reshape(TOK, width)
    u = u4.reshape(TOK, width)
    raw = raw4.reshape(TOK, QW + KW)
    qm = qm6.reshape(GROUPS, 2, TOK, PAIR)
    kv = kv4.reshape(TOK, 2 * KW)
    kvs = [kv] + [partner(kv, k) for k in range(1, half)]
    acc = None
    for k in range(half):
        acc = attend_call(2 + 4 * k, sc, qm, kvs[k], acc)
    ob, mix, lse = project_call(sc, acc, w_o, a_o_t, b_o, jnp.asarray(pick_one))

    def both(m, o):
        pair = jnp.stack([jnp.where(core == 0, m, o), jnp.where(core == 0, o, m)])
        return jnp.swapaxes(pair.reshape(2, 2, CH, width), 0, 1).reshape(TOK, width)

    ed = both(cot_mine, cot_other)
    h, down, du, gb_gu, ga_d, gb_d, ga_gu = ffn_call(
        sc, x, mix, other_core(mix), ed, gain_f, w_gu, gu_rec, w_down, a_gu_t, b_gu, a_down_t,
        b_down,
    )
    dh, dom, delta, gb_o, ga_o = back_mix_call(
        sc, h, ed, du, other_core(du), gain_f, w_o, a_o_t, b_o, acc, ob, jnp.asarray(pick_sum)
    )
    lse = lse.reshape(GROUPS, 2, TOK)
    delta = delta.reshape(GROUPS, 2, TOK)
    dq = None
    got = []
    for k in list(range(1, half)) + [0]:
        dq, dk, dv = attend_back_call(2 + 4 * k, k == 0, sc, qm, dom, kvs[k], lse, delta, dq)
        if k:
            got += [partner(dk, k), partner(dv, k)]
    du1, ga_qkv, gb_qkv = qkv_back_call(
        sc, dq.reshape(QW, TOK), dk, dv, got, raw, cos.reshape(TOK, PAIR), sin.reshape(TOK, PAIR),
        g_qk, ones, u, w_own, w_rec, a_qkv_t, b_q, key_up_weight, value_up_weight,
    )

    def block_of(v, which):
        v = v.reshape(2, 2, CH, v.shape[1])
        return lax.dynamic_index_in_dim(v, which, 1, keepdims=False).reshape(rows, v.shape[3])

    def home(v):
        back = swap(v.astype(bf16)).astype(f32)
        return jnp.where(stays, v, back).reshape(rows, 1, width)

    down_got = other_core(block_of(down, 1 - core)).astype(f32)
    layer_out = home(block_of(h, core) + (block_of(down, core).astype(f32) + down_got))
    du_got = other_core(block_of(du1, 1 - core).astype(bf16)).astype(f32)
    d_u = block_of(du1, core) + du_got
    xin = mine.astype(f32)
    inv = lax.rsqrt(jnp.mean(xin * xin, axis=1, keepdims=True) + epsilon)
    w = d_u * gain_a
    grad_in = block_of(dh, core) + inv * w - xin * inv**3 * jnp.mean(xin * w, axis=1, keepdims=True)
    input_grad = home(grad_in)

    shared = jnp.concatenate([gb_d, ga_gu, gb_o, ga_qkv], axis=0)
    shared = shared.astype(f32) + other_core(shared).astype(f32)
    n_shared = shared.shape[0] // 2
    shared = lax.dynamic_slice_in_dim(shared, core * n_shared, n_shared, 0).astype(bf16)
    pieces = [shared, gb_gu, ga_d, ga_o, gb_qkv]
    sizes = [p.size for p in pieces]
    flat = jnp.concatenate([p.reshape(-1) for p in pieces]).reshape(half, -1, 128)
    total = lax.dynamic_index_in_dim(flat, place, 0, keepdims=False).astype(f32)
    for k in range(1, half):
        sent = lax.dynamic_index_in_dim(flat, place ^ k, 0, keepdims=False)
        total += partner(sent, k).astype(f32)
    shard = total.astype(bf16)
    spread = [shard] + [partner(shard, k) for k in range(1, half)]
    spread = jnp.stack(spread)
    spread = jnp.concatenate(
        [lax.dynamic_index_in_dim(spread, place ^ p, 0) for p in range(half)]
    )
    side_pairs = [(i, (i + half) % n_ctx) for i in range(n_ctx)]
    spread = jnp.stack([spread, lax.ppermute(spread, "ctx", side_pairs)])
    spread = jnp.stack([lax.dynamic_index_in_dim(spread, side ^ s, 0, keepdims=False) for s in range(2)])
    lines = [spread]
    for k in range(1, n_seq):
        lines.append(lax.ppermute(spread, "seq", [(i, i ^ k) for i in range(n_seq)]))
    lines = jnp.stack(lines)
    seq_at = lax.axis_index("seq")
    lines = jnp.concatenate([lax.dynamic_index_in_dim(lines, seq_at ^ s, 0) for s in range(n_seq)])
    lines = lines.reshape(2 * n_seq, -1)
    twin = other_core(lines)
    cores = (jnp.where(core == 0, lines, twin), jnp.where(core == 0, twin, lines))
    onehot = (set_index[None, :] == jnp.arange(ADAPTER_SETS, dtype=jnp.int32)[:, None]).astype(f32)

    def place_sets(v):
        v = v.astype(f32)
        shape = (ADAPTER_SETS,) + (1,) * (v.ndim - 1)
        out = onehot[:, 0].reshape(shape) * v[0][None]
        for n in range(1, v.shape[0]):
            out += onehot[:, n].reshape(shape) * v[n][None]
        return out

    def piece(which, shape):
        start = sum(sizes[:which])
        return [c[:, start : start + sizes[which]].reshape((2 * n_seq,) + shape) for c in cores]

    sh = place_sets(jnp.concatenate(piece(0, (n_shared, width)), axis=1))
    r_gu = place_sets(jnp.concatenate(piece(1, (2, R, HF)), axis=3))
    r_ad = place_sets(jnp.concatenate(piece(2, (R, HF)), axis=2))
    r_ao = place_sets(jnp.concatenate(piece(3, (R, QW)), axis=2))
    qkv0, qkv1 = piece(4, (R, EW))
    r_bq = place_sets(jnp.concatenate([qkv0[..., :QW], qkv1[..., :QW]], axis=2))
    r_bk = place_sets(jnp.concatenate([qkv0[..., QW : QW + KW], qkv1[..., QW : QW + KW]], axis=2))
    r_bv = place_sets(jnp.concatenate([qkv0[..., QW + KW :], qkv1[..., QW + KW :]], axis=2))
    return (
        layer_out,
        input_grad,
        jnp.swapaxes(sh[:, 4 * R :], 1, 2),
        r_bq,
        r_bk,
        r_bv,
        jnp.swapaxes(r_ao, 1, 2),
        sh[:, 3 * R : 4 * R],
        jnp.swapaxes(sh[:, R : 3 * R], 1, 2),
        r_gu,
        jnp.swapaxes(r_ad, 1, 2),
        sh[:, :R],
    )


def solution(mesh):
    tokens = P("ctx", ("seq", "wsh"), None)
    in_specs = (
        (tokens, tokens) + (P("wsh", None),) * 4 + (P(),) * 15 + (P(("seq", "wsh"), None),)
    )
    out_specs = (tokens, tokens) + (P(),) * 10
    return jax.shard_map(
        per_device, mesh=mesh, in_specs=in_specs, out_specs=out_specs, check_vma=False
    )
```

time: 693 us -> 303 us (0.44)
  waiting for transfers between devices: 321 us -> 66.1 us
  matrix products: 190 us -> 0 us
  Pallas kernels: 0 us -> 128 us
  local copies, waits for them, and re-layouts: 93.8 us -> 30 us
  starting transfers between devices: 0.82 us -> 42.5 us
  other arithmetic: 59.5 us -> 29.5 us
  between operations: 16.5 us -> 2.02 us
    psum x1 -> x0, waiting for transfers between devices: 229 us -> none  [per_device(): lax.psum((set_terms[0], set_terms[1], set_terms[2], set_terms[3], set_ter...]
    dot_general x73 -> x0, matrix products: 190 us -> none  [the longest x69 169 us: contract(): return jnp.einsum(form, left, right, preferred_element_type=jnp.float32)]
    pallas_call x0 -> x13, Pallas kernels: none -> 128 us  [the longest x4 35.3 us: attend_back_call(): pl.pallas_call(functools.partial(attend_back_kernel, base, first, has_dq)...]
    ppermute x0 -> x32, waiting for transfers between devices: none -> 66.1 us  [the longest x5 20.4 us: swap(): return lax.ppermute(v, ('ctx', 'wsh'), swap_pairs)]
    reduce_scatter x1 -> x0, waiting for transfers between devices: 59.8 us -> none  [per_device(): lax.psum_scatter(all_grad.astype(jnp.bfloat16), 'ctx', scatter_dimension=...]
    ppermute x0 -> x32, starting transfers between devices: none -> 42.5 us  [the longest x5 16.9 us: swap(): return lax.ppermute(v, ('ctx', 'wsh'), swap_pairs)]
    all_gather x5 -> x0, waiting for transfers between devices: 29.6 us -> none  [the longest x1 22.2 us: per_device(): key_value_piece = lax.all_gather(kv_local, 'ctx', axis=1, tiled=True)]
    reduce_sum x11 -> x1, other arithmetic: 20.5 us -> 0.35 us  [per_device(): inv = lax.rsqrt(jnp.mean(xin * xin, axis=1, keepdims=True) + epsilon)]
  transfers between devices with their start and end apart: 7 -> 32, of which waited for: 4 -> 18; matrix products, arithmetic and copies ran while one was open for 29% -> 11% of each run, Pallas kernels for 0% -> 18%
where the time goes in v1:
time: 303 us; the launch traced here: 298 us
  Pallas kernels  128 us (42%)
  waiting for transfers between devices  66.1 us (22%)
  starting transfers between devices  42.5 us (14%)
  local copies, waits for them, and re-layouts  30 us (10%)
  other arithmetic  29.5 us (10%)
    pallas_call x4, Pallas kernels, attend_back_call(): pl.pallas_call(functools.partial(attend_back_kernel, base, first, has_dq)...  35.3 us
    pallas_call x1, Pallas kernels, ffn_call(): pl.pallas_call(ffn_kernel, grid_spec=pltpu.PrefetchScalarGridSpec(num_sca...  30.9 us
    pallas_call x4, Pallas kernels, attend_call(): pl.pallas_call(functools.partial(attend_kernel, base, first), grid_spec=p...  28.7 us
    ppermute x5, waiting for transfers between devices, swap(): return lax.ppermute(v, ('ctx', 'wsh'), swap_pairs)  20.4 us
    ppermute x15, waiting for transfers between devices, partner(): lax.ppermute(v, 'ctx', [(s * half + p, s * half + (p ^ k)) for s in range...  17.5 us
    ppermute x5, starting transfers between devices, swap(): return lax.ppermute(v, ('ctx', 'wsh'), swap_pairs)  16.9 us
    ppermute x1, waiting for transfers between devices, per_device(): spread = jnp.stack([spread, lax.ppermute(spread, 'ctx', side_pairs)])  13.7 us
    ppermute x15, starting transfers between devices, partner(): lax.ppermute(v, 'ctx', [(s * half + p, s * half + (p ^ k)) for s in range...  13.3 us
  transfers between devices with their start and end apart: 32, of which 18 were waited for; matrix products, arithmetic and copies ran while one was open for 11% of the time, Pallas kernels for 18%

profile of v1, /device:TPU:1, one launch (start us, length us, event | category | flops | bytes accessed | tf_op | source)
XLA Modules:
  0.0 298.2 jit_solution(18299015011664034178)
XLA Ops:
  0.6 5.6 %collective-permute-start = (s32[1,16]{1,0:T(1,128)}, s32[1,16]{1,0:T(1,128)S(1)}, u32[]{:S(2)}, u32[]{:S(2)}) collective-permute-start(s32[1,16]{1,0:T(1,128)} %param.51), channel_id=1, source_target_pairs={{1,8},{3,10},{5,12},{7,14},{8,1},{10,3},{12,5},{14,7},{17,24},{19,... | collective-permute-start | bytes 200 | tf_op jit(solution)/shard_map/ppermute | solution.py:690
  6.3 2.7 constant_dynamic-slice_fusion.10
  9.0 2.5 pad_maximum_fusion
  12.6 1.9 collective-permute-start.1
  15.9 1.1 pad_maximum_fusion.2.w_own.rest_12_
  18.6 1.3 concatenate.74.sc
  19.8 10.1 %collective-permute-done.1 = bf16[256,1024]{1,0:T(8,128)(2,1)} collective-permute-done((bf16[256,1024]{1,0:T(8,128)(2,1)}, bf16[256,1024]{1,0:T(8,128)(2,1)}, u32[]{:S(2)}, u32[]{:S(2)}) %collective-permute-start.1) | collective-permute-done | bytes 524320 | tf_op jit(solution)/shard_map/ppermute | solution.py:690
  29.9 1.3 broadcast_select_fusion.5.mine
  31.5 1.3 pad_maximum_fusion.8
  33.9 8.6 %qkv.1 = (bf16[2,2,128,1024]{3,2,1,0:T(8,128)(2,1)}, bf16[2,2,128,1024]{3,2,1,0:T(8,128)(2,1)}, f32[2,2,128,768]{3,2,1,0:T(8,128)}, bf16[4,2,2,2,128,128]{5,4,3,2,1,0:T(8,128)(2,1)}, bf16[2,2,128,512]{3,2,1,0:T(8,128)(2,1)}) custom-call(s32[18]{0:T(128)} %concatenate.74.sc, bf16[256,1024]{1,0:T(8,128)(2,1)} %copy-done, bf16[256,1024]{1,0:T(8,128)(2,1)} %copy-done.12, ...), custom_call_target="tpu_custom_call" | custom-call | flops 1073741824 | bytes 8000000 | tf_op jit(solution)/shard_map/qkv/pallas_call | solution.py:153
  42.6 1.3 collective-permute-start.6
  43.9 4.2 %collective-permute-start.8 = (bf16[256,1024]{1,0:T(8,128)(2,1)S(1)}, bf16[256,1024]{1,0:T(8,128)(2,1)S(1)}, u32[]{:S(2)}, u32[]{:S(2)}) collective-permute-start(bf16[256,1024]{1,0:T(8,128)(2,1)S(1)} %bitcast.256), channel_id=1, source_target_pairs={{1,8},{3,10},{5,12},{7,14},{8,1},{10,3},{12,5},{14,7},{17,24},{19,... | collective-permute-start | bytes 1572872 | tf_op jit(solution)/shard_map/ppermute | solution.py:690
  48.2 7.0 %attend.4.rest_0_ = f32[4,512,256]{2,1,0:T(8,128)} custom-call(s32[18]{0:T(128)} %concatenate.74.sc, bf16[4,2,512,128]{3,2,1,0:T(8,128)(2,1)} %bitcast.288, bf16[512,512]{1,0:T(8,128)(2,1)} %bitcast.301, bf16[512,512]{1,0:T(8,128)(2,1)} %bitcast.302), custom_call_target="tpu_custom_call" | custom-call | flops 2400000000 | bytes 5000000 | tf_op jit(solution)/shard_map/attend/pallas_call | solution.py:244
  56.7 7.2 %attend.5.rest_0_ = f32[4,512,256]{2,1,0:T(8,128)} custom-call(s32[18]{0:T(128)} %concatenate.74.sc, bf16[4,2,512,128]{3,2,1,0:T(8,128)(2,1)} %bitcast.289, bf16[512,512]{1,0:T(8,128)(2,1)} %copy-done.39, bf16[512,512]{1,0:T(8,128)(2,1)} %copy-done.39, f32[4,512,256]{2,1,0:T(8,128)} %attend.4.rest_0_), custom_call_target="tpu_custom_call", output_to_operand_aliasing={{}: (4, {})} | custom-call | flops 2400000000 | bytes 5000000 | tf_op jit(solution)/shard_map/attend/pallas_call | solution.py:244
  64.7 7.3 %attend.6.rest_0_ = f32[4,512,256]{2,1,0:T(8,128)} custom-call(s32[18]{0:T(128)} %concatenate.74.sc, bf16[4,2,512,128]{3,2,1,0:T(8,128)(2,1)} %bitcast.290, bf16[512,512]{1,0:T(8,128)(2,1)} %copy-done.38, bf16[512,512]{1,0:T(8,128)(2,1)} %copy-done.38, f32[4,512,256]{2,1,0:T(8,128)} %attend.5.rest_0_), custom_call_target="tpu_custom_call", output_to_operand_aliasing={{}: (4, {})} | custom-call | flops 2400000000 | bytes 5000000 | tf_op jit(solution)/shard_map/attend/pallas_call | solution.py:244
  72.0 1.6 collective-permute-done.4.k.v
  74.4 7.2 %attend.7.acc = f32[4,512,256]{2,1,0:T(8,128)} custom-call(s32[18]{0:T(128)} %concatenate.74.sc, bf16[4,2,512,128]{3,2,1,0:T(8,128)(2,1)} %bitcast.291, bf16[512,512]{1,0:T(8,128)(2,1)} %copy-done.40, bf16[512,512]{1,0:T(8,128)(2,1)} %copy-done.40, f32[4,512,256]{2,1,0:T(8,128)} %attend.6.rest_0_), custom_call_target="tpu_custom_call", output_to_operand_aliasing={{}: (4, {})} | custom-call | flops 2400000000 | bytes 5000000 | tf_op jit(solution)/shard_map/attend/pallas_call | solution.py:244
  81.6 5.9 %project.1 = (bf16[512,512]{1,0:T(8,128)(2,1)}, bf16[512,1024]{1,0:T(8,128)(2,1)}, f32[8,512]{1,0:T(8,128)}) custom-call(s32[18]{0:T(128)} %concatenate.74.sc, f32[4,512,256]{2,1,0:T(8,128)} %attend.7.acc, bf16[512,1024]{1,0:T(8,128)(2,1)} %w_o.3, bf16[8,16,1024]{2,1,0:T(8,128)(2,1)} %bitcast.250, bf16[8,16,1024]{2,1,0:T(8,128)(2,1)} %b_o.3, ...), custom_call_target="tpu_custom_call" | custom-call | flops 536870912 | bytes 6000000 | tf_op jit(solution)/shard_map/project/pallas_call | solution.py:284
  87.6 1.6 collective-permute-start.7
  89.9 2.3 collective-permute-done.9
  92.3 1.1 pad_maximum_fusion.4
  94.4 30.9 %ffn.1 = (f32[512,1024]{1,0:T(8,128)}, bf16[512,1024]{1,0:T(8,128)(2,1)}, bf16[512,1024]{1,0:T(8,128)(2,1)}, bf16[2,16,2304]{2,1,0:T(8,128)(2,1)}, bf16[16,2304]...) custom-call(s32[18]{0:T(128)} %concatenate.74.sc, bf16[512,1024]{1,0:T(8,128)(2,1)} %bitcast.296, ...), custom_call_target="tpu_custom_call" | custom-call | flops 14495514624 | bytes 25000000 | tf_op jit(solution)/shard_map/ffn/pallas_call | solution.py:367
  126.6 1.6 collective-permute-done.13.du_b
  129.2 8.4 %back_mix.1 = (f32[512,1024]{1,0:T(8,128)}, bf16[4,2,512,128]{3,2,1,0:T(8,128)(2,1)}, f32[8,512]{1,0:T(8,128)}, bf16[16,1024]{1,0:T(8,128)(2,1)}, bf16[16,512]{1,0:T(8,128)(2,1)}) custom-call(s32[18]{0:T(128)} %concatenate.74.sc, f32[512,1024]{1,0:T(8,128)} %get-tuple-element.51.h, bf16[512,1024]{1,0:T(8,128)(2,1)} %bitcast.225, ...), custom_call_target="tpu_custom_call" | custom-call | flops 536870912 | bytes 12000000 | tf_op jit(solution)/shard_map/back_mix/pallas_call | solution.py:450
  137.6 1.3 reshape.423.delta
  139.0 8.2 %attend_back.4 = (f32[4,2,64,512]{3,2,1,0:T(8,128)}, bf16[512,256]{1,0:T(8,128)(2,1)}, bf16[512,256]{1,0:T(8,128)(2,1)}) custom-call(s32[18]{0:T(128)} %concatenate.74.sc, bf16[4,2,512,128]{3,2,1,0:T(8,128)(2,1)} %bitcast.292, bf16[4,2,512,128]{3,2,1,0:T(8,128)(2,1)} %get-tuple-element.56.dom, bf16[512,512]{1,0:T(8,128)(2,1)} %copy-done.39, ...), custom_call_target="tpu_custom_call" | custom-call | flops 6000000000 | bytes 6000000 | tf_op jit(solution)/shard_map/attend_back/pallas_call | solution.py:541
  147.2 8.4 %attend_back.5 = (f32[4,2,64,512]{3,2,1,0:T(8,128)}, bf16[512,256]{1,0:T(8,128)(2,1)}, bf16[512,256]{1,0:T(8,128)(2,1)}) custom-call(s32[18]{0:T(128)} %concatenate.74.sc, bf16[4,2,512,128]{3,2,1,0:T(8,128)(2,1)} %bitcast.293, bf16[4,2,512,128]{3,2,1,0:T(8,128)(2,1)} %get-tuple-element.56.dom, ...), custom_call_target="tpu_custom_call", output_to_operand_aliasing={{0}: (7, {})} | custom-call | flops 6000000000 | bytes 6000000 | tf_op jit(solution)/shard_map/attend_back/pallas_call | solution.py:541
  155.6 8.5 %attend_back.6 = (f32[4,2,64,512]{3,2,1,0:T(8,128)}, bf16[512,256]{1,0:T(8,128)(2,1)}, bf16[512,256]{1,0:T(8,128)(2,1)}) custom-call(s32[18]{0:T(128)} %concatenate.74.sc, bf16[4,2,512,128]{3,2,1,0:T(8,128)(2,1)} %bitcast.294, bf16[4,2,512,128]{3,2,1,0:T(8,128)(2,1)} %get-tuple-element.56.dom, ...), custom_call_target="tpu_custom_call", output_to_operand_aliasing={{0}: (7, {})} | custom-call | flops 6000000000 | bytes 6000000 | tf_op jit(solution)/shard_map/attend_back/pallas_call | solution.py:541
  164.8 1.3 pad_maximum_fusion.10
  166.1 1.8 collective-permute-start.19
  168.0 1.3 collective-permute-start.17
  169.3 1.2 collective-permute-start.14
  170.6 2.2 collective-permute-done.18.rest_4_
  172.8 1.2 collective-permute-start.15
  174.0 10.3 %attend_back.7 = (f32[4,2,64,512]{3,2,1,0:T(8,128)}, f32[512,256]{1,0:T(8,128)}, f32[512,256]{1,0:T(8,128)}) custom-call(s32[18]{0:T(128)} %concatenate.74.sc, bf16[4,2,512,128]{3,2,1,0:T(8,128)(2,1)} %bitcast.295, bf16[4,2,512,128]{3,2,1,0:T(8,128)(2,1)} %get-tuple-element.56.dom, bf16[512,512]{1,0:T(8,128)(2,1)} %bitcast.303, ...), custom_call_target="tpu_custom_call", output_to_operand_aliasing={{0}: (7, {})} | custom-call | flops 6000000000 | bytes 6000000 | tf_op jit(solution)/shard_map/attend_back/pallas_call | solution.py:541
  184.3 5.4 %collective-permute-done.17.rest_3_ = bf16[512,256]{1,0:T(8,128)(2,1)S(1)} collective-permute-done((bf16[512,256]{1,0:T(8,128)(2,1)S(1)}, bf16[512,256]{1,0:T(8,128)(2,1)S(1)}, u32[]{:S(2)}, u32[]{:S(2)}) %collective-permute-start.17) | collective-permute-done | bytes 262176 | tf_op jit(solution)/shard_map/ppermute | solution.py:696
  191.0 10.2 %qkv_back.1 = (f32[512,1024]{1,0:T(8,128)}, bf16[48,1024]{1,0:T(8,128)(2,1)}, bf16[16,1024]{1,0:T(8,128)(2,1)}) custom-call(s32[18]{0:T(128)} %concatenate.74.sc, f32[512,512]{1,0:T(8,128)} %bitcast.247, f32[512,256]{1,0:T(8,128)} %get-tuple-element.63.dk, f32[512,256]{1,0:T(8,128)} %get-tuple-element.64.dv, bf16[512,256]{1,0:T(8,128)(2,1)} %copy-done.21, ...), custom_call_target="tpu_custom_call" | custom-call | flops 1073741824 | bytes 12000000 | tf_op jit(solution)/shard_map/qkv_back/pallas_call | solution.py:618
  205.2 1.7 collective-permute-start.25
  206.9 1.4 collective-permute-done.23
  209.0 1.9 collective-permute-done.25
  212.1 1.6 collective-permute-start.28
  215.4 1.4 collective-permute-done.28
  217.0 1.2 collective-permute-start.29
  218.2 3.6 %collective-permute-start.11 = (bf16[256,1024]{1,0:T(8,128)(2,1)S(1)}, bf16[256,1024]{1,0:T(8,128)(2,1)S(1)}, u32[]{:S(2)}, u32[]{:S(2)}) collective-permute-start(bf16[256,1024]{1,0:T(8,128)(2,1)S(1)} %bitcast.264), channel_id=1, source_target_pairs={{0,1},{1,0},{2,3},{3,2},{4,5},{5,4},{6,7},{7,6},{8,9},{9,8},{10,11... | collective-permute-start | bytes 1572872 | tf_op jit(solution)/shard_map/ppermute | solution.py:693
  222.3 13.7 %collective-permute-done.29 = bf16[4,376,128]{2,1,0:T(8,128)(2,1)S(1)} collective-permute-done((bf16[4,376,128]{2,1,0:T(8,128)(2,1)S(1)}, bf16[4,376,128]{2,1,0:T(8,128)(2,1)S(1)}, u32[]{:S(2)}, u32[]{:S(2)}) %collective-permute-start.29) | collective-permute-done | bytes 385056 | tf_op jit(solution)/shard_map/ppermute | solution.py:831
  236.4 1.3 collective-permute-start.30
  237.7 1.1 fusion.8
  238.8 3.0 %collective-permute-start.12 = (bf16[256,1024]{1,0:T(8,128)(2,1)}, bf16[256,1024]{1,0:T(8,128)(2,1)}, u32[]{:S(2)}, u32[]{:S(2)}) collective-permute-start(bf16[256,1024]{1,0:T(8,128)(2,1)} %fusion.8), channel_id=1, source_target_pairs={{1,8},{3,10},{5,12},{7,14},{8,1},{10,3},{12,5},{14,7},{17,24},{19,... | collective-permute-start | bytes 1572872 | tf_op jit(solution)/shard_map/ppermute | solution.py:690
  241.8 1.0 constant_dynamic-slice_fusion.5
  243.3 10.2 %collective-permute-done.30 = bf16[2,4,376,128]{3,2,1,0:T(8,128)(2,1)S(1)} collective-permute-done((bf16[2,4,376,128]{3,2,1,0:T(8,128)(2,1)S(1)}, bf16[2,4,376,128]{3,2,1,0:T(8,128)(2,1)S(1)}, u32[]{:S(2)}, u32[]{:S(2)}) %collective-permute-start.30) | collective-permute-done | bytes 770080 | tf_op jit(solution)/shard_map/ppermute | solution.py:835
  254.1 1.3 pad_maximum_fusion.1
  255.4 3.1 %reshape.436 = bf16[4,192512]{1,0:T(4,128)(2,1)} reshape(bf16[2,2,4,376,128]{4,3,2,1,0:T(8,128)(2,1)} %pad_maximum_fusion.1) | data formatting | bytes 3080192 | tf_op jit(solution)/shard_map/reshape | solution.py:839
  258.5 2.5 collective-permute-start.31
  261.0 1.9 fusion.20
  262.9 2.2 collective-permute-start.21
  265.1 1.3 select_bitcast_fusion.1
  266.4 2.0 copy.58
  268.5 10.3 %collective-permute-done.21 = bf16[256,1024]{1,0:T(8,128)(2,1)S(1)} collective-permute-done((bf16[256,1024]{1,0:T(8,128)(2,1)S(1)}, bf16[256,1024]{1,0:T(8,128)(2,1)S(1)}, u32[]{:S(2)}, u32[]{:S(2)}) %collective-permute-start.21) | collective-permute-done | bytes 524320 | tf_op jit(solution)/shard_map/ppermute | solution.py:690
  278.9 2.1 copy.59
  281.0 1.3 broadcast_select_fusion.1
  285.2 1.2 slice_bitcast_fusion
  287.5 1.0 slice_bitcast_fusion.1
  289.6 2.0 multiply_add_fusion.2
  291.6 3.3 %multiply_add_fusion = f32[8,2,16,4608]{3,2,1,0:T(8,128)} fusion(f32[2,16,4608]{2,1,0:T(8,128)S(1)} %get-tuple-element.117, f32[8]{0:T(128)S(1)} %get-tuple-element.185, f32[2,16,4608]{2,1,0:T(8,128)S(1)} %get-tuple-element.118, f32[8]{0:T(128)S(1)} %get-tuple-element.186, f32[2,16,4608]{2,1,0:T(8,128)S(1)} %get-tuple-element.119, ...), kind=kLoop, calls=%fused_computation.1 | loop fusion | flops 8257536 | bytes 7078016 | tf_op jit(solution)/shard_map/add | solution.py:849
  (235 shorter events, 32.5 us)
Async XLA Ops:
  0.6 17.0 %collective-permute-start = (s32[1,16]{1,0:T(1,128)}, s32[1,16]{1,0:T(1,128)S(1)}, u32[]{:S(2)}, u32[]{:S(2)}) collective-permute-start(s32[1,16]{1,0:T(1,128)} %param.51), channel_id=1, source_target_pairs={{1,8},{3,10},{5,12},{7,14},{8,1},{10,3},{12,5},{14,7},{17,24},{19,... | collective-permute-start | bytes 200 | tf_op jit(solution)/shard_map/ppermute | solution.py:690
  11.5 81.9 %collective-permute-start.10 = (bf16[512,4608]{1,0:T(8,128)(2,1)}, bf16[512,4608]{1,0:T(8,128)(2,1)}, u32[]{:S(2)}, u32[]{:S(2)}) collective-permute-start(bf16[512,4608]{1,0:T(8,128)(2,1)} %pad_maximum_fusion), channel_id=1, source_target_pairs={{0,1},{1,0},{2,3},{3,2},{4,5},{5,4},{6,7},{7,6},{8,9},{9,8},{10,11... | collective-permute-start | bytes 14155784 | tf_op jit(solution)/shard_map/ppermute | solution.py:693
  11.6 3.5 %copy-start.34 = (bf16[64]{0:T(256)(128)(2,1)S(1)}, bf16[64]{0:T(256)(128)(2,1)}, u32[]{:S(2)}) copy-start(bf16[64]{0:T(256)(128)(2,1)} %param.38) | copy-start | bytes 388
  11.6 3.6 %copy-start.45 = (bf16[64]{0:T(256)(128)(2,1)S(1)}, bf16[64]{0:T(256)(128)(2,1)}, u32[]{:S(2)}) copy-start(bf16[64]{0:T(256)(128)(2,1)} %param.39) | copy-start | bytes 388
  11.8 5.2 %copy-start.35 = (s32[4]{0:T(128)S(1)}, s32[4]{0:T(128)}, u32[]{:S(2)}) copy-start(s32[4]{0:T(128)} %param.50) | copy-start | bytes 52
  11.8 5.8 %copy-start.36 = (s32[1,16]{1,0:T(1,128)S(1)}, s32[1,16]{1,0:T(1,128)}, u32[]{:S(2)}) copy-start(s32[1,16]{1,0:T(1,128)} %param.51) | copy-start | bytes 196
  12.0 19.3 %copy-start.33 = (f32[32]{0:T(128)S(1)}, f32[32]{0:T(128)}, u32[]{:S(2)}) copy-start(f32[32]{0:T(128)} %constant.157.clone) | copy-start | bytes 388
  12.0 19.4 %copy-start.15 = (f32[128,32]{1,0:T(8,128)S(1)}, f32[128,32]{1,0:T(8,128)}, u32[]{:S(2)}) copy-start(f32[128,32]{1,0:T(8,128)} %constant.166) | copy-start | bytes 49156
  12.0 19.4 %copy-start.16 = (f32[128,32]{1,0:T(8,128)S(1)}, f32[128,32]{1,0:T(8,128)}, u32[]{:S(2)}) copy-start(f32[128,32]{1,0:T(8,128)} %constant.167) | copy-start | bytes 49156
  12.0 20.8 %collective-permute-start.3 = (bf16[512,1024]{1,0:T(8,128)(2,1)S(1)}, bf16[512,1024]{1,0:T(8,128)(2,1)S(1)}, u32[]{:S(2)}, u32[]{:S(2)}) collective-permute-start(bf16[512,1024]{1,0:T(8,128)(2,1)S(1)} %pad_maximum_fusion.3), channel_id=1, source_target_pairs={{0,1},{1,0},{2,3},{3,2},{4,5},{5,4},{6,7},{7,6},{8,9},{9,8},{10,11... | collective-permute-start | bytes 3145736 | tf_op jit(solution)/shard_map/ppermute | solution.py:693
  12.6 17.3 %collective-permute-start.1 = (bf16[256,1024]{1,0:T(8,128)(2,1)}, bf16[256,1024]{1,0:T(8,128)(2,1)}, u32[]{:S(2)}, u32[]{:S(2)}) collective-permute-start(bf16[256,1024]{1,0:T(8,128)(2,1)} %bitcast.5), channel_id=1, source_target_pairs={{1,8},{3,10},{5,12},{7,14},{8,1},{10,3},{12,5},{14,7},{17,24},{19,... | collective-permute-start | bytes 1572872 | tf_op jit(solution)/shard_map/ppermute | solution.py:690
  31.2 2.0 collective-permute-start.2
  33.9 10.0 %copy-start.14 = (bf16[256,1,1024]{2,0,1:T(8,128)(2,1)S(1)}, bf16[256,1,1024]{2,0,1:T(8,128)(2,1)}, u32[]{:S(2)}) copy-start(bf16[256,1,1024]{2,0,1:T(8,128)(2,1)} %param.31) | copy-start | bytes 1572868
  42.6 13.3 %collective-permute-start.6 = (bf16[512,512]{1,0:T(8,128)(2,1)}, bf16[512,512]{1,0:T(8,128)(2,1)S(1)}, u32[]{:S(2)}, u32[]{:S(2)}) collective-permute-start(bf16[512,512]{1,0:T(8,128)(2,1)} %bitcast.298), channel_id=1, source_target_pairs={{0,2},{2,0},{4,6},{6,4},{8,10},{10,8},{12,14},{14,12},{1,3},{3,1},... | collective-permute-start | bytes 1572872 | tf_op jit(solution)/shard_map/ppermute | solution.py:696
  43.9 20.0 %collective-permute-start.5 = (bf16[512,512]{1,0:T(8,128)(2,1)}, bf16[512,512]{1,0:T(8,128)(2,1)S(1)}, u32[]{:S(2)}, u32[]{:S(2)}) collective-permute-start(bf16[512,512]{1,0:T(8,128)(2,1)} %bitcast.299), channel_id=1, source_target_pairs={{0,4},{2,6},{4,0},{6,2},{8,12},{10,14},{12,8},{14,10},{1,5},{3,7},... | collective-permute-start | bytes 1572872 | tf_op jit(solution)/shard_map/ppermute | solution.py:696
  43.9 45.3 %collective-permute-start.8 = (bf16[256,1024]{1,0:T(8,128)(2,1)S(1)}, bf16[256,1024]{1,0:T(8,128)(2,1)S(1)}, u32[]{:S(2)}, u32[]{:S(2)}) collective-permute-start(bf16[256,1024]{1,0:T(8,128)(2,1)S(1)} %bitcast.256), channel_id=1, source_target_pairs={{1,8},{3,10},{5,12},{7,14},{8,1},{10,3},{12,5},{14,7},{17,24},{19,... | collective-permute-start | bytes 1572872 | tf_op jit(solution)/shard_map/ppermute | solution.py:690
  48.1 25.5 %collective-permute-start.4 = (bf16[512,512]{1,0:T(8,128)(2,1)}, bf16[512,512]{1,0:T(8,128)(2,1)S(1)}, u32[]{:S(2)}, u32[]{:S(2)}) collective-permute-start(bf16[512,512]{1,0:T(8,128)(2,1)} %bitcast.300), channel_id=1, source_target_pairs={{0,6},{2,4},{4,2},{6,0},{8,14},{10,12},{12,10},{14,8},{1,7},{3,5},... | collective-permute-start | bytes 1572872 | tf_op jit(solution)/shard_map/ppermute | solution.py:696
  81.6 7.7 %copy-start.32 = (bf16[1024]{0:T(1024)(128)(2,1)S(1)}, bf16[1024]{0:T(1024)(128)(2,1)}, u32[]{:S(2)}) copy-start(bf16[1024]{0:T(1024)(128)(2,1)} %param.37) | copy-start | bytes 6148
  87.6 5.8 %collective-permute-start.7 = (bf16[512,1024]{1,0:T(8,128)(2,1)}, bf16[512,1024]{1,0:T(8,128)(2,1)S(1)}, u32[]{:S(2)}, u32[]{:S(2)}) collective-permute-start(bf16[512,1024]{1,0:T(8,128)(2,1)} %get-tuple-element.50.mix_a), channel_id=1, source_target_pairs={{0,1},{1,0},{2,3},{3,2},{4,5},{5,4},{6,7},{7,6},{8,9},{9,8},{10,11... | collective-permute-start | bytes 3145736 | tf_op jit(solution)/shard_map/ppermute | solution.py:693
  89.2 3.0 collective-permute-start.9
  94.4 31.6 %copy-start.30 = (f32[8,512]{1,0:T(8,128)S(1)}, f32[8,512]{1,0:T(8,128)}, u32[]{:S(2)}) copy-start(f32[8,512]{1,0:T(8,128)} %get-tuple-element.57) | copy-start | bytes 49156
  125.3 2.9 collective-permute-start.13
  155.6 10.5 %copy-start.28 = (bf16[16,1024]{1,0:T(8,128)(2,1)S(1)}, bf16[16,1024]{1,0:T(8,128)(2,1)}, u32[]{:S(2)}) copy-start(bf16[16,1024]{1,0:T(8,128)(2,1)} %get-tuple-element.74) | copy-start | bytes 98308
  155.6 10.5 %copy-start.25 = (bf16[32,1024]{1,0:T(8,128)(2,1)S(1)}, bf16[32,1024]{1,0:T(8,128)(2,1)}, u32[]{:S(2)}) copy-start(bf16[32,1024]{1,0:T(8,128)(2,1)} %get-tuple-element.75) | copy-start | bytes 196612
  155.6 12.3 %copy-start.44 = (bf16[512,256]{1,0:T(8,128)(2,1)S(1)}, bf16[512,256]{1,0:T(8,128)(2,1)}, u32[]{:S(2)}) copy-start(bf16[512,256]{1,0:T(8,128)(2,1)} %get-tuple-element.67) | copy-start | bytes 786436
  155.6 12.4 %copy-start.43 = (bf16[512,256]{1,0:T(8,128)(2,1)S(1)}, bf16[512,256]{1,0:T(8,128)(2,1)}, u32[]{:S(2)}) copy-start(bf16[512,256]{1,0:T(8,128)(2,1)} %get-tuple-element.68) | copy-start | bytes 786436
  155.6 13.7 %copy-start.42 = (bf16[512,256]{1,0:T(8,128)(2,1)S(1)}, bf16[512,256]{1,0:T(8,128)(2,1)}, u32[]{:S(2)}) copy-start(bf16[512,256]{1,0:T(8,128)(2,1)} %get-tuple-element.65) | copy-start | bytes 786436
  155.6 17.2 %copy-start.41 = (bf16[512,256]{1,0:T(8,128)(2,1)S(1)}, bf16[512,256]{1,0:T(8,128)(2,1)}, u32[]{:S(2)}) copy-start(bf16[512,256]{1,0:T(8,128)(2,1)} %get-tuple-element.66) | copy-start | bytes 786436
  164.1 8.7 %collective-permute-start.18 = (bf16[512,256]{1,0:T(8,128)(2,1)}, bf16[512,256]{1,0:T(8,128)(2,1)S(1)}, u32[]{:S(2)}, u32[]{:S(2)}) collective-permute-start(bf16[512,256]{1,0:T(8,128)(2,1)} %get-tuple-element.69), channel_id=1, source_target_pairs={{0,6},{2,4},{4,2},{6,0},{8,14},{10,12},{12,10},{14,8},{1,7},{3,5},... | collective-permute-start | bytes 786440 | tf_op jit(solution)/shard_map/ppermute | solution.py:696
  166.1 18.2 %collective-permute-start.19 = (bf16[512,256]{1,0:T(8,128)(2,1)}, bf16[512,256]{1,0:T(8,128)(2,1)S(1)}, u32[]{:S(2)}, u32[]{:S(2)}) collective-permute-start(bf16[512,256]{1,0:T(8,128)(2,1)} %get-tuple-element.70), channel_id=1, source_target_pairs={{0,6},{2,4},{4,2},{6,0},{8,14},{10,12},{12,10},{14,8},{1,7},{3,5},... | collective-permute-start | bytes 786440 | tf_op jit(solution)/shard_map/ppermute | solution.py:696
  167.8 16.5 %collective-permute-start.16 = (bf16[512,256]{1,0:T(8,128)(2,1)S(1)}, bf16[512,256]{1,0:T(8,128)(2,1)S(1)}, u32[]{:S(2)}, u32[]{:S(2)}) collective-permute-start(bf16[512,256]{1,0:T(8,128)(2,1)S(1)} %copy-done.44), channel_id=1, source_target_pairs={{0,4},{2,6},{4,0},{6,2},{8,12},{10,14},{12,8},{14,10},{1,5},{3,7},... | collective-permute-start | bytes 786440 | tf_op jit(solution)/shard_map/ppermute | solution.py:696
  168.0 21.7 %collective-permute-start.17 = (bf16[512,256]{1,0:T(8,128)(2,1)S(1)}, bf16[512,256]{1,0:T(8,128)(2,1)S(1)}, u32[]{:S(2)}, u32[]{:S(2)}) collective-permute-start(bf16[512,256]{1,0:T(8,128)(2,1)S(1)} %copy-done.43), channel_id=1, source_target_pairs={{0,4},{2,6},{4,0},{6,2},{8,12},{10,14},{12,8},{14,10},{1,5},{3,7},... | collective-permute-start | bytes 786440 | tf_op jit(solution)/shard_map/ppermute | solution.py:696
  169.3 20.4 %collective-permute-start.14 = (bf16[512,256]{1,0:T(8,128)(2,1)S(1)}, bf16[512,256]{1,0:T(8,128)(2,1)S(1)}, u32[]{:S(2)}, u32[]{:S(2)}) collective-permute-start(bf16[512,256]{1,0:T(8,128)(2,1)S(1)} %copy-done.42), channel_id=1, source_target_pairs={{0,2},{2,0},{4,6},{6,4},{8,10},{10,8},{12,14},{14,12},{1,3},{3,1},... | collective-permute-start | bytes 786440 | tf_op jit(solution)/shard_map/ppermute | solution.py:696
  172.8 11.5 %copy-start.17 = (bf16[512,256]{1,0:T(8,128)(2,1)}, bf16[512,256]{1,0:T(8,128)(2,1)S(1)}, u32[]{:S(2)}) copy-start(bf16[512,256]{1,0:T(8,128)(2,1)S(1)} %collective-permute-done.18.rest_4_) | copy-start | bytes 786436
  172.8 17.5 %collective-permute-start.15 = (bf16[512,256]{1,0:T(8,128)(2,1)S(1)}, bf16[512,256]{1,0:T(8,128)(2,1)S(1)}, u32[]{:S(2)}, u32[]{:S(2)}) collective-permute-start(bf16[512,256]{1,0:T(8,128)(2,1)S(1)} %copy-done.41), channel_id=1, source_target_pairs={{0,2},{2,0},{4,6},{6,4},{8,10},{10,8},{12,14},{14,12},{1,3},{3,1},... | collective-permute-start | bytes 786440 | tf_op jit(solution)/shard_map/ppermute | solution.py:696
  174.0 10.3 %copy-start.27 = (bf16[16,1024]{1,0:T(8,128)(2,1)S(1)}, bf16[16,1024]{1,0:T(8,128)(2,1)}, u32[]{:S(2)}) copy-start(bf16[16,1024]{1,0:T(8,128)(2,1)} %get-tuple-element.76) | copy-start | bytes 98308
  184.3 6.0 %copy-start.18 = (bf16[512,256]{1,0:T(8,128)(2,1)}, bf16[512,256]{1,0:T(8,128)(2,1)S(1)}, u32[]{:S(2)}) copy-start(bf16[512,256]{1,0:T(8,128)(2,1)S(1)} %collective-permute-done.19.rest_5_) | copy-start | bytes 786436
  184.3 6.0 %copy-start.19 = (bf16[512,256]{1,0:T(8,128)(2,1)}, bf16[512,256]{1,0:T(8,128)(2,1)S(1)}, u32[]{:S(2)}) copy-start(bf16[512,256]{1,0:T(8,128)(2,1)S(1)} %collective-permute-done.16.rest_2_) | copy-start | bytes 786436
  191.0 11.9 %copy-start.23 = (bf16[2,16,2304]{2,1,0:T(8,128)(2,1)S(1)}, bf16[2,16,2304]{2,1,0:T(8,128)(2,1)}, u32[]{:S(2)}) copy-start(bf16[2,16,2304]{2,1,0:T(8,128)(2,1)} %get-tuple-element.78) | copy-start | bytes 442372
  191.0 12.1 %copy-start.24 = (bf16[16,2304]{1,0:T(8,128)(2,1)S(1)}, bf16[16,2304]{1,0:T(8,128)(2,1)}, u32[]{:S(2)}) copy-start(bf16[16,2304]{1,0:T(8,128)(2,1)} %get-tuple-element.79) | copy-start | bytes 221188
  191.0 12.2 %copy-start.29 = (bf16[16,512]{1,0:T(8,128)(2,1)S(1)}, bf16[16,512]{1,0:T(8,128)(2,1)}, u32[]{:S(2)}) copy-start(bf16[16,512]{1,0:T(8,128)(2,1)} %get-tuple-element.80) | copy-start | bytes 49156
  202.1 1.9 collective-permute-start.22
  204.1 14.1 %copy-start.11 = (bf16[512,1024]{1,0:T(8,128)(2,1)S(1)}, bf16[512,1024]{1,0:T(8,128)(2,1)}, u32[]{:S(2)}) copy-start(bf16[512,1024]{1,0:T(8,128)(2,1)} %get-tuple-element.52) | copy-start | bytes 3145732
  204.2 4.1 %collective-permute-start.23 = (bf16[376,128]{1,0:T(8,128)(2,1)S(1)}, bf16[376,128]{1,0:T(8,128)(2,1)S(1)}, u32[]{:S(2)}, u32[]{:S(2)}) collective-permute-start(bf16[376,128]{1,0:T(8,128)(2,1)S(1)} %get-tuple-element.150), channel_id=1, source_target_pairs={{0,2},{2,0},{4,6},{6,4},{8,10},{10,8},{12,14},{14,12},{1,3},{3,1},... | collective-permute-start | bytes 288776 | tf_op jit(solution)/shard_map/ppermute | solution.py:696
  205.2 3.7 %collective-permute-start.24 = (bf16[376,128]{1,0:T(8,128)(2,1)S(1)}, bf16[376,128]{1,0:T(8,128)(2,1)S(1)}, u32[]{:S(2)}, u32[]{:S(2)}) collective-permute-start(bf16[376,128]{1,0:T(8,128)(2,1)S(1)} %get-tuple-element.152), channel_id=1, source_target_pairs={{0,4},{2,6},{4,0},{6,2},{8,12},{10,14},{12,8},{14,10},{1,5},{3,7},... | collective-permute-start | bytes 288776 | tf_op jit(solution)/shard_map/ppermute | solution.py:696
  205.2 5.7 %collective-permute-start.25 = (bf16[376,128]{1,0:T(8,128)(2,1)S(1)}, bf16[376,128]{1,0:T(8,128)(2,1)S(1)}, u32[]{:S(2)}, u32[]{:S(2)}) collective-permute-start(bf16[376,128]{1,0:T(8,128)(2,1)S(1)} %get-tuple-element.151), channel_id=1, source_target_pairs={{0,6},{2,4},{4,2},{6,0},{8,14},{10,12},{12,10},{14,8},{1,7},{3,5},... | collective-permute-start | bytes 288776 | tf_op jit(solution)/shard_map/ppermute | solution.py:696
  211.0 3.5 %collective-permute-start.26 = (bf16[376,128]{1,0:T(8,128)(2,1)S(1)}, bf16[376,128]{1,0:T(8,128)(2,1)S(1)}, u32[]{:S(2)}, u32[]{:S(2)}) collective-permute-start(bf16[376,128]{1,0:T(8,128)(2,1)S(1)} %fusion.13), channel_id=1, source_target_pairs={{0,2},{2,0},{4,6},{6,4},{8,10},{10,8},{12,14},{14,12},{1,3},{3,1},... | collective-permute-start | bytes 288776 | tf_op jit(solution)/shard_map/ppermute | solution.py:696
  212.0 3.4 %collective-permute-start.27 = (bf16[376,128]{1,0:T(8,128)(2,1)S(1)}, bf16[376,128]{1,0:T(8,128)(2,1)S(1)}, u32[]{:S(2)}, u32[]{:S(2)}) collective-permute-start(bf16[376,128]{1,0:T(8,128)(2,1)S(1)} %fusion.13), channel_id=1, source_target_pairs={{0,4},{2,6},{4,0},{6,2},{8,12},{10,14},{12,8},{14,10},{1,5},{3,7},... | collective-permute-start | bytes 288776 | tf_op jit(solution)/shard_map/ppermute | solution.py:696
  212.1 4.7 %collective-permute-start.28 = (bf16[376,128]{1,0:T(8,128)(2,1)S(1)}, bf16[376,128]{1,0:T(8,128)(2,1)S(1)}, u32[]{:S(2)}, u32[]{:S(2)}) collective-permute-start(bf16[376,128]{1,0:T(8,128)(2,1)S(1)} %fusion.13), channel_id=1, source_target_pairs={{0,6},{2,4},{4,2},{6,0},{8,14},{10,12},{12,10},{14,8},{1,7},{3,5},... | collective-permute-start | bytes 288776 | tf_op jit(solution)/shard_map/ppermute | solution.py:696
  216.8 5.0 %copy-start.3 = (f32[512,1024]{1,0:T(8,128)S(1)}, f32[512,1024]{1,0:T(8,128)}, u32[]{:S(2)}) copy-start(f32[512,1024]{1,0:T(8,128)} %get-tuple-element.51.h) | copy-start | bytes 6291460
  217.0 4.9 %copy-start.9 = (f32[512,1024]{1,0:T(8,128)S(1)}, f32[512,1024]{1,0:T(8,128)}, u32[]{:S(2)}) copy-start(f32[512,1024]{1,0:T(8,128)} %get-tuple-element.73) | copy-start | bytes 6291460
  217.0 19.0 %collective-permute-start.29 = (bf16[4,376,128]{2,1,0:T(8,128)(2,1)S(1)}, bf16[4,376,128]{2,1,0:T(8,128)(2,1)S(1)}, u32[]{:S(2)}, u32[]{:S(2)}) collective-permute-start(bf16[4,376,128]{2,1,0:T(8,128)(2,1)S(1)} %get-tuple-element.144), channel_id=1, source_target_pairs={{0,8},{2,10},{4,12},{6,14},{8,0},{10,2},{12,4},{14,6},{1,9},{3,11}... | collective-permute-start | bytes 1155080 | tf_op jit(solution)/shard_map/ppermute | solution.py:831
  218.2 19.5 %collective-permute-start.11 = (bf16[256,1024]{1,0:T(8,128)(2,1)S(1)}, bf16[256,1024]{1,0:T(8,128)(2,1)S(1)}, u32[]{:S(2)}, u32[]{:S(2)}) collective-permute-start(bf16[256,1024]{1,0:T(8,128)(2,1)S(1)} %bitcast.264), channel_id=1, source_target_pairs={{0,1},{1,0},{2,3},{3,2},{4,5},{5,4},{6,7},{7,6},{8,9},{9,8},{10,11... | collective-permute-start | bytes 1572872 | tf_op jit(solution)/shard_map/ppermute | solution.py:693
  222.0 21.0 %collective-permute-start.20 = (bf16[256,1024]{1,0:T(8,128)(2,1)S(1)}, bf16[256,1024]{1,0:T(8,128)(2,1)S(1)}, u32[]{:S(2)}, u32[]{:S(2)}) collective-permute-start(bf16[256,1024]{1,0:T(8,128)(2,1)S(1)} %bitcast.263), channel_id=1, source_target_pairs={{0,1},{1,0},{2,3},{3,2},{4,5},{5,4},{6,7},{7,6},{8,9},{9,8},{10,11... | collective-permute-start | bytes 1572872 | tf_op jit(solution)/shard_map/ppermute | solution.py:693
  236.3 5.5 %copy-start.13 = (f32[512,1024]{1,0:T(8,128)S(1)}, f32[512,1024]{1,0:T(8,128)}, u32[]{:S(2)}) copy-start(f32[512,1024]{1,0:T(8,128)} %get-tuple-element.55) | copy-start | bytes 6291460
  236.4 17.2 %collective-permute-start.30 = (bf16[2,4,376,128]{3,2,1,0:T(8,128)(2,1)S(1)}, bf16[2,4,376,128]{3,2,1,0:T(8,128)(2,1)S(1)}, u32[]{:S(2)}, u32[]{:S(2)}) collective-permute-start(bf16[2,4,376,128]{3,2,1,0:T(8,128)(2,1)S(1)} %get-tuple-element.140), channel_id=1, source_target_pairs={{0,16},{16,0},{1,17},{17,1},{2,18},{18,2},{3,19},{19,3},{4,20},{20... | collective-permute-start | bytes 2310152 | tf_op jit(solution)/shard_map/ppermute | solution.py:835
  237.7 5.1 %copy-start.6 = (bf16[256,1024]{1,0:T(8,128)(2,1)}, bf16[256,1024]{1,0:T(8,128)(2,1)S(1)}, u32[]{:S(2)}) copy-start(bf16[256,1024]{1,0:T(8,128)(2,1)S(1)} %collective-permute-done.11) | copy-start | bytes 1572868
  238.8 4.2 %copy-start.1 = (bf16[256,1024]{1,0:T(8,128)(2,1)S(1)}, bf16[256,1024]{1,0:T(8,128)(2,1)}, u32[]{:S(2)}) copy-start(bf16[256,1024]{1,0:T(8,128)(2,1)} %copy-done) | copy-start | bytes 1572868
  238.8 4.2 %copy-start.26 = (f32[1024]{0:T(1024)S(1)}, f32[1024]{0:T(1024)}, u32[]{:S(2)}) copy-start(f32[1024]{0:T(1024)} %convert_element_type.146) | copy-start | bytes 12292
  238.8 26.3 %collective-permute-start.12 = (bf16[256,1024]{1,0:T(8,128)(2,1)}, bf16[256,1024]{1,0:T(8,128)(2,1)}, u32[]{:S(2)}, u32[]{:S(2)}) collective-permute-start(bf16[256,1024]{1,0:T(8,128)(2,1)} %fusion.8), channel_id=1, source_target_pairs={{1,8},{3,10},{5,12},{7,14},{8,1},{10,3},{12,5},{14,7},{17,24},{19,... | collective-permute-start | bytes 1572872 | tf_op jit(solution)/shard_map/ppermute | solution.py:690
  243.0 10.6 %copy-start.8 = (bf16[256,1024]{1,0:T(8,128)(2,1)}, bf16[256,1024]{1,0:T(8,128)(2,1)S(1)}, u32[]{:S(2)}) copy-start(bf16[256,1024]{1,0:T(8,128)(2,1)S(1)} %collective-permute-done.20) | copy-start | bytes 1572868
  258.5 22.5 %collective-permute-start.31 = (bf16[4,192512]{1,0:T(4,128)(2,1)}, bf16[4,192512]{1,0:T(4,128)(2,1)S(1)}, u32[]{:S(2)}, u32[]{:S(2)}) collective-permute-start(bf16[4,192512]{1,0:T(4,128)(2,1)} %reshape.436), channel_id=1, source_target_pairs={{0,1},{1,0},{2,3},{3,2},{4,5},{5,4},{6,7},{7,6},{8,9},{9,8},{10,11... | collective-permute-start | bytes 4620296 | tf_op jit(solution)/shard_map/ppermute | solution.py:693
  261.0 4.1 %copy-start.7 = (bf16[256,1024]{1,0:T(8,128)(2,1)S(1)}, bf16[256,1024]{1,0:T(8,128)(2,1)}, u32[]{:S(2)}) copy-start(bf16[256,1024]{1,0:T(8,128)(2,1)} %copy-done.6) | copy-start | bytes 1572868
  262.9 15.9 %collective-permute-start.21 = (bf16[256,1024]{1,0:T(8,128)(2,1)S(1)}, bf16[256,1024]{1,0:T(8,128)(2,1)S(1)}, u32[]{:S(2)}, u32[]{:S(2)}) collective-permute-start(bf16[256,1024]{1,0:T(8,128)(2,1)S(1)} %get-tuple-element.108), channel_id=1, source_target_pairs={{1,8},{3,10},{5,12},{7,14},{8,1},{10,3},{12,5},{14,7},{17,24},{19,... | collective-permute-start | bytes 1572872 | tf_op jit(solution)/shard_map/ppermute | solution.py:690
  (14 other events, 18.0 us)

commit v2 on v1

v2 whole, which is shorter than its diff:
```python
import functools
import math

import jax
import jax.numpy as jnp
import numpy as np
from jax import lax
from jax.experimental import pallas as pl
from jax.experimental.pallas import tpu as pltpu
from jax.sharding import PartitionSpec as P

QUERY_HEADS = 16
KEY_VALUE_HEADS = 8
HEAD_SIZE = 64
FF = 4608
ADAPTER_RANK = 16
ADAPTER_SETS = 8
CH = 128

epsilon = 1e-05
rope_base = 1000000.0

TOK = 4 * CH
PAIR = 2 * HEAD_SIZE
QW = QUERY_HEADS * HEAD_SIZE // 2
KW = KEY_VALUE_HEADS * HEAD_SIZE // 2
EW = QW + 2 * KW
GROUPS = KEY_VALUE_HEADS // 2
HF = FF // 2
TF = 768
NT = HF // TF
R = ADAPTER_RANK
MIB = 1024 * 1024
f32 = jnp.float32
bf16 = jnp.bfloat16


def mm(a, b):
    return lax.dot_general(a, b, (((1,), (0,)), ((), ())), preferred_element_type=f32)


def mm_nt(a, b):
    return lax.dot_general(a, b, (((1,), (1,)), ((), ())), preferred_element_type=f32)


def params(mib):
    return pltpu.CompilerParams(
        dimension_semantics=("arbitrary",), vmem_limit_bytes=mib * MIB
    )


def cost(flops, nbytes):
    return pl.CostEstimate(flops=int(flops), bytes_accessed=int(nbytes), transcendentals=0)


def whole(shape):
    return pl.BlockSpec(shape, lambda *_: (0,) * len(shape))


def split_dot(x, ones):
    hi = x.astype(bf16)
    lo = (x - hi.astype(f32)).astype(bf16)
    return mm(hi, ones) + mm(lo, ones)


def head_mean(x, ones):
    width = ones.shape[0]
    parts = [
        split_dot(x[:, i : i + width], ones) for i in range(0, x.shape[1], width)
    ]
    return jnp.concatenate(parts, axis=1) * (1.0 / HEAD_SIZE)


def lane_iota(shape):
    return lax.broadcasted_iota(jnp.int32, shape, len(shape) - 1)


def half_turn(x):
    width = x.shape[1]
    near = pltpu.roll(x, HEAD_SIZE // 2, 1)
    far = pltpu.roll(x, width - HEAD_SIZE // 2, 1)
    return jnp.where(lane_iota(x.shape) % HEAD_SIZE < HEAD_SIZE // 2, far, near)


def widen(table, width):
    return jnp.concatenate([table] * (width // table.shape[1]), axis=1)


def put_masked(x, out):
    rows = x.shape[0]
    left = lane_iota((rows, PAIR)) < HEAD_SIZE
    for g in range(GROUPS):
        tile = x[:, g * PAIR : (g + 1) * PAIR]
        turned = pltpu.roll(tile, HEAD_SIZE, 1)
        if g % 2 == 0:
            pair = (jnp.where(left, tile, 0.0), jnp.where(left, turned, 0.0))
        else:
            pair = (jnp.where(left, 0.0, turned), jnp.where(left, 0.0, tile))
        for j in range(2):
            out[g, j * rows : (j + 1) * rows, :] = pair[j].astype(bf16)


def in_order(core, m, o):
    a = jnp.where(core == 0, m, o)
    b = jnp.where(core == 0, o, m)
    return jnp.concatenate([a[:CH], b[:CH], a[CH:], b[CH:]], axis=0)


def lanes_at(index, depth):
    return pl.ds(pl.multiple_of(index * depth, depth), depth)


def put_tile(sc, ref, per_shard, index, value):
    shard = (index // per_shard) ^ sc[2]
    row = shard * (per_shard * R) + (index % per_shard) * R
    ref[pl.ds(pl.multiple_of(row, R), R), :] = value.astype(ref.dtype)


def flag_base(n_seq):
    return 4 + 2 * n_seq


def qkv_kernel(
    sc, mine, other, cos, sin, w_own, w_rec_q, w_rec_kv, gain, a_t, b_q, b_k, b_v, g_qk, ones,
    u_out, raw_out, qm_out, kv_out, u_s, b_s,
):
    core = sc[0]
    a = jnp.where(core == 0, mine[0], other[0])
    b = jnp.where(core == 0, other[0], mine[0])
    x = jnp.concatenate([a, b], axis=0).astype(f32)
    inv = lax.rsqrt(jnp.mean(x * x, axis=1, keepdims=True) + epsilon)
    u = (x * inv * gain[...]).astype(bf16)
    u_s[...] = u
    u_out[...] = u
    depth = w_own.shape[0]

    @pl.when(pl.program_id(0) == 0)
    def _():
        b_s[...] = jnp.zeros_like(b_s)
        b_s[0:R, 0:QW] = b_q[0]
        b_s[R : 2 * R, QW : QW + KW] = b_k[0]
        b_s[2 * R : 3 * R, QW + KW : EW] = b_v[0]

    rank = mm_nt(u, a_t[0]).astype(bf16)
    raw = mm(u_s[:, lanes_at(core, depth)], w_own[...])
    u_rec = u_s[:, lanes_at(1 - core, depth)]
    raw += jnp.concatenate([mm(u_rec, w_rec_q[...]), mm(u_rec, w_rec_kv[...])], axis=1)
    raw += mm(rank, b_s[...])
    qk = raw[:, : QW + KW]
    raw_out[...] = qk
    normed = qk * lax.rsqrt(head_mean(qk * qk, ones[...]) + epsilon) * g_qk[...]
    turned = normed * widen(cos[...], QW + KW) + half_turn(normed) * widen(sin[...], QW + KW)

    put_masked(turned[:, :QW] * (1.0 / math.sqrt(HEAD_SIZE)), qm_out)
    kv_out[...] = jnp.concatenate([turned[:, QW:], raw[:, QW + KW :]], axis=1).astype(bf16)


def qkv_call(sc, mine, other, cos, sin, w_own, w_rec_q, w_rec_kv, gain, a_t, b_q, b_k, b_v, g_qk, ones):
    rows, width = mine.shape
    depth = w_own.shape[0]
    n = TOK // 2

    def rows_spec(cols):
        return pl.BlockSpec((n, cols), lambda i, s: (i, 0))

    half_spec = pl.BlockSpec((1, rows // 2, width), lambda i, s: (i, 0, 0))
    return pl.pallas_call(
        qkv_kernel,
        grid_spec=pltpu.PrefetchScalarGridSpec(
            num_scalar_prefetch=1,
            grid=(2,),
            in_specs=[
                half_spec, half_spec,
                rows_spec(PAIR), rows_spec(PAIR),
                whole((depth, EW)), whole((depth, QW)), whole((depth, 2 * KW)),
                whole((1, width)),
                pl.BlockSpec((1, 3 * R, width), lambda i, s: (s[1], 0, 0)),
                pl.BlockSpec((1, R, QW), lambda i, s: (s[1], 0, s[0])),
                pl.BlockSpec((1, R, KW), lambda i, s: (s[1], 0, s[0])),
                pl.BlockSpec((1, R, KW), lambda i, s: (s[1], 0, s[0])),
                whole((1, QW + KW)), whole(ones.shape),
            ],
            out_specs=[
                rows_spec(width), rows_spec(QW + KW),
                pl.BlockSpec((GROUPS, TOK, PAIR), lambda i, s: (0, i, 0)),
                rows_spec(2 * KW),
            ],
            scratch_shapes=[pltpu.VMEM((n, width), bf16), pltpu.VMEM((3 * R, EW), bf16)],
        ),
        out_shape=[
            jax.ShapeDtypeStruct((TOK, width), bf16),
            jax.ShapeDtypeStruct((TOK, QW + KW), f32),
            jax.ShapeDtypeStruct((GROUPS, 2 * TOK, PAIR), bf16),
            jax.ShapeDtypeStruct((TOK, 2 * KW), bf16),
        ],
        compiler_params=params(20),
        cost_estimate=cost(1e8, 1e6),
        name="qkv",
    )(
        sc, mine.reshape(2, rows // 2, width), other.reshape(2, rows // 2, width), cos, sin,
        w_own, w_rec_q, w_rec_kv, gain, a_t, b_q, b_k, b_v, g_qk, ones,
    )


def block_mask(sc, base, first, high, keys_first):
    shape = (2 * CH, 2 * CH)
    row = lax.broadcasted_iota(jnp.int32, shape, 0)
    col = lax.broadcasted_iota(jnp.int32, shape, 1)
    q, k = (col, row) if keys_first else (row, col)

    def pick(qb, kb):
        if first and qb == kb:
            return (k <= q).astype(f32)
        flag = sc[base + qb * 2 + kb]
        flag = 1 - flag if high else flag
        return flag.astype(f32)

    by_key = [jnp.where(k < CH, pick(qb, 0), pick(qb, 1)) for qb in range(2)]
    return jnp.where(q < CH, by_key[0], by_key[1])


def attend_kernel(bases, first, sc, qm, *rest):
    kvs = rest[: 2 * len(bases)]
    if first:
        acc_out, mask, vx = rest[2 * len(bases) :]
    else:
        acc_in, acc_out, mask, vx = rest[2 * len(bases) :]
    g = pl.program_id(0)
    n = 2 * CH

    @pl.when(g == 0)
    def _():
        for i, base in enumerate(bases):
            mask[i, 0] = block_mask(sc, base, first, False, False).astype(bf16)
            mask[i, 1] = block_mask(sc, base, first, True, False).astype(bf16)
        vx[:, :, PAIR:] = jnp.ones((len(bases), TOK, PAIR), bf16)

    o_low = o_high = None
    for i in range(len(bases)):
        k, v = kvs[2 * i], kvs[2 * i + 1]
        vx[i, :, :PAIR] = v[...]
        s_high = mm_nt(qm[0, 2 * n :, :], k[...])
        s_low = mm_nt(qm[0, : 2 * n, :], k[:n, :])
        p_all = jnp.exp(s_high[:, :n]).astype(bf16)
        p_high = jnp.exp(s_high[:, n:]).astype(bf16)
        p_low = jnp.exp(s_low).astype(bf16)
        m_low, m_high = mask[i, 0], mask[i, 1]
        p_high = jnp.concatenate([p_high[:n] * m_high, p_high[n:] * m_high], axis=0)
        p_low = jnp.concatenate([p_low[:n] * m_low, p_low[n:] * m_low], axis=0)
        high = mm(jnp.concatenate([p_all, p_high], axis=1), vx[i])
        low = mm(p_low, vx[i, :n, :])
        o_high = high if i == 0 else o_high + high
        o_low = low if i == 0 else o_low + low
    left = lane_iota((n, PAIR)) < HEAD_SIZE
    even = g % 2 == 0
    for lh, o in ((0, o_low), (1, o_high)):
        rows = slice(lh * n, (lh + 1) * n)
        o0, o1 = o[:n, :PAIR], o[n:, :PAIR]
        move = pltpu.roll(jnp.where(even, o1, o0), HEAD_SIZE, 1)
        value = jnp.where(left, jnp.where(even, o0, move), jnp.where(even, move, o1))
        norm = jnp.where(left, o[:n, PAIR:], o[n:, PAIR:])
        if not first:
            value += acc_in[0, rows, :PAIR]
            norm += acc_in[0, rows, PAIR:]
        acc_out[0, rows, :PAIR] = value
        acc_out[0, rows, PAIR:] = norm


def attend_call(bases, sc, qm, kvs, acc):
    first = acc is None
    acc_spec = pl.BlockSpec((1, TOK, 2 * PAIR), lambda g, s: (g, 0, 0))
    kv_specs = [
        pl.BlockSpec((TOK, PAIR), lambda g, s: (0, g // 2)),
        pl.BlockSpec((TOK, PAIR), lambda g, s: (0, GROUPS // 2 + g // 2)),
    ]
    n = len(bases)
    return pl.pallas_call(
        functools.partial(attend_kernel, bases, first),
        grid_spec=pltpu.PrefetchScalarGridSpec(
            num_scalar_prefetch=1,
            grid=(GROUPS,),
            in_specs=[pl.BlockSpec((1, 2 * TOK, PAIR), lambda g, s: (g, 0, 0))]
            + kv_specs * n
            + ([] if first else [acc_spec]),
            out_specs=acc_spec,
            scratch_shapes=[
                pltpu.VMEM((n, 2, 2 * CH, 2 * CH), bf16),
                pltpu.VMEM((n, TOK, 2 * PAIR), bf16),
            ],
        ),
        out_shape=jax.ShapeDtypeStruct((GROUPS, TOK, 2 * PAIR), f32),
        input_output_aliases={} if first else {2 + 2 * n: 0},
        compiler_params=params(12 if n < 8 else 40),
        cost_estimate=cost(1e8, 1e6),
        name="attend",
    )(sc, qm, *[kv for kv in kvs for _ in range(2)], *([] if first else [acc]))


def head_lines(tiles, out):
    rows = tiles[0].shape[0]
    lane = lane_iota(tiles[0].shape) % HEAD_SIZE
    packed = tiles[0]
    for g in range(1, GROUPS):
        packed = jnp.where(lane == g, tiles[g], packed)
    turned = packed.T
    for g in range(GROUPS):
        for j in range(2):
            row = j * HEAD_SIZE + g
            out[g, :, j * rows : (j + 1) * rows] = turned[row : row + 1, :]


def project_kernel(sc, acc, w_o, a_o, b_o, ob_out, mix_out, lse_out):
    parts, norms = [], []
    for g in range(GROUPS):
        norm = acc[g, :, PAIR:]
        parts.append(acc[g, :, :PAIR] / norm)
        norms.append(norm)
    ob = jnp.concatenate(parts, axis=1).astype(bf16)
    ob_out[...] = ob
    head_lines(norms, lse_out)
    lse_out[...] = jnp.log(lse_out[...])
    rank = mm_nt(ob, a_o[0]).astype(bf16)
    mix_out[...] = (mm(ob, w_o[...]) + mm(rank, b_o[0])).astype(bf16)


def project_call(sc, acc, w_o, a_o, b_o):
    width = w_o.shape[1]
    n = TOK // 2
    return pl.pallas_call(
        project_kernel,
        grid_spec=pltpu.PrefetchScalarGridSpec(
            num_scalar_prefetch=1,
            grid=(2,),
            in_specs=[
                pl.BlockSpec((GROUPS, n, 2 * PAIR), lambda i, s: (0, i, 0)),
                whole(w_o.shape),
                pl.BlockSpec((1, R, QW), lambda i, s: (s[1], 0, s[0])),
                pl.BlockSpec((1, R, width), lambda i, s: (s[1], 0, 0)),
            ],
            out_specs=[
                pl.BlockSpec((n, QW), lambda i, s: (i, 0)),
                pl.BlockSpec((n, width), lambda i, s: (i, 0)),
                pl.BlockSpec((GROUPS, 1, 2 * n), lambda i, s: (0, 0, i)),
            ],
        ),
        out_shape=[
            jax.ShapeDtypeStruct((TOK, QW), bf16),
            jax.ShapeDtypeStruct((TOK, width), bf16),
            jax.ShapeDtypeStruct((GROUPS, 1, 2 * TOK), f32),
        ],
        compiler_params=params(14),
        cost_estimate=cost(1e8, 1e6),
        name="project",
    )(sc, acc, w_o, a_o, b_o)


def hidden_back_kernel(sc, c_mine, c_low, c_high, w_d, a_d, b_d, out, ed_out, drT_out, ed_s, dr_s):
    @pl.when(pl.program_id(0) == 0)
    def _():
        c_other = jnp.concatenate([c_low[...], c_high[...]], axis=0)
        ed = in_order(sc[0], c_mine[...], c_other)
        ed_s[...] = ed
        ed_out[...] = ed
        dr_s[...] = mm_nt(ed, b_d[0]).astype(bf16)
        drT_out[...] = mm_nt(b_d[0], ed).astype(bf16)

    out[...] = mm_nt(ed_s[...], w_d[...]) + mm(dr_s[...], a_d[0])


def hidden_back_call(sc, c_mine, c_low, c_high, w_d, a_d, b_d):
    rows, width = c_mine.shape
    return pl.pallas_call(
        hidden_back_kernel,
        grid_spec=pltpu.PrefetchScalarGridSpec(
            num_scalar_prefetch=1,
            grid=(NT,),
            in_specs=[
                whole((rows, width)), whole((CH, width)), whole((CH, width)),
                pl.BlockSpec((TF, width), lambda i, s: (i, 0)),
                pl.BlockSpec((1, R, TF), lambda i, s: (s[1], 0, s[0] * NT + i)),
                pl.BlockSpec((1, R, width), lambda i, s: (s[1], 0, 0)),
            ],
            out_specs=[
                pl.BlockSpec((TOK, TF), lambda i, s: (0, i)), whole((TOK, width)), whole((R, TOK)),
            ],
            scratch_shapes=[pltpu.VMEM((TOK, width), bf16), pltpu.VMEM((TOK, R), bf16)],
        ),
        out_shape=[
            jax.ShapeDtypeStruct((TOK, HF), f32),
            jax.ShapeDtypeStruct((TOK, width), bf16),
            jax.ShapeDtypeStruct((R, TOK), bf16),
        ],
        compiler_params=params(20),
        cost_estimate=cost(1e8, 1e6),
        name="hidden_back",
    )(sc, c_mine, c_low, c_high, w_d, a_d, b_d)


GU_TILES = 3 * HF // 128


def early_tiles(width):
    return GU_TILES + 4 * width // 128 + QW // 128


def ffn_kernel(
    per_shard,
    sc, mine, other, mix_a, mix_b, dh_tile, ed, drdT, gain, wg_own, wu_own, wg_rec, wu_rec, w_d,
    a_gu, b_gu, a_d, b_d,
    y_out, down_out, du_out, pay,
    u_s, down_s, du_s, rgu_s, rguT_s, rdT_s, drguT_s,
):
    i = pl.program_id(0)
    core = sc[0]
    depth = wg_own.shape[0]
    width = u_s.shape[1]
    own = lanes_at(core, depth)
    rec = lanes_at(1 - core, depth)

    @pl.when(i == 0)
    def _():
        x = in_order(core, mine[...], other[...]).astype(f32)
        h = x + (mix_a[...].astype(f32) + mix_b[...].astype(f32))
        inv = lax.rsqrt(jnp.mean(h * h, axis=1, keepdims=True) + epsilon)
        u = (h * inv * gain[...]).astype(bf16)
        u_s[...] = u
        rgu_s[...] = mm_nt(u, a_gu[0]).astype(bf16)
        rguT_s[...] = mm_nt(a_gu[0], u).astype(bf16)
        rdT_s[...] = jnp.zeros_like(rdT_s)
        drguT_s[...] = jnp.zeros_like(drguT_s)
        pay[...] = jnp.zeros_like(pay)

    u_own, u_rec = u_s[:, own], u_s[:, rec]
    gate = mm(u_own, wg_own[...]) + mm(u_rec, wg_rec[...]) + mm(rgu_s[:, :R], b_gu[0, 0])
    up = mm(u_own, wu_own[...]) + mm(u_rec, wu_rec[...]) + mm(rgu_s[:, R:], b_gu[0, 1])
    d_hid = dh_tile[...]
    sig = jax.nn.sigmoid(gate)
    silu = gate * sig
    hid = (silu * up).astype(bf16)
    e_g = (d_hid * up * (sig * (1.0 + gate * (1.0 - sig)))).astype(bf16)
    e_u = (d_hid * silu).astype(bf16)
    down = mm(hid, w_d[...])
    du_own = mm_nt(e_g, wg_own[...]) + mm_nt(e_u, wu_own[...])
    du_rec = mm_nt(e_g, wg_rec[...]) + mm_nt(e_u, wu_rec[...])

    @pl.when(i == 0)
    def _():
        down_s[...] = down
        du_s[:, own] = du_own
        du_s[:, rec] = du_rec

    @pl.when(i > 0)
    def _():
        down_s[...] += down
        du_s[:, own] += du_own
        du_s[:, rec] += du_rec

    rdT_s[...] += mm_nt(a_d[0], hid)
    drguT_s[:R, :] += mm_nt(b_gu[0, 0], e_g)
    drguT_s[R:, :] += mm_nt(b_gu[0, 1], e_u)
    grads = (mm(rguT_s[:R], e_g), mm(rguT_s[R:], e_u), mm(drdT[...], hid))
    for t in range(TF // 128):
        for q in range(3):
            index = (i * (TF // 128) + t) * 3 + q
            put_tile(sc, pay, per_shard, index, grads[q][:, t * 128 : (t + 1) * 128])

    @pl.when(i == pl.num_programs(0) - 1)
    def _():
        rdT = rdT_s[...].astype(bf16)
        drT = drguT_s[...].astype(bf16)
        tn = (((0,), (0,)), ((), ()))
        down_s[...] += lax.dot_general(rdT, b_d[0], tn, preferred_element_type=f32)
        du_out[...] = (
            du_s[...] + lax.dot_general(drT, a_gu[0], tn, preferred_element_type=f32)
        ).astype(bf16)
        for lh in range(2):
            at = slice(lh * CH, (lh + 1) * CH)
            row = pl.ds(pl.multiple_of(lh * 2 * CH + core * CH, CH), CH)
            out = pl.ds(pl.multiple_of(lh * 2 * CH + (1 - core) * CH, CH), CH)
            mix = mix_a[row, :].astype(f32) + mix_b[row, :].astype(f32)
            y_out[at, :] = (mine[at, :].astype(f32) + mix) + down_s[row, :]
            down_out[at, :] = down_s[out, :].astype(bf16)
        gb = mm(rdT, ed[...])
        ga = mm(drT, u_s[...])
        for t in range(width // 128):
            at = slice(t * 128, (t + 1) * 128)
            put_tile(sc, pay, per_shard, GU_TILES + t, gb[:, at])
            for q in range(2):
                index = GU_TILES + width // 128 + t * 2 + q
                put_tile(sc, pay, per_shard, index, ga[q * R : (q + 1) * R, at])


def ffn_call(
    half, sc, mine, other, mix_a, mix_b, d_hid, ed, drdT, gain, w_gu, w_rec, w_d, a_gu, b_gu,
    a_d, b_d,
):
    rows, width = mine.shape
    depth = w_gu.shape[0]
    per_shard = -(-early_tiles(width) // half)
    block = whole((rows, width))
    full = whole((TOK, width))
    return pl.pallas_call(
        functools.partial(ffn_kernel, per_shard),
        grid_spec=pltpu.PrefetchScalarGridSpec(
            num_scalar_prefetch=1,
            grid=(NT,),
            in_specs=[
                block, block, full, full,
                pl.BlockSpec((TOK, TF), lambda i, s: (0, i)),
                full, whole((R, TOK)), whole((1, width)),
                pl.BlockSpec((depth, TF), lambda i, s: (0, s[0] * NT + i)),
                pl.BlockSpec((depth, TF), lambda i, s: (0, 2 * NT + s[0] * NT + i)),
                pl.BlockSpec((depth, TF), lambda i, s: (0, i)),
                pl.BlockSpec((depth, TF), lambda i, s: (0, NT + i)),
                pl.BlockSpec((TF, width), lambda i, s: (i, 0)),
                pl.BlockSpec((1, 2 * R, width), lambda i, s: (s[1], 0, 0)),
                pl.BlockSpec((1, 2, R, TF), lambda i, s: (s[1], 0, 0, s[0] * NT + i)),
                pl.BlockSpec((1, R, TF), lambda i, s: (s[1], 0, s[0] * NT + i)),
                pl.BlockSpec((1, R, width), lambda i, s: (s[1], 0, 0)),
            ],
            out_specs=[block, block, full, whole((half * per_shard * R, 128))],
            scratch_shapes=[
                pltpu.VMEM((TOK, width), bf16),
                pltpu.VMEM((TOK, width), f32),
                pltpu.VMEM((TOK, width), f32),
                pltpu.VMEM((TOK, 2 * R), bf16),
                pltpu.VMEM((2 * R, TOK), bf16),
                pltpu.VMEM((R, TOK), f32),
                pltpu.VMEM((2 * R, TOK), f32),
            ],
        ),
        out_shape=[
            jax.ShapeDtypeStruct((rows, width), f32),
            jax.ShapeDtypeStruct((rows, width), bf16),
            jax.ShapeDtypeStruct((TOK, width), bf16),
            jax.ShapeDtypeStruct((half * per_shard * R, 128), bf16),
        ],
        compiler_params=params(40),
        cost_estimate=cost(1e9, 2.5e6),
        name="ffn",
    )(
        sc, mine, other, mix_a, mix_b, d_hid, ed, drdT, gain, w_gu, w_gu, w_rec, w_rec, w_d,
        a_gu, b_gu, a_d, b_d,
    )


def back_mix_kernel(
    per_shard,
    sc, mine, other, mix_a, mix_b, ed, du_a, du_b, gain, w_o, a_o, b_o, ob, ones, pay_in,
    dh_out, dom_out, delta_out, pay, dh_s, gb_s, ga_s,
):
    i = pl.program_id(0)
    core = sc[0]

    def pair(m, o):
        a = jnp.where(core == 0, m[0], o[0])
        b = jnp.where(core == 0, o[0], m[0])
        return jnp.concatenate([a, b], axis=0).astype(f32)

    hv = pair(mine, other) + (mix_a[...].astype(f32) + mix_b[...].astype(f32))
    inv = lax.rsqrt(jnp.mean(hv * hv, axis=1, keepdims=True) + epsilon)
    w = gain[...] * (du_a[...].astype(f32) + du_b[...].astype(f32))
    dh = ed[...].astype(f32) + inv * w - hv * (
        inv * inv * inv * jnp.mean(hv * w, axis=1, keepdims=True)
    )
    dh_s[...] = dh
    dh_out[...] = dh_s[pl.ds(pl.multiple_of(core * CH, CH), CH), :]
    e_o = dh.astype(bf16)
    obv = ob[...]
    dr = mm_nt(e_o, b_o[0]).astype(bf16)
    drT = mm_nt(b_o[0], e_o).astype(bf16)
    rT = mm_nt(a_o[0], obv).astype(bf16)
    gb = mm(rT, e_o)
    ga = mm(drT, obv)

    @pl.when(i == 0)
    def _():
        gb_s[...] = gb
        ga_s[...] = ga

    @pl.when(i > 0)
    def _():
        gb_s[...] += gb
        ga_s[...] += ga
        pay[...] = pay_in[...]
        n_w = dh_s.shape[1] // 128
        for t in range(n_w):
            index = GU_TILES + 3 * n_w + t
            put_tile(sc, pay, per_shard, index, gb_s[:, t * 128 : (t + 1) * 128])
        for t in range(QW // 128):
            index = GU_TILES + 4 * n_w + t
            put_tile(sc, pay, per_shard, index, ga_s[:, t * 128 : (t + 1) * 128])

    d_o = (mm_nt(e_o, w_o[...]) + mm(dr, a_o[0])).astype(bf16).astype(f32)
    prod = head_mean(d_o * obv.astype(f32), ones[...]) * HEAD_SIZE
    head_lines([prod[:, g * PAIR : (g + 1) * PAIR] for g in range(GROUPS)], delta_out)
    put_masked(d_o, dom_out)


def back_mix_call(
    half, sc, mine, other, mix_a, mix_b, ed, du_a, du_b, gain, w_o, a_o, b_o, ob, ones, pay,
):
    rows, width = mine.shape
    per_shard = -(-early_tiles(width) // half)
    n = TOK // 2
    block = pl.BlockSpec((1, rows // 2, width), lambda i, s: (i, 0, 0))
    full = pl.BlockSpec((n, width), lambda i, s: (i, 0))

    def two(v):
        return v.reshape(2, rows // 2, width)

    return pl.pallas_call(
        functools.partial(back_mix_kernel, per_shard),
        grid_spec=pltpu.PrefetchScalarGridSpec(
            num_scalar_prefetch=1,
            grid=(2,),
            in_specs=[
                block, block, full, full, full, full, full,
                whole((1, width)), whole(w_o.shape),
                pl.BlockSpec((1, R, QW), lambda i, s: (s[1], 0, s[0])),
                pl.BlockSpec((1, R, width), lambda i, s: (s[1], 0, 0)),
                pl.BlockSpec((n, QW), lambda i, s: (i, 0)),
                whole(ones.shape), whole(pay.shape),
            ],
            out_specs=[
                pl.BlockSpec((rows // 2, width), lambda i, s: (i, 0)),
                pl.BlockSpec((GROUPS, TOK, PAIR), lambda i, s: (0, i, 0)),
                pl.BlockSpec((GROUPS, 1, 2 * n), lambda i, s: (0, 0, i)),
                whole(pay.shape),
            ],
            scratch_shapes=[
                pltpu.VMEM((n, width), f32), pltpu.VMEM((R, width), f32), pltpu.VMEM((R, QW), f32),
            ],
        ),
        out_shape=[
            jax.ShapeDtypeStruct((rows, width), f32),
            jax.ShapeDtypeStruct((GROUPS, 2 * TOK, PAIR), bf16),
            jax.ShapeDtypeStruct((GROUPS, 1, 2 * TOK), f32),
            jax.ShapeDtypeStruct(pay.shape, pay.dtype),
        ],
        input_output_aliases={14: 3},
        compiler_params=params(24),
        cost_estimate=cost(1e8, 1e6),
        name="back_mix",
    )(
        sc, two(mine), two(other), mix_a, mix_b, ed, du_a, du_b, gain,
        w_o, a_o, b_o, ob, ones, pay,
    )


def attend_back_kernel(base, first, has_dq, sc, qm, dom, k, v, lse, delta, *rest):
    if has_dq:
        dq_in, dq_out, dkv_out, dkv, kt, mask = rest
    else:
        dq_out, dkv_out, dkv, kt, mask = rest
    g = pl.program_id(0)
    side = g % 2
    n = 2 * CH

    @pl.when(g == 0)
    def _():
        mask[0] = block_mask(sc, base, first, False, True)
        mask[1] = block_mask(sc, base, first, True, True)

    @pl.when(side == 0)
    def _():
        kt[...] = k[...].astype(f32).T.astype(bf16)

    kth = kt.at[pl.ds(pl.multiple_of(side * HEAD_SIZE, HEAD_SIZE), HEAD_SIZE), :]
    q_all, do_all = qm[0], dom[0]
    q_high, do_high = qm[0, 2 * n :, :], dom[0, 2 * n :, :]
    s_low = mm_nt(k[:n, :], q_all)
    s_high = mm_nt(k[n:, :], q_high)
    dp_low = mm_nt(v[:n, :], do_all)
    dp_high = mm_nt(v[n:, :], do_high)
    m_low, m_high = mask[0], mask[1]
    lse_all, delta_all = lse[0], delta[0]
    p_low = jnp.exp(s_low - lse_all)
    p_low = jnp.concatenate(
        [p_low[:, :n] * m_low, p_low[:, n : 2 * n] * m_low, p_low[:, 2 * n :]], axis=1
    )
    p_high = jnp.exp(s_high - lse_all[:, 2 * n :])
    p_high = jnp.concatenate([p_high[:, :n] * m_high, p_high[:, n:] * m_high], axis=1)
    ds_low = (p_low * (dp_low - delta_all)).astype(bf16)
    ds_high = (p_high * (dp_high - delta_all[:, 2 * n :])).astype(bf16)
    p_low, p_high = p_low.astype(bf16), p_high.astype(bf16)
    dk_low, dk_high = mm(ds_low, q_all), mm(ds_high, q_high)
    dv_low, dv_high = mm(p_low, do_all), mm(p_high, do_high)
    dq_low = mm(kth[:, :n], ds_low)
    dq_high = mm(kth[:, n:], ds_high)
    dq = jnp.concatenate([dq_low[:, : 2 * n], dq_low[:, 2 * n :] + dq_high], axis=1)
    dq_out[0] = dq_in[0] + dq if has_dq else dq

    @pl.when(side == 0)
    def _():
        dkv[0, :n, :] = dk_low
        dkv[0, n:, :] = dk_high
        dkv[1, :n, :] = dv_low
        dkv[1, n:, :] = dv_high

    @pl.when(side == 1)
    def _():
        dkv_out[0, :n, :] = (dkv[0, :n, :] + dk_low).astype(dkv_out.dtype)
        dkv_out[0, n:, :] = (dkv[0, n:, :] + dk_high).astype(dkv_out.dtype)
        dkv_out[1, :n, :] = (dkv[1, :n, :] + dv_low).astype(dkv_out.dtype)
        dkv_out[1, n:, :] = (dkv[1, n:, :] + dv_high).astype(dkv_out.dtype)


def attend_back_call(base, first, sc, qm, dom, kv, lse, delta, dq):
    has_dq = dq is not None
    dq_spec = pl.BlockSpec((1, HEAD_SIZE, 2 * TOK), lambda g, s: (g, 0, 0))
    row_spec = pl.BlockSpec((1, 1, 2 * TOK), lambda g, s: (g, 0, 0))
    return pl.pallas_call(
        functools.partial(attend_back_kernel, base, first, has_dq),
        grid_spec=pltpu.PrefetchScalarGridSpec(
            num_scalar_prefetch=1,
            grid=(GROUPS,),
            in_specs=[
                pl.BlockSpec((1, 2 * TOK, PAIR), lambda g, s: (g, 0, 0)),
                pl.BlockSpec((1, 2 * TOK, PAIR), lambda g, s: (g, 0, 0)),
                pl.BlockSpec((TOK, PAIR), lambda g, s: (0, g // 2)),
                pl.BlockSpec((TOK, PAIR), lambda g, s: (0, GROUPS // 2 + g // 2)),
                row_spec, row_spec,
            ]
            + ([dq_spec] if has_dq else []),
            out_specs=[dq_spec, pl.BlockSpec((2, TOK, PAIR), lambda g, s: (0, 0, g // 2))],
            scratch_shapes=[
                pltpu.VMEM((2, TOK, PAIR), f32),
                pltpu.VMEM((PAIR, TOK), bf16),
                pltpu.VMEM((2, 2 * CH, 2 * CH), f32),
            ],
        ),
        out_shape=[
            jax.ShapeDtypeStruct((GROUPS, HEAD_SIZE, 2 * TOK), f32),
            jax.ShapeDtypeStruct((2, TOK, KW), f32 if first else bf16),
        ],
        input_output_aliases={7: 0} if has_dq else {},
        compiler_params=params(16),
        cost_estimate=cost(1e8, 1e6),
        name="attend_back",
    )(sc, qm, dom, kv, kv, lse, delta, *([dq] if has_dq else []))


def late_tiles(width):
    return 4 * width // 128


def qkv_back_kernel(per_shard, parts, sc, dq, dkv, *rest):
    got = rest[:parts]
    (raw, cos, sin, g_qk, ones, u, w_own, w_rec_q, w_rec_kv, a_t, b_q, b_k, b_v,
     du_out, send_out, pay, e_s, b_s, du_s, ga_s, gb_s) = rest[parts:]
    i = pl.program_id(0)
    core = sc[0]
    width = QW + KW

    @pl.when(i == 0)
    def _():
        b_s[...] = jnp.zeros_like(b_s)
        b_s[0:R, 0:QW] = b_q[0]
        b_s[R : 2 * R, QW:width] = b_k[0]
        b_s[2 * R : 3 * R, width:EW] = b_v[0]
        ga_s[...] = jnp.zeros_like(ga_s)
        gb_s[...] = jnp.zeros_like(gb_s)
        pay[...] = jnp.zeros_like(pay)

    m = dq.shape[2] // 2
    heads = [dq[g, :, j * m : (j + 1) * m] for g in range(GROUPS) for j in range(2)]
    d_q = jnp.concatenate(heads, axis=0).T * (1.0 / math.sqrt(HEAD_SIZE))
    d_k, d_v = dkv[0], dkv[1]
    for n in range(parts):
        d_k = d_k + got[n][0].astype(f32)
        d_v = d_v + got[n][1].astype(f32)
    grad = jnp.concatenate([d_q, d_k], axis=1)
    grad = grad * widen(cos[...], width) - half_turn(grad) * widen(sin[...], width)
    v = raw[...]
    inv = lax.rsqrt(head_mean(v * v, ones[...]) + epsilon)
    w = grad * g_qk[...]
    grad = inv * w - v * (inv * inv * inv) * head_mean(v * w, ones[...])
    e_s[:, :width] = grad.astype(bf16)
    e_s[:, width:] = d_v.astype(bf16)
    e = e_s[...]
    uv = u[...]
    dr = mm_nt(e, b_s[...]).astype(bf16)
    drT = mm_nt(b_s[...], e).astype(bf16)
    rT = mm_nt(a_t[0], uv).astype(bf16)
    gb_s[...] += mm(rT, e)
    ga_s[...] += mm(drT, uv)
    depth = w_own.shape[0]
    du_s[...] = mm(dr, a_t[0])
    du_s[:, lanes_at(core, depth)] += mm_nt(e, w_own[...])
    du_s[:, lanes_at(1 - core, depth)] += mm_nt(e[:, :QW], w_rec_q[...]) + mm_nt(
        e[:, QW:], w_rec_kv[...]
    )
    du_out[...] = du_s[pl.ds(pl.multiple_of(core * CH, CH), CH), :]
    send_out[...] = du_s[pl.ds(pl.multiple_of((1 - core) * CH, CH), CH), :].astype(bf16)

    @pl.when(i == pl.num_programs(0) - 1)
    def _():
        n = uv.shape[1] // 128
        for t in range(n):
            at = slice(t * 128, (t + 1) * 128)
            for q in range(3):
                put_tile(sc, pay, per_shard, t * 3 + q, ga_s[q * R : (q + 1) * R, at])
        for t in range(EW // 128):
            at = slice(t * 128, (t + 1) * 128)
            q = 0 if t < QW // 128 else (1 if t < width // 128 else 2)
            put_tile(sc, pay, per_shard, 3 * n + t, gb_s[q * R : (q + 1) * R, at])


def qkv_back_call(
    half, sc, dq, dkv, got, raw, cos, sin, g_qk, ones, u, w_own, w_rec_q, w_rec_kv, a_t, b_q, b_k,
    b_v,
):
    width = u.shape[1]
    depth = w_own.shape[0]
    parts = len(got)
    n = TOK // 2
    per_shard = -(-late_tiles(width) // half)

    def rows_spec(cols):
        return pl.BlockSpec((n, cols), lambda i, s: (i, 0))

    dkv_spec = pl.BlockSpec((2, n, KW), lambda i, s: (0, i, 0))
    half_spec = pl.BlockSpec((CH, width), lambda i, s: (i, 0))
    return pl.pallas_call(
        functools.partial(qkv_back_kernel, per_shard, parts),
        grid_spec=pltpu.PrefetchScalarGridSpec(
            num_scalar_prefetch=1,
            grid=(2,),
            in_specs=[pl.BlockSpec((GROUPS, HEAD_SIZE, 2 * n), lambda i, s: (0, 0, i)), dkv_spec]
            + [dkv_spec] * parts
            + [
                rows_spec(QW + KW), rows_spec(PAIR), rows_spec(PAIR), whole(g_qk.shape),
                whole(ones.shape), rows_spec(width), whole(w_own.shape),
                whole(w_rec_q.shape), whole(w_rec_kv.shape),
                pl.BlockSpec((1, 3 * R, width), lambda i, s: (s[1], 0, 0)),
                pl.BlockSpec((1, R, QW), lambda i, s: (s[1], 0, s[0])),
                pl.BlockSpec((1, R, KW), lambda i, s: (s[1], 0, s[0])),
                pl.BlockSpec((1, R, KW), lambda i, s: (s[1], 0, s[0])),
            ],
            out_specs=[half_spec, half_spec, whole((half * per_shard * R, 128))],
            scratch_shapes=[
                pltpu.VMEM((n, EW), bf16), pltpu.VMEM((3 * R, EW), bf16),
                pltpu.VMEM((n, width), f32), pltpu.VMEM((3 * R, width), f32),
                pltpu.VMEM((3 * R, EW), f32),
            ],
        ),
        out_shape=[
            jax.ShapeDtypeStruct((TOK // 2, width), f32),
            jax.ShapeDtypeStruct((TOK // 2, width), bf16),
            jax.ShapeDtypeStruct((half * per_shard * R, 128), bf16),
        ],
        compiler_params=params(24),
        cost_estimate=cost(1e8, 1e6),
        name="qkv_back",
    )(
        sc, dq, dkv, *got, raw, cos, sin, g_qk, ones, u, w_own, w_rec_q, w_rec_kv, a_t, b_q, b_k,
        b_v,
    )


def norm_back_kernel(x, du, got, dh, gain, out, low_out):
    v = x[...].astype(f32)
    inv = lax.rsqrt(jnp.mean(v * v, axis=1, keepdims=True) + epsilon)
    w = (du[...] + got[...].astype(f32)) * gain[...]
    grad = dh[...] + inv * w - v * (inv * inv * inv * jnp.mean(v * w, axis=1, keepdims=True))
    out[...] = grad
    low_out[...] = grad.astype(bf16)


def norm_back_call(x, du, got, dh, gain):
    rows, width = x.shape
    spec = pl.BlockSpec((rows // 2, width), lambda i: (i, 0))
    return pl.pallas_call(
        norm_back_kernel,
        grid=(2,),
        in_specs=[spec, spec, spec, spec, pl.BlockSpec((1, width), lambda i: (0, 0))],
        out_specs=[spec, spec],
        out_shape=[
            jax.ShapeDtypeStruct((rows, width), f32),
            jax.ShapeDtypeStruct((rows, width), bf16),
        ],
        compiler_params=params(10),
        cost_estimate=cost(1e7, 1e6),
        name="norm_back",
    )(x, du, got, dh, gain)


def home_kernel(stays, own, back, out):
    v = jnp.where(stays[0] == 1, own[...], back[...].astype(f32))
    n = v.shape[1] // 128
    for t in range(n):
        out[pl.ds(t, v.shape[0], stride=n), :] = v[:, t * 128 : (t + 1) * 128]


def home_call(stays, own, back):
    rows, width = own.shape
    n = width // 128
    spec = pl.BlockSpec((rows // 2, width), lambda i, s: (i, 0))
    out = pl.pallas_call(
        home_kernel,
        grid_spec=pltpu.PrefetchScalarGridSpec(
            num_scalar_prefetch=1,
            grid=(2,),
            in_specs=[spec, spec],
            out_specs=pl.BlockSpec((rows // 2 * n, 128), lambda i, s: (i, 0)),
        ),
        out_shape=jax.ShapeDtypeStruct((rows * n, 128), f32),
        compiler_params=params(8),
        cost_estimate=cost(1e7, 1e6),
        name="home",
    )(stays, own, back)
    return out.reshape(rows, 1, width)


def place_kernel(pieces, half, n_seq, per_shard, sc, own_core, twin, *rest):
    outs, box, sem = rest[:-2], rest[-2], rest[-1]
    core, place, own = sc[0], sc[2], sc[3]
    which = pl.program_id(0)
    parts, _, group = own_core.shape[:3]

    @pl.when(which == 0)
    def _():
        copies = []
        for c, source in enumerate((own_core, twin)):
            for part in range(parts):
                for k in range(half):
                    copies.append(
                        pltpu.make_async_copy(
                            source.at[part, k],
                            box.at[core ^ c, place ^ k, pl.ds(part * group, group)],
                            sem.at[(c * parts + part) * half + k],
                        )
                    )
        for copy in copies:
            copy.start()
        for copy in copies:
            copy.wait()

    for out in outs:
        out[...] = jnp.zeros_like(out)
    for b in range(2 * n_seq):
        rel = own ^ b

        @pl.when(sc[4 + b] == which)
        def _():
            for c in range(2):
                for index, target, lead, lane, shift in pieces:
                    at = lane + c * shift
                    rows = slice((index % per_shard) * R, (index % per_shard + 1) * R)
                    value = box[c, index // per_shard, rel, rows, :].astype(f32)
                    outs[target][(0,) + lead + (slice(at, at + 128),)] += value


def place_call(pieces, shapes, n_seq, sc, own_core, twin):
    parts, half, _, rows, _ = own_core.shape

    def out_spec(shape):
        zeros = (0,) * len(shape)
        return pl.BlockSpec((1,) + shape, lambda i, s: (i,) + zeros)

    return pl.pallas_call(
        functools.partial(place_kernel, pieces, half, n_seq, rows // R),
        grid_spec=pltpu.PrefetchScalarGridSpec(
            num_scalar_prefetch=1,
            grid=(ADAPTER_SETS,),
            in_specs=[pl.BlockSpec(memory_space=pl.ANY)] * 2,
            out_specs=[out_spec(shape) for shape in shapes],
            scratch_shapes=[
                pltpu.VMEM((2, half, 2 * n_seq, rows, 128), bf16),
                pltpu.SemaphoreType.DMA((2 * parts * half,)),
            ],
        ),
        out_shape=[jax.ShapeDtypeStruct((ADAPTER_SETS,) + shape, f32) for shape in shapes],
        compiler_params=params(24),
        cost_estimate=cost(1e7, 1e6),
        name="place",
    )(sc, own_core, twin)


def rope_parts():
    freq = np.exp(-math.log(rope_base) * 2.0 * np.arange(HEAD_SIZE // 2) / HEAD_SIZE)
    angle = np.arange(CH)[:, None] * freq[None, :]
    return freq, np.cos(angle).astype(np.float32), np.sin(angle).astype(np.float32)


def rope_tables(stretches):
    freq, cos_t, sin_t = rope_parts()
    angle = (stretches.astype(f32) * CH)[:, None] * jnp.asarray(freq.astype(np.float32))[None, :]
    cos_a, sin_a = jnp.cos(angle)[:, None, :], jnp.sin(angle)[:, None, :]
    cos = cos_a * cos_t[None] - sin_a * sin_t[None]
    sin = sin_a * cos_t[None] + cos_a * sin_t[None]
    return (
        jnp.concatenate([cos, cos, cos, cos], axis=-1).reshape(TOK, PAIR),
        jnp.concatenate([-sin, sin, -sin, sin], axis=-1).reshape(TOK, PAIR),
    )


def after(value, *earlier):
    return lax.optimization_barrier((value,) + earlier)[0]


def per_device(
    hidden_in, cotangent, query_key_value_weight, w_o, w_gu, w_down, g_attn, g_ffn, g_q,
    key_norm_gain, a_qkv, b_q, key_up_weight, value_up_weight, a_o, b_o, a_gu, b_gu, a_down,
    b_down, set_index, stretch_order,
):
    rows, _, width = hidden_in.shape
    n_ctx = lax.axis_size("ctx")
    n_seq = lax.axis_size("seq")
    half = n_ctx // 2
    core = lax.axis_index("wsh")
    ctx = lax.axis_index("ctx")
    side = ctx // half
    place = ctx % half
    own_seq = lax.axis_index("seq") * 2 + side
    stays = core == side

    def line(s, p, c):
        return (s * half + p) * 2 + c

    swap_pairs = [
        (line(s, p, c), line(c, p, s))
        for s in range(2) for p in range(half) for c in range(2) if s != c
    ]

    def swap(v):
        return lax.ppermute(v, ("ctx", "wsh"), swap_pairs)

    def other_core(v):
        return lax.ppermute(v, "wsh", [(0, 1), (1, 0)])

    def partner(v, k):
        return lax.ppermute(
            v, "ctx", [(s * half + p, s * half + (p ^ k)) for s in range(2) for p in range(half)]
        )

    def other_seq(v, d):
        pairs = [
            (s * n_ctx + i, (s ^ (d // 2)) * n_ctx + (i + half * (d % 2)) % n_ctx)
            for s in range(n_seq) for i in range(n_ctx)
        ]
        return lax.ppermute(v, ("seq", "ctx"), pairs)

    hid = hidden_in.reshape(rows, width)
    cot = cotangent.reshape(rows, width)
    mine = jnp.where(stays, hid, swap(hid))
    order = jnp.where(stays, stretch_order[0], swap(stretch_order)[0])
    other = other_core(mine)

    query_key_value_weight = after(query_key_value_weight, order)

    def cols(w, start, size, which):
        return lax.dynamic_slice_in_dim(w, start + which * size, size, 1)

    def qkv_cols(which):
        return jnp.concatenate(
            [
                cols(query_key_value_weight, 0, QW, which),
                cols(query_key_value_weight, 2 * QW, KW, which),
                cols(query_key_value_weight, 2 * QW + 2 * KW, KW, which),
            ],
            axis=1,
        )

    w_own = qkv_cols(core)
    w_send = after(qkv_cols(1 - core), mine)
    w_rec_q, w_rec_kv = other_core(w_send[:, :QW]), other_core(w_send[:, QW:])

    own_set = lax.dynamic_index_in_dim(set_index, own_seq, keepdims=False)
    low = order.reshape(2, half, 2)
    here = lax.dynamic_index_in_dim(low, place, 1, keepdims=False)
    flags = []
    for k in range(half):
        there = lax.dynamic_index_in_dim(low, place ^ k, 1, keepdims=False)
        flags.append((there[None, :, 0] < here[:, None, 0]).astype(jnp.int32).reshape(4))
    sc = jnp.concatenate(
        [jnp.stack([core, own_set, place, own_seq]).astype(jnp.int32), set_index] + flags
    )
    base = flag_base(n_seq)
    cos, sin = rope_tables(here.T.reshape(4))
    ones = jnp.asarray(np.kron(np.eye(4), np.ones((HEAD_SIZE, HEAD_SIZE))), bf16)
    gain_a = g_attn.astype(f32)[None]
    gain_f = g_ffn.astype(f32)[None]
    g_qk = jnp.concatenate(
        [jnp.tile(g_q, QW // HEAD_SIZE), jnp.tile(key_norm_gain, KW // HEAD_SIZE)]
    ).astype(f32)[None]
    a_qkv_t = jnp.swapaxes(a_qkv, 1, 2)
    a_o_t = jnp.swapaxes(a_o, 1, 2)
    a_gu_t = jnp.swapaxes(a_gu, 1, 2)
    a_down_t = jnp.swapaxes(a_down, 1, 2)

    u, raw, qm, kv = qkv_call(
        sc, mine, other, cos, sin, w_own, w_rec_q, w_rec_kv, gain_a, a_qkv_t, b_q, key_up_weight,
        value_up_weight, g_qk, ones,
    )
    kvs = [kv] + [partner(kv, k) for k in range(1, half)]
    acc = attend_call([base], sc, qm, [kv], None)
    cot = after(cot, mine)
    c_mine = jnp.where(stays, cot, swap(cot))
    c_sent = after(c_mine, acc)
    d_hid, ed, drdT = hidden_back_call(
        sc, c_mine, other_core(c_sent[:CH]), other_core(c_sent[CH:]), w_down, a_down_t, b_down
    )
    w_gu_late = after(w_gu, kv)
    gu_send = jnp.concatenate(
        [cols(w_gu_late, 0, HF, 1 - core), cols(w_gu_late, FF, HF, 1 - core)], axis=1
    )
    gu_rec = other_core(after(gu_send, d_hid, *kvs))
    acc = attend_call(
        [base + 4 * k for k in range(1, half)], sc, qm, kvs[1:], after(acc, d_hid, gu_send)
    )
    ob, mix, lse = project_call(sc, acc, w_o, a_o_t, b_o)
    mix_got = other_core(mix)
    y, down, du, pay_early = ffn_call(
        half, sc, mine, other, mix, mix_got, d_hid, ed, drdT, gain_f, w_gu, gu_rec, w_down,
        a_gu_t, b_gu, a_down_t, b_down,
    )
    dh, dom, delta, pay_early = back_mix_call(
        half, sc, mine, other, mix, mix_got, ed, du, other_core(du), gain_f, w_o, a_o_t, b_o, ob,
        ones, pay_early,
    )

    def summed(pay):
        shards = pay.reshape(half, -1, 128)
        total = shards[0].astype(f32)
        for k in range(1, half):
            total += partner(shards[k], k).astype(f32)
        return total.astype(bf16)

    dq = None
    got = []
    early = summed(pay_early)
    for k in list(range(1, half)) + [0]:
        dq, dkv = attend_back_call(base + 4 * k, k == 0, sc, qm, dom, kvs[k], lse, delta, dq)
        if k:
            got.append(partner(dkv, k))
        if k == half - 2:
            dq = after(dq, early)
    early = jnp.stack([early, other_seq(early, 1)])
    early = after(early, dq, *got)
    early_got = [early] + [partner(early, k) for k in range(1, half)]

    du_own, du_send, pay_late = qkv_back_call(
        half, sc, dq, dkv, got, raw, cos, sin, g_qk, ones, u, w_own, w_rec_q, w_rec_kv, a_qkv_t, b_q,
        key_up_weight, value_up_weight,
    )
    early = jnp.stack([after(v, pay_late) for v in early_got])
    early_got = [early] + [other_seq(early, 2 * d) for d in range(1, n_seq)]
    late = summed(pay_late)
    late = jnp.stack([late] + [other_seq(late, d) for d in range(1, 2 * n_seq)])
    early = jnp.stack([after(v, late) for v in early_got])
    early_twin = other_core(early)

    layer = y + other_core(after(down, dom)).astype(f32)
    stay_flag = stays.astype(jnp.int32).reshape(1)
    layer_out = home_call(stay_flag, layer, swap(layer.astype(bf16)))

    n_w = width // 128
    pieces = []
    for t in range(HF // 128):
        for q in range(2):
            pieces.append((t * 3 + q, 0, (q, slice(0, R)), t * 128, HF))
        pieces.append((t * 3 + 2, 1, (slice(0, R),), t * 128, HF))
    for t in range(n_w):
        pieces.append((GU_TILES + t, 2, (slice(0, R),), t * 128, 0))
        for q in range(2):
            rows_at = (slice(q * R, (q + 1) * R),)
            pieces.append((GU_TILES + n_w + t * 2 + q, 3, rows_at, t * 128, 0))
    for t in range(n_w):
        pieces.append((GU_TILES + 3 * n_w + t, 4, (slice(0, R),), t * 128, 0))
    for t in range(QW // 128):
        pieces.append((GU_TILES + 4 * n_w + t, 5, (slice(0, R),), t * 128, QW))
    r_gu, r_ad, r_bd, r_agu, r_bo, r_ao = place_call(
        pieces,
        [(2, R, FF), (R, FF), (R, width), (2 * R, width), (R, width), (R, 2 * QW)],
        n_seq, sc, early, early_twin,
    )

    late = jnp.stack([late] + [partner(late, k) for k in range(1, half)])[None]
    late_twin = after(other_core(late), r_gu)
    grad_in, grad_low = norm_back_call(mine, du_own, other_core(du_send), dh, gain_a)
    input_grad = home_call(stay_flag, grad_in, swap(grad_low))

    pieces = []
    first_rows = (slice(0, R),)
    for t in range(n_w):
        for q in range(3):
            pieces.append((t * 3 + q, 0, (slice(q * R, (q + 1) * R),), t * 128, 0))
    for t in range(EW // 128):
        at = 3 * n_w + t
        if t < QW // 128:
            pieces.append((at, 1, first_rows, t * 128, QW))
        elif t < (QW + KW) // 128:
            pieces.append((at, 2, first_rows, t * 128 - QW, KW))
        else:
            pieces.append((at, 3, first_rows, t * 128 - QW - KW, KW))
    r_aqkv, r_bq, r_bk, r_bv = place_call(
        pieces,
        [(3 * R, width), (R, 2 * QW), (R, 2 * KW), (R, 2 * KW)],
        n_seq, sc, late, late_twin,
    )
    return (
        layer_out,
        input_grad,
        jnp.swapaxes(r_aqkv, 1, 2),
        r_bq,
        r_bk,
        r_bv,
        jnp.swapaxes(r_ao, 1, 2),
        r_bo,
        jnp.swapaxes(r_agu, 1, 2),
        r_gu,
        jnp.swapaxes(r_ad, 1, 2),
        r_bd,
    )


def solution(mesh):
    tokens = P("ctx", ("seq", "wsh"), None)
    in_specs = (
        (tokens, tokens) + (P("wsh", None),) * 4 + (P(),) * 15 + (P(("seq", "wsh"), None),)
    )
    out_specs = (tokens, tokens) + (P(),) * 10
    return jax.shard_map(
        per_device, mesh=mesh, in_specs=in_specs, out_specs=out_specs, check_vma=False
    )
```

time: 303 us -> 240 us (0.79); the launches traced: 298 us -> 240 us
  other arithmetic: 29.5 us -> 7.08 us
  Pallas kernels: 128 us -> 111 us
  local copies, waits for them, and re-layouts: 30 us -> 14.7 us
  waiting for transfers between devices: 66.1 us -> 60 us
  starting transfers between devices: 42.5 us -> 45.7 us
    pallas_call x4, Pallas kernels: 35.3 us -> 24.6 us  [attend_back_call(): pl.pallas_call(functools.partial(attend_back_kernel, base, first, has_dq)...]
    add x6 -> x0, other arithmetic: 9.31 us -> none  [place_sets(): out += onehot[:, n].reshape(shape) * v[n][None]]
    ppermute x12 -> x17, waiting for transfers between devices: 28.2 us -> 22.6 us  [the longest x5 15.4 us: other_seq(): return lax.ppermute(v, ('seq', 'ctx'), pairs)]
    unnamed x114 -> x74, local copies, waits for them, and re-layouts: 11.6 us -> 6.09 us
    reshape x5 -> x0, local copies, waits for them, and re-layouts: 5.35 us -> none  [the longest x1 3.09 us: per_device(): lines = lines.reshape(2 * n_seq, -1)]
    ppermute x15 -> x18, starting transfers between devices: 13.3 us -> 17.6 us  [partner(): lax.ppermute(v, 'ctx', [(s * half + p, s * half + (p ^ k)) for s in range...]
    pallas_call x1, Pallas kernels: 8.64 us -> 4.86 us  [qkv_call(): pl.pallas_call(qkv_kernel, grid_spec=pltpu.PrefetchScalarGridSpec(num_sca...]
    pallas_call x1, Pallas kernels: 5.91 us -> 2.41 us  [project_call(): pl.pallas_call(project_kernel, grid_spec=pltpu.PrefetchScalarGridSpec(num...]
  transfers between devices with their start and end apart: 32 -> 40, of which waited for: 18 -> 15; matrix products, arithmetic and copies ran while one was open for 11% -> 6% of each run, Pallas kernels for 18% -> 29%
where the time goes in v2:
time: 240 us
  Pallas kernels  111 us (46%)
  waiting for transfers between devices  60 us (25%)
  starting transfers between devices  45.7 us (19%)
  local copies, waits for them, and re-layouts  14.7 us (6%)
  other arithmetic  7.08 us (3%)
    pallas_call x1, Pallas kernels, ffn_call(): pl.pallas_call(functools.partial(ffn_kernel, per_shard), grid_spec=pltpu....  29.2 us
    pallas_call x4, Pallas kernels, attend_back_call(): pl.pallas_call(functools.partial(attend_back_kernel, base, first, has_dq)...  24.6 us
    ppermute x5, waiting for transfers between devices, swap(): return lax.ppermute(v, ('ctx', 'wsh'), swap_pairs)  23.2 us
    ppermute x18, starting transfers between devices, partner(): lax.ppermute(v, 'ctx', [(s * half + p, s * half + (p ^ k)) for s in range...  17.6 us
    ppermute x5, starting transfers between devices, swap(): return lax.ppermute(v, ('ctx', 'wsh'), swap_pairs)  16 us
    pallas_call x2, Pallas kernels, place_call(): pl.pallas_call(functools.partial(place_kernel, pieces, half, n_seq, rows...  15.6 us
    ppermute x5, waiting for transfers between devices, other_seq(): return lax.ppermute(v, ('seq', 'ctx'), pairs)  15.4 us
    ppermute x18, waiting for transfers between devices, partner(): lax.ppermute(v, 'ctx', [(s * half + p, s * half + (p ^ k)) for s in range...  14.3 us
  transfers between devices with their start and end apart: 40, of which 15 were waited for; matrix products, arithmetic and copies ran while one was open for 6% of the time, Pallas kernels for 29%

profile of v2, /device:TPU:1, one launch (start us, length us, event | category | flops | bytes accessed | tf_op | source)
XLA Modules:
  0.0 239.8 jit_solution(15608663381815140945)
XLA Ops:
  0.7 5.7 %collective-permute-start.1 = (bf16[256,1024]{1,0:T(8,128)(2,1)}, bf16[256,1024]{1,0:T(8,128)(2,1)}, u32[]{:S(2)}, u32[]{:S(2)}) collective-permute-start(bf16[256,1024]{1,0:T(8,128)(2,1)} %bitcast.73), channel_id=1, source_target_pairs={{1,8},{3,10},{5,12},{7,14},{8,1},{10,3},{12,5},{14,7},{17,24},{19,... | collective-permute-start | bytes 1572872 | tf_op jit(solution)/shard_map/ppermute | solution.py:1028
  6.4 1.9 collective-permute-start
  8.4 0.7 tile.4
  9.1 0.7 tile.5
  9.9 0.7 broadcast_in_dim.23
  10.6 1.2 dynamic_slice.42
  11.8 1.3 constant_dynamic-slice_fusion.4
  13.6 5.6 %collective-permute-done = s32[1,16]{1,0:T(1,128)S(1)} collective-permute-done((s32[1,16]{1,0:T(1,128)}, s32[1,16]{1,0:T(1,128)S(1)}, u32[]{:S(2)}, u32[]{:S(2)}) %collective-permute-start) | collective-permute-done | bytes 96 | tf_op jit(solution)/shard_map/ppermute | solution.py:1028
  20.2 0.7 concatenate.34.sc
  21.1 1.1 broadcast_select_fusion.1.mine.x
  22.4 0.6 collective-permute-start.3
  23.1 1.9 collective-permute-start.8
  25.8 4.9 %qkv.1 = (bf16[512,1024]{1,0:T(8,128)(2,1)S(1)}, f32[512,768]{1,0:T(8,128)S(1)}, bf16[4,1024,128]{2,1,0:T(8,128)(2,1)S(1)}, bf16[512,512]{1,0:T(8,128)(2,1)S(1)}) custom-call(s32[24]{0:T(128)S(1)} %concatenate.34.sc, bf16[2,128,1024]{2,1,0:T(8,128)(2,1)S(1)} %bitcast.51, bf16[2,128,1024]{2,1,0:T(8,128)(2,1)S(1)} %bitcast.53, ...), custom_call_target="tpu_custom_call" | custom-call | flops 100000000 | bytes 1000000 | tf_op jit(solution)/shard_map/qkv/pallas_call | solution.py:167
  30.7 1.1 copy-done.9
  31.8 1.2 collective-permute-start.5
  33.1 3.7 %collective-permute-start.6 = (bf16[512,512]{1,0:T(8,128)(2,1)S(1)}, bf16[512,512]{1,0:T(8,128)(2,1)S(1)}, u32[]{:S(2)}, u32[]{:S(2)}) collective-permute-start(bf16[512,512]{1,0:T(8,128)(2,1)S(1)} %get-tuple-element.71.rest_0_.rest_1_.k.v), channel_id=1, source_target_pairs={{0,4},{2,6},{4,0},{6,2},{8,12},{10,14},{12,8},{14,10},{1,5},{3,7},... | collective-permute-start | bytes 1572872 | tf_op jit(solution)/shard_map/ppermute | solution.py:1034
  36.8 3.5 %attend.2.rest_6_ = f32[4,512,256]{2,1,0:T(8,128)S(1)} custom-call(s32[24]{0:T(128)S(1)} %concatenate.34.sc, bf16[4,1024,128]{2,1,0:T(8,128)(2,1)S(1)} %get-tuple-element.70.qm, bf16[512,512]{1,0:T(8,128)(2,1)S(1)} %get-tuple-element.71.rest_0_.rest_1_.k.v, bf16[512,512]{1,0:T(8,128)(2,1)S(1)} %get-tuple-element.71.rest_0_.rest_1_.k.v), custom_call_target="tpu_custom_call" | custom-call | flops 100000000 | bytes 1000000 | tf_op jit(solution)/shard_map/attend/pallas_call | solution.py:277
  40.5 0.5 collective-permute-start.9
  41.0 2.7 %constant_dynamic-slice_fusion.1 = (bf16[512,2304]{1,0:T(8,128)(2,1)S(1)}, bf16[512,2304]{1,0:T(8,128)(2,1)S(1)}) fusion(bf16[512,9216]{1,0:T(8,128)(2,1)} %wu_own.1, s32[]{:T(128)S(6)} %select_n.96, s32[]{:T(128)S(6)} %select_n.97), kind=kLoop, calls=%fused_computation.19 | loop fusion | bytes 9437192 | tf_op jit(solution)/shard_map/dynamic_slice | solution.py:1054
  43.7 2.8 %pad_maximum_fusion = bf16[512,4608]{1,0:T(8,128)(2,1)} fusion(bf16[512,2304]{1,0:T(8,128)(2,1)S(1)} %get-tuple-element.153, bf16[512,2304]{1,0:T(8,128)(2,1)S(1)} %get-tuple-element.152), kind=kLoop, calls=%fused_computation | loop fusion | flops 9437184 | bytes 9437184 | tf_op jit(solution)/shard_map/concatenate | solution.py:1106
  46.5 1.1 slice-done
  48.1 5.1 %hidden_back.1 = (f32[512,2304]{1,0:T(8,128)S(1)}, bf16[512,1024]{1,0:T(8,128)(2,1)S(1)}, bf16[16,512]{1,0:T(8,128)(2,1)S(1)}) custom-call(s32[24]{0:T(128)S(1)} %concatenate.34.sc, bf16[256,1024]{1,0:T(8,128)(2,1)S(1)} %broadcast_select_fusion.c_mine, bf16[128,1024]{1,0:T(8,128)(2,1)S(1)} %collective-permute-done.9.c_low, ...), custom_call_target="tpu_custom_call" | custom-call | flops 100000000 | bytes 1000000 | tf_op jit(solution)/shard_map/hidden_back/pallas_call | solution.py:372
  53.3 10.3 %collective-permute-done.7.rest_4_.rest_5_.k.v = bf16[512,512]{1,0:T(8,128)(2,1)S(1)} collective-permute-done((bf16[512,512]{1,0:T(8,128)(2,1)S(1)}, bf16[512,512]{1,0:T(8,128)(2,1)S(1)}, u32[]{:S(2)}, u32[]{:S(2)}) %collective-permute-start.7) | collective-permute-done | bytes 524320 | tf_op jit(solution)/shard_map/ppermute | solution.py:1034
  64.0 7.8 %attend.3.acc = f32[4,512,256]{2,1,0:T(8,128)S(1)} custom-call(s32[24]{0:T(128)S(1)} %concatenate.34.sc, bf16[4,1024,128]{2,1,0:T(8,128)(2,1)S(1)} %get-tuple-element.70.qm, bf16[512,512]{1,0:T(8,128)(2,1)S(1)} %collective-permute-done.5.rest_0_.rest_1_.k.v, ...), custom_call_target="tpu_custom_call", output_to_operand_aliasing={{}: (8, {})} | custom-call | flops 100000000 | bytes 1000000 | tf_op jit(solution)/shard_map/attend/pallas_call | solution.py:277
  71.9 2.4 %project.1 = (bf16[512,512]{1,0:T(8,128)(2,1)S(1)}, bf16[512,1024]{1,0:T(8,128)(2,1)S(1)}, f32[4,1,1024]{2,1,0:T(1,128)S(1)}) custom-call(s32[24]{0:T(128)S(1)} %concatenate.34.sc, f32[4,512,256]{2,1,0:T(8,128)S(1)} %attend.3.acc, bf16[512,1024]{1,0:T(8,128)(2,1)S(1)} %copy-done.2, bf16[8,16,1024]{2,1,0:T(8,128)(2,1)S(1)} %bitcast.59, ...), custom_call_target="tpu_custom_call" | custom-call | flops 100000000 | bytes 1000000 | tf_op jit(solution)/shard_map/project/pallas_call | solution.py:329
  74.5 2.5 %collective-permute-done.11.mix_b = bf16[512,1024]{1,0:T(8,128)(2,1)S(1)} collective-permute-done((bf16[512,1024]{1,0:T(8,128)(2,1)S(1)}, bf16[512,1024]{1,0:T(8,128)(2,1)S(1)}, u32[]{:S(2)}, u32[]{:S(2)}) %collective-permute-start.11) | collective-permute-done | bytes 1048608 | tf_op jit(solution)/shard_map/ppermute | solution.py:1031
  77.0 2.2 copy-done.24
  79.2 29.2 %ffn.1 = (f32[256,1024]{1,0:T(8,128)S(1)}, bf16[256,1024]{1,0:T(8,128)(2,1)S(1)}, bf16[512,1024]{1,0:T(8,128)(2,1)S(1)}, bf16[1472,128]{1,0:T(8,128)(2,1)S(1)}) custom-call(s32[24]{0:T(128)S(1)} %concatenate.34.sc, bf16[256,1024]{1,0:T(8,128)(2,1)S(1)} %broadcast_select_fusion.1.mine.x, bf16[256,1024]{1,0:T(8,128)(2,1)S(1)} %collective-permute-done.2.other, ...), custom_call_target="tpu_custom_call" | custom-call | flops 1000000000 | bytes 2500000 | tf_op jit(solution)/shard_map/ffn/pallas_call | solution.py:502
  108.7 2.5 %collective-permute-done.13.du_b = bf16[512,1024]{1,0:T(8,128)(2,1)S(1)} collective-permute-done((bf16[512,1024]{1,0:T(8,128)(2,1)S(1)}, bf16[512,1024]{1,0:T(8,128)(2,1)S(1)}, u32[]{:S(2)}, u32[]{:S(2)}) %collective-permute-start.13) | collective-permute-done | bytes 1048608 | tf_op jit(solution)/shard_map/ppermute | solution.py:1031
  111.2 5.4 %back_mix.1 = (f32[256,1024]{1,0:T(8,128)S(1)}, bf16[4,1024,128]{2,1,0:T(8,128)(2,1)S(1)}, f32[4,1,1024]{2,1,0:T(1,128)S(1)}, bf16[1472,128]{1,0:T(8,128)(2,1)S(1)}) custom-call(s32[24]{0:T(128)S(1)} %concatenate.34.sc, bf16[2,128,1024]{2,1,0:T(8,128)(2,1)S(1)} %bitcast.52, bf16[2,128,1024]{2,1,0:T(8,128)(2,1)S(1)} %bitcast.54, ...), custom_call_target="tpu_custom_call", output_to_operand_aliasing={{3}: (14, {})} | custom-call | flops 100000000 | bytes 1000000 | tf_op jit(solution)/shard_map/back_mix/pallas_call | solution.py:612
  117.1 2.2 collective-permute-start.18
  119.4 6.1 %attend_back.4 = (f32[4,64,1024]{2,1,0:T(8,128)S(1)}, bf16[2,512,256]{2,1,0:T(8,128)(2,1)S(1)}) custom-call(s32[24]{0:T(128)S(1)} %concatenate.34.sc, bf16[4,1024,128]{2,1,0:T(8,128)(2,1)S(1)} %get-tuple-element.70.qm, bf16[4,1024,128]{2,1,0:T(8,128)(2,1)S(1)} %get-tuple-element.86.dom, bf16[512,512]{1,0:T(8,128)(2,1)S(1)} %collective-permute-done.5.rest_0_.rest_1_.k.v, ...), custom_call_target="tpu_custom_call" | custom-call | flops 100000000 | bytes 1000000 | tf_op jit(solution)/shard_map/attend_back/pallas_call | solution.py:713
  125.5 6.3 %attend_back.5 = (f32[4,64,1024]{2,1,0:T(8,128)S(1)}, bf16[2,512,256]{2,1,0:T(8,128)(2,1)S(1)}) custom-call(s32[24]{0:T(128)S(1)} %concatenate.34.sc, bf16[4,1024,128]{2,1,0:T(8,128)(2,1)S(1)} %get-tuple-element.70.qm, bf16[4,1024,128]{2,1,0:T(8,128)(2,1)S(1)} %get-tuple-element.86.dom, ...), custom_call_target="tpu_custom_call", output_to_operand_aliasing={{0}: (7, {})} | custom-call | flops 100000000 | bytes 1000000 | tf_op jit(solution)/shard_map/attend_back/pallas_call | solution.py:713
  132.4 6.1 %attend_back.6 = (f32[4,64,1024]{2,1,0:T(8,128)S(1)}, bf16[2,512,256]{2,1,0:T(8,128)(2,1)S(1)}) custom-call(s32[24]{0:T(128)S(1)} %concatenate.34.sc, bf16[4,1024,128]{2,1,0:T(8,128)(2,1)S(1)} %get-tuple-element.70.qm, bf16[4,1024,128]{2,1,0:T(8,128)(2,1)S(1)} %get-tuple-element.86.dom, ...), custom_call_target="tpu_custom_call", output_to_operand_aliasing={{0}: (7, {})} | custom-call | flops 100000000 | bytes 1000000 | tf_op jit(solution)/shard_map/attend_back/pallas_call | solution.py:713
  138.5 2.2 collective-permute-start.21
  140.8 6.1 %attend_back.7 = (f32[4,64,1024]{2,1,0:T(8,128)S(1)}, f32[2,512,256]{2,1,0:T(8,128)S(1)}) custom-call(s32[24]{0:T(128)S(1)} %concatenate.34.sc, bf16[4,1024,128]{2,1,0:T(8,128)(2,1)S(1)} %get-tuple-element.70.qm, bf16[4,1024,128]{2,1,0:T(8,128)(2,1)S(1)} %get-tuple-element.86.dom, ...), custom_call_target="tpu_custom_call", output_to_operand_aliasing={{0}: (7, {})} | custom-call | flops 100000000 | bytes 1000000 | tf_op jit(solution)/shard_map/attend_back/pallas_call | solution.py:713
  146.9 8.8 %collective-permute-done.34 = bf16[368,128]{1,0:T(8,128)(2,1)S(1)} collective-permute-done((bf16[368,128]{1,0:T(8,128)(2,1)S(1)}, bf16[368,128]{1,0:T(8,128)(2,1)S(1)}, u32[]{:S(2)}, u32[]{:S(2)}) %collective-permute-start.34) | collective-permute-done | bytes 94240 | tf_op jit(solution)/shard_map/ppermute | solution.py:1043
  155.7 1.9 collective-permute-done.21.rest_2_
  157.7 1.1 collective-permute-start.35
  158.7 1.6 collective-permute-start.37
  160.3 6.5 %qkv_back.1 = (f32[256,1024]{1,0:T(8,128)S(1)}, bf16[256,1024]{1,0:T(8,128)(2,1)S(1)}, bf16[512,128]{1,0:T(8,128)(2,1)S(1)}) custom-call(s32[24]{0:T(128)S(1)} %concatenate.34.sc, f32[4,64,1024]{2,1,0:T(8,128)S(1)} %get-tuple-element.95.dq, f32[2,512,256]{2,1,0:T(8,128)S(1)} %get-tuple-element.96.dkv, ...), custom_call_target="tpu_custom_call" | custom-call | flops 100000000 | bytes 1000000 | tf_op jit(solution)/shard_map/qkv_back/pallas_call | solution.py:825
  167.0 1.3 collective-permute-start.38
  168.3 1.1 collective-permute-start.24
  169.4 1.6 collective-permute-start.26
  171.1 1.1 collective-permute-done.25
  172.2 0.9 collective-permute-done.26
  173.1 1.0 collective-permute-start.27
  174.3 2.4 collective-permute-start.29
  176.8 6.5 %collective-permute-done.28 = bf16[128,128]{1,0:T(8,128)(2,1)S(1)} collective-permute-done((bf16[128,128]{1,0:T(8,128)(2,1)S(1)}, bf16[128,128]{1,0:T(8,128)(2,1)S(1)}, u32[]{:S(2)}, u32[]{:S(2)}) %collective-permute-start.28) | collective-permute-done | bytes 32800 | tf_op jit(solution)/shard_map/ppermute | solution.py:1043
  183.5 4.5 %collective-permute-start.39 = (bf16[2,4,2,368,128]{4,3,2,1,0:T(8,128)(2,1)S(1)}, bf16[2,4,2,368,128]{4,3,2,1,0:T(8,128)(2,1)}, u32[]{:S(2)}, u32[]{:S(2)}) collective-permute-start(bf16[2,4,2,368,128]{4,3,2,1,0:T(8,128)(2,1)S(1)} %pad_maximum_fusion.1.own_core), channel_id=1, source_target_pairs={{0,1},{1,0},{2,3},{3,2},{4,5},{5,4},{6,7},{7,6},{8,9},{9,8},{10,11... | collective-permute-start | bytes 4521992 | tf_op jit(solution)/shard_map/ppermute | solution.py:1031
  188.5 1.1 collective-permute-start.30
  189.6 2.0 collective-permute-done.14
  191.5 0.8 collective-permute-start.32
  192.3 1.0 fusion.2
  193.3 3.1 %collective-permute-start.15 = (bf16[256,1024]{1,0:T(8,128)(2,1)}, bf16[256,1024]{1,0:T(8,128)(2,1)}, u32[]{:S(2)}, u32[]{:S(2)}) collective-permute-start(bf16[256,1024]{1,0:T(8,128)(2,1)} %get-tuple-element.150), channel_id=1, source_target_pairs={{1,8},{3,10},{5,12},{7,14},{8,1},{10,3},{12,5},{14,7},{17,24},{19,... | collective-permute-start | bytes 1572872 | tf_op jit(solution)/shard_map/ppermute | solution.py:1028
  196.4 1.3 norm_back.1
  197.7 1.0 copy-done.17
  198.7 3.3 %collective-permute-start.23 = (bf16[256,1024]{1,0:T(8,128)(2,1)}, bf16[256,1024]{1,0:T(8,128)(2,1)}, u32[]{:S(2)}, u32[]{:S(2)}) collective-permute-start(bf16[256,1024]{1,0:T(8,128)(2,1)} %get-tuple-element.106), channel_id=1, source_target_pairs={{1,8},{3,10},{5,12},{7,14},{8,1},{10,3},{12,5},{14,7},{17,24},{19,... | collective-permute-start | bytes 1572872 | tf_op jit(solution)/shard_map/ppermute | solution.py:1028
  202.2 14.0 %collective-permute-done.15.back = bf16[256,1024]{1,0:T(8,128)(2,1)} collective-permute-done((bf16[256,1024]{1,0:T(8,128)(2,1)}, bf16[256,1024]{1,0:T(8,128)(2,1)}, u32[]{:S(2)}, u32[]{:S(2)}) %collective-permute-start.15) | collective-permute-done | bytes 524320 | tf_op jit(solution)/shard_map/ppermute | solution.py:1028
  216.3 2.1 home.2
  218.3 3.5 %collective-permute-done.23.back = bf16[256,1024]{1,0:T(8,128)(2,1)} collective-permute-done((bf16[256,1024]{1,0:T(8,128)(2,1)}, bf16[256,1024]{1,0:T(8,128)(2,1)}, u32[]{:S(2)}, u32[]{:S(2)}) %collective-permute-start.23) | collective-permute-done | bytes 524320 | tf_op jit(solution)/shard_map/ppermute | solution.py:1028
  221.9 2.1 home.3
  223.9 9.8 %place.2 = (f32[8,2,16,4608]{3,2,1,0:T(8,128)}, f32[8,16,4608]{2,1,0:T(8,128)}, f32[8,16,1024]{2,1,0:T(8,128)}, f32[8,32,1024]{2,1,0:T(8,128)}, f32[8,16,1024]{2,1,0:T(8,128)}, /*index=5*/f32[8,16,1024]{2,1,0:T(8,128)}) custom-call(s32[24]{0:T(128)S(1)} %concatenate.34.sc, bf16[2,4,2,368,128]{4,3,2,1,0:T(8,128)(2,1)S(1)} %pad_maximum_fusion.1.own_core, ...), custom_call_target="tpu_custom_call" | custom-call | flops 10000000 | bytes 1000000 | tf_op jit(solution)/shard_map/place/pallas_call | solution.py:962
  233.8 5.8 %place.3 = (f32[8,48,1024]{2,1,0:T(8,128)}, f32[8,16,1024]{2,1,0:T(8,128)}, f32[8,16,512]{2,1,0:T(8,128)}, f32[8,16,512]{2,1,0:T(8,128)}) custom-call(s32[24]{0:T(128)S(1)} %concatenate.34.sc, bf16[1,4,4,128,128]{4,3,2,1,0:T(8,128)(2,1)S(1)} %maximum_bitcast_fusion.own_core, bf16[1,4,4,128,128]{4,3,2,1,0:T(8,128)(2,1)} %collective-permute-done.33.twin), custom_call_target="tpu_custom_call" | custom-call | flops 10000000 | bytes 1000000 | tf_op jit(solution)/shard_map/place/pallas_call | solution.py:962
  (154 shorter events, 7.0 us)
Async XLA Ops:
  0.6 12.4 %copy-start.26 = (bf16[512,2048]{1,0:T(8,128)(2,1)S(1)}, bf16[512,2048]{1,0:T(8,128)(2,1)}, u32[]{:S(2)}) copy-start(bf16[512,2048]{1,0:T(8,128)(2,1)} %param.30) | copy-start | bytes 6291460
  0.7 20.4 %collective-permute-start.1 = (bf16[256,1024]{1,0:T(8,128)(2,1)}, bf16[256,1024]{1,0:T(8,128)(2,1)}, u32[]{:S(2)}, u32[]{:S(2)}) collective-permute-start(bf16[256,1024]{1,0:T(8,128)(2,1)} %bitcast.73), channel_id=1, source_target_pairs={{1,8},{3,10},{5,12},{7,14},{8,1},{10,3},{12,5},{14,7},{17,24},{19,... | collective-permute-start | bytes 1572872 | tf_op jit(solution)/shard_map/ppermute | solution.py:1028
  6.4 12.8 %collective-permute-start = (s32[1,16]{1,0:T(1,128)}, s32[1,16]{1,0:T(1,128)S(1)}, u32[]{:S(2)}, u32[]{:S(2)}) collective-permute-start(s32[1,16]{1,0:T(1,128)} %param.49), channel_id=1, source_target_pairs={{1,8},{3,10},{5,12},{7,14},{8,1},{10,3},{12,5},{14,7},{17,24},{19,... | collective-permute-start | bytes 200 | tf_op jit(solution)/shard_map/ppermute | solution.py:1028
  13.2 6.0 %copy-start.34 = (s32[1,16]{1,0:T(1,128)S(1)}, s32[1,16]{1,0:T(1,128)}, u32[]{:S(2)}) copy-start(s32[1,16]{1,0:T(1,128)} %param.49) | copy-start | bytes 196
  13.3 7.0 %copy-start.32 = (s32[4]{0:T(128)S(1)}, s32[4]{0:T(128)}, u32[]{:S(2)}) copy-start(s32[4]{0:T(128)} %param.48) | copy-start | bytes 52
  13.3 7.7 %copy-start.33 = (f32[32]{0:T(128)S(1)}, f32[32]{0:T(128)}, u32[]{:S(2)}) copy-start(f32[32]{0:T(128)} %constant.92.clone) | copy-start | bytes 388
  13.3 7.8 %copy-start.27 = (bf16[256,1,1024]{2,0,1:T(8,128)(2,1)S(1)}, bf16[256,1,1024]{2,0,1:T(8,128)(2,1)}, u32[]{:S(2)}) copy-start(bf16[256,1,1024]{2,0,1:T(8,128)(2,1)} %param.28) | copy-start | bytes 1572868
  13.6 9.5 %copy-start.28 = (bf16[256,1,1024]{2,0,1:T(8,128)(2,1)S(1)}, bf16[256,1,1024]{2,0,1:T(8,128)(2,1)}, u32[]{:S(2)}) copy-start(bf16[256,1,1024]{2,0,1:T(8,128)(2,1)} %param.29) | copy-start | bytes 1572868
  13.6 11.4 %copy-start.29 = (f32[128,32]{1,0:T(8,128)S(1)}, f32[128,32]{1,0:T(8,128)}, u32[]{:S(2)}) copy-start(f32[128,32]{1,0:T(8,128)} %constant.100) | copy-start | bytes 49156
  13.6 11.4 %copy-start.30 = (f32[128,32]{1,0:T(8,128)S(1)}, f32[128,32]{1,0:T(8,128)}, u32[]{:S(2)}) copy-start(f32[128,32]{1,0:T(8,128)} %constant.99) | copy-start | bytes 49156
  22.3 3.5 %collective-permute-start.2 = (bf16[256,1024]{1,0:T(8,128)(2,1)S(1)}, bf16[256,1024]{1,0:T(8,128)(2,1)S(1)}, u32[]{:S(2)}, u32[]{:S(2)}) collective-permute-start(bf16[256,1024]{1,0:T(8,128)(2,1)S(1)} %broadcast_select_fusion.1.mine.x), channel_id=1, source_target_pairs={{0,1},{1,0},{2,3},{3,2},{4,5},{5,4},{6,7},{7,6},{8,9},{9,8},{10,11... | collective-permute-start | bytes 1572872 | tf_op jit(solution)/shard_map/ppermute | solution.py:1031
  22.4 3.2 %collective-permute-start.3 = (bf16[512,512]{1,0:T(8,128)(2,1)S(1)}, bf16[512,512]{1,0:T(8,128)(2,1)S(1)}, u32[]{:S(2)}, u32[]{:S(2)}) collective-permute-start(bf16[512,512]{1,0:T(8,128)(2,1)S(1)} %get-tuple-element.161), channel_id=1, source_target_pairs={{0,1},{1,0},{2,3},{3,2},{4,5},{5,4},{6,7},{7,6},{8,9},{9,8},{10,11... | collective-permute-start | bytes 1572872 | tf_op jit(solution)/shard_map/ppermute | solution.py:1031
  23.0 2.8 %collective-permute-start.4 = (bf16[512,512]{1,0:T(8,128)(2,1)S(1)}, bf16[512,512]{1,0:T(8,128)(2,1)S(1)}, u32[]{:S(2)}, u32[]{:S(2)}) collective-permute-start(bf16[512,512]{1,0:T(8,128)(2,1)S(1)} %get-tuple-element.160), channel_id=1, source_target_pairs={{0,1},{1,0},{2,3},{3,2},{4,5},{5,4},{6,7},{7,6},{8,9},{9,8},{10,11... | collective-permute-start | bytes 1572872 | tf_op jit(solution)/shard_map/ppermute | solution.py:1031
  23.1 17.2 %collective-permute-start.8 = (bf16[256,1024]{1,0:T(8,128)(2,1)S(1)}, bf16[256,1024]{1,0:T(8,128)(2,1)S(1)}, u32[]{:S(2)}, u32[]{:S(2)}) collective-permute-start(bf16[256,1024]{1,0:T(8,128)(2,1)S(1)} %bitcast.74), channel_id=1, source_target_pairs={{1,8},{3,10},{5,12},{7,14},{8,1},{10,3},{12,5},{14,7},{17,24},{19,... | collective-permute-start | bytes 1572872 | tf_op jit(solution)/shard_map/ppermute | solution.py:1028
  25.6 5.1 %copy-start.5 = (bf16[512,512]{1,0:T(8,128)(2,1)}, bf16[512,512]{1,0:T(8,128)(2,1)S(1)}, u32[]{:S(2)}) copy-start(bf16[512,512]{1,0:T(8,128)(2,1)S(1)} %collective-permute-done.3.w_rec_q.rest_10_) | copy-start | bytes 1572868
  25.8 4.9 %copy-start.7 = (bf16[512,512]{1,0:T(8,128)(2,1)}, bf16[512,512]{1,0:T(8,128)(2,1)S(1)}, u32[]{:S(2)}) copy-start(bf16[512,512]{1,0:T(8,128)(2,1)S(1)} %collective-permute-done.4.w_rec_kv.rest_11_) | copy-start | bytes 1572868
  31.8 8.4 %copy-start.13 = (bf16[512,1024]{1,0:T(8,128)(2,1)}, bf16[512,1024]{1,0:T(8,128)(2,1)S(1)}, u32[]{:S(2)}) copy-start(bf16[512,1024]{1,0:T(8,128)(2,1)S(1)} %get-tuple-element.101.rest_8_) | copy-start | bytes 3145732
  31.8 21.4 %collective-permute-start.5 = (bf16[512,512]{1,0:T(8,128)(2,1)S(1)}, bf16[512,512]{1,0:T(8,128)(2,1)S(1)}, u32[]{:S(2)}, u32[]{:S(2)}) collective-permute-start(bf16[512,512]{1,0:T(8,128)(2,1)S(1)} %get-tuple-element.71.rest_0_.rest_1_.k.v), channel_id=1, source_target_pairs={{0,2},{2,0},{4,6},{6,4},{8,10},{10,8},{12,14},{14,12},{1,3},{3,1},... | collective-permute-start | bytes 1572872 | tf_op jit(solution)/shard_map/ppermute | solution.py:1034
  33.1 20.2 %collective-permute-start.6 = (bf16[512,512]{1,0:T(8,128)(2,1)S(1)}, bf16[512,512]{1,0:T(8,128)(2,1)S(1)}, u32[]{:S(2)}, u32[]{:S(2)}) collective-permute-start(bf16[512,512]{1,0:T(8,128)(2,1)S(1)} %get-tuple-element.71.rest_0_.rest_1_.k.v), channel_id=1, source_target_pairs={{0,4},{2,6},{4,0},{6,2},{8,12},{10,14},{12,8},{14,10},{1,5},{3,7},... | collective-permute-start | bytes 1572872 | tf_op jit(solution)/shard_map/ppermute | solution.py:1034
  36.8 26.7 %collective-permute-start.7 = (bf16[512,512]{1,0:T(8,128)(2,1)S(1)}, bf16[512,512]{1,0:T(8,128)(2,1)S(1)}, u32[]{:S(2)}, u32[]{:S(2)}) collective-permute-start(bf16[512,512]{1,0:T(8,128)(2,1)S(1)} %get-tuple-element.71.rest_0_.rest_1_.k.v), channel_id=1, source_target_pairs={{0,6},{2,4},{4,2},{6,0},{8,14},{10,12},{12,10},{14,8},{1,7},{3,5},... | collective-permute-start | bytes 1572872 | tf_op jit(solution)/shard_map/ppermute | solution.py:1034
  40.4 6.1 %collective-permute-start.10 = (bf16[128,1024]{1,0:T(8,128)(2,1)S(1)}, bf16[128,1024]{1,0:T(8,128)(2,1)S(1)}, u32[]{:S(2)}, u32[]{:S(2)}) collective-permute-start(bf16[128,1024]{1,0:T(8,128)(2,1)S(1)} %get-tuple-element.162), channel_id=1, source_target_pairs={{0,1},{1,0},{2,3},{3,2},{4,5},{5,4},{6,7},{7,6},{8,9},{9,8},{10,11... | collective-permute-start | bytes 786440 | tf_op jit(solution)/shard_map/ppermute | solution.py:1031
  40.5 6.0 %collective-permute-start.9 = (bf16[128,1024]{1,0:T(8,128)(2,1)S(1)}, bf16[128,1024]{1,0:T(8,128)(2,1)S(1)}, u32[]{:S(2)}, u32[]{:S(2)}) collective-permute-start(bf16[128,1024]{1,0:T(8,128)(2,1)S(1)} %get-tuple-element.163), channel_id=1, source_target_pairs={{0,1},{1,0},{2,3},{3,2},{4,5},{5,4},{6,7},{7,6},{8,9},{9,8},{10,11... | collective-permute-start | bytes 786440 | tf_op jit(solution)/shard_map/ppermute | solution.py:1031
  48.1 15.4 %copy-start.25 = (bf16[512,4608]{1,0:T(8,128)(2,1)S(1)}, bf16[512,4608]{1,0:T(8,128)(2,1)}, u32[]{:S(2)}) copy-start(bf16[512,4608]{1,0:T(8,128)(2,1)} %pad_maximum_fusion) | copy-start | bytes 14155780
  53.2 18.6 %copy-start = (f32[512,2304]{1,0:T(8,128)}, f32[512,2304]{1,0:T(8,128)S(1)}, u32[]{:S(2)}) copy-start(f32[512,2304]{1,0:T(8,128)S(1)} %get-tuple-element.74.dh_tile) | copy-start | bytes 14155780
  63.5 8.3 %copy-start.2 = (bf16[512,1024]{1,0:T(8,128)(2,1)S(1)}, bf16[512,1024]{1,0:T(8,128)(2,1)}, u32[]{:S(2)}) copy-start(bf16[512,1024]{1,0:T(8,128)(2,1)} %w_o.3) | copy-start | bytes 3145732
  63.5 8.3 %copy-start.19 = (bf16[8,1024,16]{1,2,0:T(8,128)(2,1)S(1)}, bf16[8,1024,16]{1,2,0:T(8,128)(2,1)}, u32[]{:S(2)}) copy-start(bf16[8,1024,16]{1,2,0:T(8,128)(2,1)} %param.42) | copy-start | bytes 786436
  63.5 8.4 %copy-start.20 = (bf16[8,16,1024]{2,1,0:T(8,128)(2,1)S(1)}, bf16[8,16,1024]{2,1,0:T(8,128)(2,1)}, u32[]{:S(2)}) copy-start(bf16[8,16,1024]{2,1,0:T(8,128)(2,1)} %b_o.3) | copy-start | bytes 786436
  63.5 13.5 %collective-permute-start.12 = (bf16[512,4608]{1,0:T(8,128)(2,1)S(1)}, bf16[512,4608]{1,0:T(8,128)(2,1)S(1)}, u32[]{:S(2)}, u32[]{:S(2)}) collective-permute-start(bf16[512,4608]{1,0:T(8,128)(2,1)S(1)} %copy-done.25), channel_id=1, source_target_pairs={{0,1},{1,0},{2,3},{3,2},{4,5},{5,4},{6,7},{7,6},{8,9},{9,8},{10,11... | collective-permute-start | bytes 14155784 | tf_op jit(solution)/shard_map/ppermute | solution.py:1031
  71.8 7.4 %copy-start.4 = (bf16[8,2,16,4608]{3,2,1,0:T(8,128)(2,1)S(1)}, bf16[8,2,16,4608]{3,2,1,0:T(8,128)(2,1)}, u32[]{:S(2)}) copy-start(bf16[8,2,16,4608]{3,2,1,0:T(8,128)(2,1)} %b_gu.1) | copy-start | bytes 7077892
  71.8 7.4 %copy-start.21 = (bf16[8,1024,32]{1,2,0:T(8,128)(2,1)S(1)}, bf16[8,1024,32]{1,2,0:T(8,128)(2,1)}, u32[]{:S(2)}) copy-start(bf16[8,1024,32]{1,2,0:T(8,128)(2,1)} %param.44) | copy-start | bytes 1572868
  74.3 2.7 %collective-permute-start.11 = (bf16[512,1024]{1,0:T(8,128)(2,1)S(1)}, bf16[512,1024]{1,0:T(8,128)(2,1)S(1)}, u32[]{:S(2)}, u32[]{:S(2)}) collective-permute-start(bf16[512,1024]{1,0:T(8,128)(2,1)S(1)} %get-tuple-element.77.mix_a), channel_id=1, source_target_pairs={{0,1},{1,0},{2,3},{3,2},{4,5},{5,4},{6,7},{7,6},{8,9},{9,8},{10,11... | collective-permute-start | bytes 3145736 | tf_op jit(solution)/shard_map/ppermute | solution.py:1031
  108.5 2.7 %collective-permute-start.13 = (bf16[512,1024]{1,0:T(8,128)(2,1)S(1)}, bf16[512,1024]{1,0:T(8,128)(2,1)S(1)}, u32[]{:S(2)}, u32[]{:S(2)}) collective-permute-start(bf16[512,1024]{1,0:T(8,128)(2,1)S(1)} %get-tuple-element.83.du_a), channel_id=1, source_target_pairs={{0,1},{1,0},{2,3},{3,2},{4,5},{5,4},{6,7},{7,6},{8,9},{9,8},{10,11... | collective-permute-start | bytes 3145736 | tf_op jit(solution)/shard_map/ppermute | solution.py:1031
  116.7 15.7 %collective-permute-start.16 = (bf16[368,128]{1,0:T(8,128)(2,1)S(1)}, bf16[368,128]{1,0:T(8,128)(2,1)S(1)}, u32[]{:S(2)}, u32[]{:S(2)}) collective-permute-start(bf16[368,128]{1,0:T(8,128)(2,1)S(1)} %get-tuple-element.164), channel_id=1, source_target_pairs={{0,2},{2,0},{4,6},{6,4},{8,10},{10,8},{12,14},{14,12},{1,3},{3,1},... | collective-permute-start | bytes 282632 | tf_op jit(solution)/shard_map/ppermute | solution.py:1034
  117.1 15.2 %collective-permute-start.17 = (bf16[368,128]{1,0:T(8,128)(2,1)S(1)}, bf16[368,128]{1,0:T(8,128)(2,1)S(1)}, u32[]{:S(2)}, u32[]{:S(2)}) collective-permute-start(bf16[368,128]{1,0:T(8,128)(2,1)S(1)} %get-tuple-element.166), channel_id=1, source_target_pairs={{0,4},{2,6},{4,0},{6,2},{8,12},{10,14},{12,8},{14,10},{1,5},{3,7},... | collective-permute-start | bytes 282632 | tf_op jit(solution)/shard_map/ppermute | solution.py:1034
  117.1 15.2 %collective-permute-start.18 = (bf16[368,128]{1,0:T(8,128)(2,1)S(1)}, bf16[368,128]{1,0:T(8,128)(2,1)S(1)}, u32[]{:S(2)}, u32[]{:S(2)}) collective-permute-start(bf16[368,128]{1,0:T(8,128)(2,1)S(1)} %get-tuple-element.165), channel_id=1, source_target_pairs={{0,6},{2,4},{4,2},{6,0},{8,14},{10,12},{12,10},{14,8},{1,7},{3,5},... | collective-permute-start | bytes 282632 | tf_op jit(solution)/shard_map/ppermute | solution.py:1034
  131.8 23.9 %collective-permute-start.20 = (bf16[2,512,256]{2,1,0:T(8,128)(2,1)S(1)}, bf16[2,512,256]{2,1,0:T(8,128)(2,1)S(1)}, u32[]{:S(2)}, u32[]{:S(2)}) collective-permute-start(bf16[2,512,256]{2,1,0:T(8,128)(2,1)S(1)} %get-tuple-element.98), channel_id=1, source_target_pairs={{0,4},{2,6},{4,0},{6,2},{8,12},{10,14},{12,8},{14,10},{1,5},{3,7},... | collective-permute-start | bytes 1572872 | tf_op jit(solution)/shard_map/ppermute | solution.py:1034
  131.9 23.9 %collective-permute-start.19 = (bf16[2,512,256]{2,1,0:T(8,128)(2,1)S(1)}, bf16[2,512,256]{2,1,0:T(8,128)(2,1)S(1)}, u32[]{:S(2)}, u32[]{:S(2)}) collective-permute-start(bf16[2,512,256]{2,1,0:T(8,128)(2,1)S(1)} %get-tuple-element.97), channel_id=1, source_target_pairs={{0,2},{2,0},{4,6},{6,4},{8,10},{10,8},{12,14},{14,12},{1,3},{3,1},... | collective-permute-start | bytes 1572872 | tf_op jit(solution)/shard_map/ppermute | solution.py:1034
  138.5 19.1 %collective-permute-start.21 = (bf16[2,512,256]{2,1,0:T(8,128)(2,1)S(1)}, bf16[2,512,256]{2,1,0:T(8,128)(2,1)S(1)}, u32[]{:S(2)}, u32[]{:S(2)}) collective-permute-start(bf16[2,512,256]{2,1,0:T(8,128)(2,1)S(1)} %get-tuple-element.99), channel_id=1, source_target_pairs={{0,6},{2,4},{4,2},{6,0},{8,14},{10,12},{12,10},{14,8},{1,7},{3,5},... | collective-permute-start | bytes 1572872 | tf_op jit(solution)/shard_map/ppermute | solution.py:1034
  140.8 14.9 %collective-permute-start.34 = (bf16[368,128]{1,0:T(8,128)(2,1)S(1)}, bf16[368,128]{1,0:T(8,128)(2,1)S(1)}, u32[]{:S(2)}, u32[]{:S(2)}) collective-permute-start(bf16[368,128]{1,0:T(8,128)(2,1)S(1)} %add_convert_fusion), channel_id=1, source_target_pairs={{0,8},{2,10},{4,12},{6,14},{8,0},{10,2},{12,4},{14,6},{16,24},{18,... | collective-permute-start | bytes 282632 | tf_op jit(solution)/shard_map/ppermute | solution.py:1043
  140.8 19.5 %copy-start.6 = (bf16[512,512]{1,0:T(8,128)(2,1)S(1)}, bf16[512,512]{1,0:T(8,128)(2,1)}, u32[]{:S(2)}) copy-start(bf16[512,512]{1,0:T(8,128)(2,1)} %copy-done.5) | copy-start | bytes 1572868
  140.8 19.5 %copy-start.8 = (bf16[512,512]{1,0:T(8,128)(2,1)S(1)}, bf16[512,512]{1,0:T(8,128)(2,1)}, u32[]{:S(2)}) copy-start(bf16[512,512]{1,0:T(8,128)(2,1)} %copy-done.7) | copy-start | bytes 1572868
  140.8 19.5 %copy-start.10 = (f32[512,768]{1,0:T(8,128)S(1)}, f32[512,768]{1,0:T(8,128)}, u32[]{:S(2)}) copy-start(f32[512,768]{1,0:T(8,128)} %copy-done.9) | copy-start | bytes 4718596
  140.8 19.5 %copy-start.14 = (bf16[512,1024]{1,0:T(8,128)(2,1)S(1)}, bf16[512,1024]{1,0:T(8,128)(2,1)}, u32[]{:S(2)}) copy-start(bf16[512,1024]{1,0:T(8,128)(2,1)} %copy-done.13) | copy-start | bytes 3145732
  140.8 19.5 %copy-start.16 = (bf16[8,16,1024]{2,1,0:T(8,128)(2,1)S(1)}, bf16[8,16,1024]{2,1,0:T(8,128)(2,1)}, u32[]{:S(2)}) copy-start(bf16[8,16,1024]{2,1,0:T(8,128)(2,1)} %rest_13_.1) | copy-start | bytes 786436
  157.7 9.2 %collective-permute-start.35 = (bf16[2,368,128]{2,1,0:T(8,128)(2,1)S(1)}, bf16[2,368,128]{2,1,0:T(8,128)(2,1)S(1)}, u32[]{:S(2)}, u32[]{:S(2)}) collective-permute-start(bf16[2,368,128]{2,1,0:T(8,128)(2,1)S(1)} %pad_maximum_fusion.7), channel_id=1, source_target_pairs={{0,2},{2,0},{4,6},{6,4},{8,10},{10,8},{12,14},{14,12},{1,3},{3,1},... | collective-permute-start | bytes 565256 | tf_op jit(solution)/shard_map/ppermute | solution.py:1034
  158.7 8.2 %collective-permute-start.36 = (bf16[2,368,128]{2,1,0:T(8,128)(2,1)S(1)}, bf16[2,368,128]{2,1,0:T(8,128)(2,1)S(1)}, u32[]{:S(2)}, u32[]{:S(2)}) collective-permute-start(bf16[2,368,128]{2,1,0:T(8,128)(2,1)S(1)} %pad_maximum_fusion.7), channel_id=1, source_target_pairs={{0,4},{2,6},{4,0},{6,2},{8,12},{10,14},{12,8},{14,10},{1,5},{3,7},... | collective-permute-start | bytes 565256 | tf_op jit(solution)/shard_map/ppermute | solution.py:1034
  158.7 8.2 %collective-permute-start.37 = (bf16[2,368,128]{2,1,0:T(8,128)(2,1)S(1)}, bf16[2,368,128]{2,1,0:T(8,128)(2,1)S(1)}, u32[]{:S(2)}, u32[]{:S(2)}) collective-permute-start(bf16[2,368,128]{2,1,0:T(8,128)(2,1)S(1)} %pad_maximum_fusion.7), channel_id=1, source_target_pairs={{0,6},{2,4},{4,2},{6,0},{8,14},{10,12},{12,10},{14,8},{1,7},{3,5},... | collective-permute-start | bytes 565256 | tf_op jit(solution)/shard_map/ppermute | solution.py:1034
  167.0 16.4 %collective-permute-start.38 = (bf16[4,2,368,128]{3,2,1,0:T(8,128)(2,1)S(1)}, bf16[4,2,368,128]{3,2,1,0:T(8,128)(2,1)S(1)}, u32[]{:S(2)}, u32[]{:S(2)}) collective-permute-start(bf16[4,2,368,128]{3,2,1,0:T(8,128)(2,1)S(1)} %pad_maximum_fusion.4), channel_id=1, source_target_pairs={{0,16},{2,18},{4,20},{6,22},{8,24},{10,26},{12,28},{14,30},{16,0},... | collective-permute-start | bytes 2261000 | tf_op jit(solution)/shard_map/ppermute | solution.py:1043
  168.3 2.8 %collective-permute-start.24 = (bf16[128,128]{1,0:T(8,128)(2,1)S(1)}, bf16[128,128]{1,0:T(8,128)(2,1)S(1)}, u32[]{:S(2)}, u32[]{:S(2)}) collective-permute-start(bf16[128,128]{1,0:T(8,128)(2,1)S(1)} %get-tuple-element.171), channel_id=1, source_target_pairs={{0,2},{2,0},{4,6},{6,4},{8,10},{10,8},{12,14},{14,12},{1,3},{3,1},... | collective-permute-start | bytes 98312 | tf_op jit(solution)/shard_map/ppermute | solution.py:1034
  169.4 2.8 %collective-permute-start.25 = (bf16[128,128]{1,0:T(8,128)(2,1)S(1)}, bf16[128,128]{1,0:T(8,128)(2,1)S(1)}, u32[]{:S(2)}, u32[]{:S(2)}) collective-permute-start(bf16[128,128]{1,0:T(8,128)(2,1)S(1)} %get-tuple-element.173), channel_id=1, source_target_pairs={{0,4},{2,6},{4,0},{6,2},{8,12},{10,14},{12,8},{14,10},{1,5},{3,7},... | collective-permute-start | bytes 98312 | tf_op jit(solution)/shard_map/ppermute | solution.py:1034
  169.4 3.7 %collective-permute-start.26 = (bf16[128,128]{1,0:T(8,128)(2,1)S(1)}, bf16[128,128]{1,0:T(8,128)(2,1)S(1)}, u32[]{:S(2)}, u32[]{:S(2)}) collective-permute-start(bf16[128,128]{1,0:T(8,128)(2,1)S(1)} %get-tuple-element.172), channel_id=1, source_target_pairs={{0,6},{2,4},{4,2},{6,0},{8,14},{10,12},{12,10},{14,8},{1,7},{3,5},... | collective-permute-start | bytes 98312 | tf_op jit(solution)/shard_map/ppermute | solution.py:1034
  173.1 3.8 %collective-permute-start.27 = (bf16[128,128]{1,0:T(8,128)(2,1)S(1)}, bf16[128,128]{1,0:T(8,128)(2,1)S(1)}, u32[]{:S(2)}, u32[]{:S(2)}) collective-permute-start(bf16[128,128]{1,0:T(8,128)(2,1)S(1)} %add_convert_fusion.1), channel_id=1, source_target_pairs={{0,8},{2,10},{4,12},{6,14},{8,0},{10,2},{12,4},{14,6},{16,24},{18,... | collective-permute-start | bytes 98312 | tf_op jit(solution)/shard_map/ppermute | solution.py:1043
  174.1 9.3 %collective-permute-start.28 = (bf16[128,128]{1,0:T(8,128)(2,1)S(1)}, bf16[128,128]{1,0:T(8,128)(2,1)S(1)}, u32[]{:S(2)}, u32[]{:S(2)}) collective-permute-start(bf16[128,128]{1,0:T(8,128)(2,1)S(1)} %add_convert_fusion.1), channel_id=1, source_target_pairs={{0,16},{2,18},{4,20},{6,22},{8,24},{10,26},{12,28},{14,30},{16,0},... | collective-permute-start | bytes 98312 | tf_op jit(solution)/shard_map/ppermute | solution.py:1043
  174.3 9.0 %collective-permute-start.29 = (bf16[128,128]{1,0:T(8,128)(2,1)S(1)}, bf16[128,128]{1,0:T(8,128)(2,1)S(1)}, u32[]{:S(2)}, u32[]{:S(2)}) collective-permute-start(bf16[128,128]{1,0:T(8,128)(2,1)S(1)} %add_convert_fusion.1), channel_id=1, source_target_pairs={{0,24},{2,26},{4,28},{6,30},{8,16},{10,18},{12,20},{14,22},{16,8},... | collective-permute-start | bytes 98312 | tf_op jit(solution)/shard_map/ppermute | solution.py:1043
  183.5 40.4 %collective-permute-start.39 = (bf16[2,4,2,368,128]{4,3,2,1,0:T(8,128)(2,1)S(1)}, bf16[2,4,2,368,128]{4,3,2,1,0:T(8,128)(2,1)}, u32[]{:S(2)}, u32[]{:S(2)}) collective-permute-start(bf16[2,4,2,368,128]{4,3,2,1,0:T(8,128)(2,1)S(1)} %pad_maximum_fusion.1.own_core), channel_id=1, source_target_pairs={{0,1},{1,0},{2,3},{3,2},{4,5},{5,4},{6,7},{7,6},{8,9},{9,8},{10,11... | collective-permute-start | bytes 4521992 | tf_op jit(solution)/shard_map/ppermute | solution.py:1031
  188.0 3.6 %collective-permute-start.14 = (bf16[256,1024]{1,0:T(8,128)(2,1)S(1)}, bf16[256,1024]{1,0:T(8,128)(2,1)S(1)}, u32[]{:S(2)}, u32[]{:S(2)}) collective-permute-start(bf16[256,1024]{1,0:T(8,128)(2,1)S(1)} %get-tuple-element.87), channel_id=1, source_target_pairs={{0,1},{1,0},{2,3},{3,2},{4,5},{5,4},{6,7},{7,6},{8,9},{9,8},{10,11... | collective-permute-start | bytes 1572872 | tf_op jit(solution)/shard_map/ppermute | solution.py:1031
  188.1 5.3 %collective-permute-start.22 = (bf16[256,1024]{1,0:T(8,128)(2,1)S(1)}, bf16[256,1024]{1,0:T(8,128)(2,1)S(1)}, u32[]{:S(2)}, u32[]{:S(2)}) collective-permute-start(bf16[256,1024]{1,0:T(8,128)(2,1)S(1)} %get-tuple-element.103), channel_id=1, source_target_pairs={{0,1},{1,0},{2,3},{3,2},{4,5},{5,4},{6,7},{7,6},{8,9},{9,8},{10,11... | collective-permute-start | bytes 1572872 | tf_op jit(solution)/shard_map/ppermute | solution.py:1031
  188.5 10.2 %collective-permute-start.30 = (bf16[4,128,128]{2,1,0:T(8,128)(2,1)S(1)}, bf16[4,128,128]{2,1,0:T(8,128)(2,1)S(1)}, u32[]{:S(2)}, u32[]{:S(2)}) collective-permute-start(bf16[4,128,128]{2,1,0:T(8,128)(2,1)S(1)} %get-tuple-element.170), channel_id=1, source_target_pairs={{0,2},{2,0},{4,6},{6,4},{8,10},{10,8},{12,14},{14,12},{1,3},{3,1},... | collective-permute-start | bytes 393224 | tf_op jit(solution)/shard_map/ppermute | solution.py:1034
  189.6 12.5 %collective-permute-start.31 = (bf16[4,128,128]{2,1,0:T(8,128)(2,1)S(1)}, bf16[4,128,128]{2,1,0:T(8,128)(2,1)S(1)}, u32[]{:S(2)}, u32[]{:S(2)}) collective-permute-start(bf16[4,128,128]{2,1,0:T(8,128)(2,1)S(1)} %get-tuple-element.170), channel_id=1, source_target_pairs={{0,4},{2,6},{4,0},{6,2},{8,12},{10,14},{12,8},{14,10},{1,5},{3,7},... | collective-permute-start | bytes 393224 | tf_op jit(solution)/shard_map/ppermute | solution.py:1034
  191.5 10.5 %collective-permute-start.32 = (bf16[4,128,128]{2,1,0:T(8,128)(2,1)S(1)}, bf16[4,128,128]{2,1,0:T(8,128)(2,1)S(1)}, u32[]{:S(2)}, u32[]{:S(2)}) collective-permute-start(bf16[4,128,128]{2,1,0:T(8,128)(2,1)S(1)} %get-tuple-element.170), channel_id=1, source_target_pairs={{0,6},{2,4},{4,2},{6,0},{8,14},{10,12},{12,10},{14,8},{1,7},{3,5},... | collective-permute-start | bytes 393224 | tf_op jit(solution)/shard_map/ppermute | solution.py:1034
  193.3 22.9 %collective-permute-start.15 = (bf16[256,1024]{1,0:T(8,128)(2,1)}, bf16[256,1024]{1,0:T(8,128)(2,1)}, u32[]{:S(2)}, u32[]{:S(2)}) collective-permute-start(bf16[256,1024]{1,0:T(8,128)(2,1)} %get-tuple-element.150), channel_id=1, source_target_pairs={{1,8},{3,10},{5,12},{7,14},{8,1},{10,3},{12,5},{14,7},{17,24},{19,... | collective-permute-start | bytes 1572872 | tf_op jit(solution)/shard_map/ppermute | solution.py:1028
  198.7 23.2 %collective-permute-start.23 = (bf16[256,1024]{1,0:T(8,128)(2,1)}, bf16[256,1024]{1,0:T(8,128)(2,1)}, u32[]{:S(2)}, u32[]{:S(2)}) collective-permute-start(bf16[256,1024]{1,0:T(8,128)(2,1)} %get-tuple-element.106), channel_id=1, source_target_pairs={{1,8},{3,10},{5,12},{7,14},{8,1},{10,3},{12,5},{14,7},{17,24},{19,... | collective-permute-start | bytes 1572872 | tf_op jit(solution)/shard_map/ppermute | solution.py:1028
  202.1 31.6 %collective-permute-start.33 = (bf16[1,4,4,128,128]{4,3,2,1,0:T(8,128)(2,1)S(1)}, bf16[1,4,4,128,128]{4,3,2,1,0:T(8,128)(2,1)}, u32[]{:S(2)}, u32[]{:S(2)}) collective-permute-start(bf16[1,4,4,128,128]{4,3,2,1,0:T(8,128)(2,1)S(1)} %maximum_bitcast_fusion.own_core), channel_id=1, source_target_pairs={{0,1},{1,0},{2,3},{3,2},{4,5},{5,4},{6,7},{7,6},{8,9},{9,8},{10,11... | collective-permute-start | bytes 1572872 | tf_op jit(solution)/shard_map/ppermute | solution.py:1031
  202.2 19.7 %copy-start.18 = (f32[256,1024]{1,0:T(8,128)S(1)}, f32[256,1024]{1,0:T(8,128)}, u32[]{:S(2)}) copy-start(f32[256,1024]{1,0:T(8,128)} %copy-done.17) | copy-start | bytes 3145732
  (13 other events, 41.3 us)

commit v3 on v2

--- a/solution.py
+++ b/solution.py
@@ -431,14 +431,18 @@
         pay[...] = jnp.zeros_like(pay)
 
     u_own, u_rec = u_s[:, own], u_s[:, rec]
-    gate = mm(u_own, wg_own[...]) + mm(u_rec, wg_rec[...]) + mm(rgu_s[:, :R], b_gu[0, 0])
-    up = mm(u_own, wu_own[...]) + mm(u_rec, wu_rec[...]) + mm(rgu_s[:, R:], b_gu[0, 1])
-    d_hid = dh_tile[...]
-    sig = jax.nn.sigmoid(gate)
-    silu = gate * sig
-    hid = (silu * up).astype(bf16)
-    e_g = (d_hid * up * (sig * (1.0 + gate * (1.0 - sig)))).astype(bf16)
-    e_u = (d_hid * silu).astype(bf16)
+    hids, egs, eus = [], [], []
+    for n in range(TF // 256):
+        at = slice(n * 256, (n + 1) * 256)
+        gate = mm(u_own, wg_own[:, at]) + mm(u_rec, wg_rec[:, at]) + mm(rgu_s[:, :R], b_gu[0, 0, :, at])
+        up = mm(u_own, wu_own[:, at]) + mm(u_rec, wu_rec[:, at]) + mm(rgu_s[:, R:], b_gu[0, 1, :, at])
+        d_hid = dh_tile[:, at]
+        sig = 0.5 + 0.5 * jnp.tanh(0.5 * gate)
+        silu = gate * sig
+        hids.append((silu * up).astype(bf16))
+        egs.append((d_hid * up * (sig + (silu - silu * sig))).astype(bf16))
+        eus.append((d_hid * silu).astype(bf16))
+    hid, e_g, e_u = [jnp.concatenate(v, axis=1) for v in (hids, egs, eus)]
     down = mm(hid, w_d[...])
     du_own = mm_nt(e_g, wg_own[...]) + mm_nt(e_u, wu_own[...])
     du_rec = mm_nt(e_g, wg_rec[...]) + mm_nt(e_u, wu_rec[...])
@@ -886,14 +890,15 @@
     )(x, du, got, dh, gain)
 
 
-def home_kernel(stays, own, back, out):
-    v = jnp.where(stays[0] == 1, own[...], back[...].astype(f32))
+def home_kernel(stays, own, low, high, out):
+    back = jnp.where(pl.program_id(0) == 0, low[...], high[...]).astype(f32)
+    v = jnp.where(stays[0] == 1, own[...], back)
     n = v.shape[1] // 128
     for t in range(n):
         out[pl.ds(t, v.shape[0], stride=n), :] = v[:, t * 128 : (t + 1) * 128]
 
 
-def home_call(stays, own, back):
+def home_call(stays, own, low, high):
     rows, width = own.shape
     n = width // 128
     spec = pl.BlockSpec((rows // 2, width), lambda i, s: (i, 0))
@@ -902,24 +907,25 @@
         grid_spec=pltpu.PrefetchScalarGridSpec(
             num_scalar_prefetch=1,
             grid=(2,),
-            in_specs=[spec, spec],
+            in_specs=[spec, whole(low.shape), whole(high.shape)],
             out_specs=pl.BlockSpec((rows // 2 * n, 128), lambda i, s: (i, 0)),
         ),
         out_shape=jax.ShapeDtypeStruct((rows * n, 128), f32),
         compiler_params=params(8),
         cost_estimate=cost(1e7, 1e6),
         name="home",
-    )(stays, own, back)
+    )(stays, own, low, high)
     return out.reshape(rows, 1, width)
 
 
 def place_kernel(pieces, half, n_seq, per_shard, sc, own_core, twin, *rest):
     outs, box, sem = rest[:-2], rest[-2], rest[-1]
     core, place, own = sc[0], sc[2], sc[3]
-    which = pl.program_id(0)
+    step = pl.program_id(0)
     parts, _, group = own_core.shape[:3]
-
-    @pl.when(which == 0)
+    count = outs[0].shape[0]
+
+    @pl.when(step == 0)
     def _():
         copies = []
         for c, source in enumerate((own_core, twin)):
@@ -928,7 +934,7 @@
                     copies.append(
                         pltpu.make_async_copy(
                             source.at[part, k],
-                            box.at[core ^ c, place ^ k, pl.ds(part * group, group)],
+                            box.at[pl.ds(part * group, group), core ^ c, place ^ k],
                             sem.at[(c * parts + part) * half + k],
                         )
                     )
@@ -941,33 +947,36 @@
         out[...] = jnp.zeros_like(out)
     for b in range(2 * n_seq):
         rel = own ^ b
-
-        @pl.when(sc[4 + b] == which)
+        slot = sc[4 + b] - step * count
+
+        @pl.when((slot >= 0) & (slot < count))
         def _():
+            held = box.at[rel]
+            into = [out.at[slot] for out in outs]
             for c in range(2):
                 for index, target, lead, lane, shift in pieces:
                     at = lane + c * shift
                     rows = slice((index % per_shard) * R, (index % per_shard + 1) * R)
-                    value = box[c, index // per_shard, rel, rows, :].astype(f32)
-                    outs[target][(0,) + lead + (slice(at, at + 128),)] += value
-
-
-def place_call(pieces, shapes, n_seq, sc, own_core, twin):
+                    value = held[c, index // per_shard, rows, :].astype(f32)
+                    into[target][lead + (slice(at, at + 128),)] += value
+
+
+def place_call(steps, pieces, shapes, n_seq, sc, own_core, twin):
     parts, half, _, rows, _ = own_core.shape
 
     def out_spec(shape):
         zeros = (0,) * len(shape)
-        return pl.BlockSpec((1,) + shape, lambda i, s: (i,) + zeros)
+        return pl.BlockSpec((ADAPTER_SETS // steps,) + shape, lambda i, s: (i,) + zeros)
 
     return pl.pallas_call(
         functools.partial(place_kernel, pieces, half, n_seq, rows // R),
         grid_spec=pltpu.PrefetchScalarGridSpec(
             num_scalar_prefetch=1,
-            grid=(ADAPTER_SETS,),
+            grid=(steps,),
             in_specs=[pl.BlockSpec(memory_space=pl.ANY)] * 2,
             out_specs=[out_spec(shape) for shape in shapes],
             scratch_shapes=[
-                pltpu.VMEM((2, half, 2 * n_seq, rows, 128), bf16),
+                pltpu.VMEM((2 * n_seq, 2, half, rows, 128), bf16),
                 pltpu.SemaphoreType.DMA((2 * parts * half,)),
             ],
         ),
@@ -1128,6 +1137,8 @@
             total += partner(shards[k], k).astype(f32)
         return total.astype(bf16)
 
+    layer = y + other_core(down).astype(f32)
+    layer_low = swap(layer.astype(bf16))
     dq = None
     got = []
     early = summed(pay_early)
@@ -1136,7 +1147,7 @@
         if k:
             got.append(partner(dkv, k))
         if k == half - 2:
-            dq = after(dq, early)
+            dq = after(dq, early, layer_low)
     early = jnp.stack([early, other_seq(early, 1)])
     early = after(early, dq, *got)
     early_got = [early] + [partner(early, k) for k in range(1, half)]
@@ -1147,14 +1158,18 @@
     )
     early = jnp.stack([after(v, pay_late) for v in early_got])
     early_got = [early] + [other_seq(early, 2 * d) for d in range(1, n_seq)]
-    late = summed(pay_late)
+    grad_in, grad_low = norm_back_call(mine, du_own, other_core(du_send), dh, gain_a)
+    late = after(summed(pay_late), grad_low)
     late = jnp.stack([late] + [other_seq(late, d) for d in range(1, 2 * n_seq)])
     early = jnp.stack([after(v, late) for v in early_got])
     early_twin = other_core(early)
-
-    layer = y + other_core(after(down, dom)).astype(f32)
+    back = swap(grad_low)
+    back_low, back_high = back[:CH], back[CH:]
+
     stay_flag = stays.astype(jnp.int32).reshape(1)
-    layer_out = home_call(stay_flag, layer, swap(layer.astype(bf16)))
+    layer_out = home_call(stay_flag, layer, layer_low[:CH], layer_low[CH:])
+    input_grad = home_call(stay_flag, grad_in, back_low, back_high)
+
 
     n_w = width // 128
     pieces = []
@@ -1172,15 +1187,14 @@
     for t in range(QW // 128):
         pieces.append((GU_TILES + 4 * n_w + t, 5, (slice(0, R),), t * 128, QW))
     r_gu, r_ad, r_bd, r_agu, r_bo, r_ao = place_call(
-        pieces,
+        2, pieces,
         [(2, R, FF), (R, FF), (R, width), (2 * R, width), (R, width), (R, 2 * QW)],
         n_seq, sc, early, early_twin,
     )
 
-    late = jnp.stack([late] + [partner(late, k) for k in range(1, half)])[None]
-    late_twin = after(other_core(late), r_gu)
-    grad_in, grad_low = norm_back_call(mine, du_own, other_core(du_send), dh, gain_a)
-    input_grad = home_call(stay_flag, grad_in, swap(grad_low))
+    late = [late] + [partner(late, k) for k in range(1, half)]
+    late = jnp.stack([after(v, r_gu) for v in late])[None]
+    late_twin = after(other_core(late), input_grad)
 
     pieces = []
     first_rows = (slice(0, R),)
@@ -1196,7 +1210,7 @@
         else:
             pieces.append((at, 3, first_rows, t * 128 - QW - KW, KW))
     r_aqkv, r_bq, r_bk, r_bv = place_call(
-        pieces,
+        1, pieces,
         [(3 * R, width), (R, 2 * QW), (R, 2 * KW), (R, 2 * KW)],
         n_seq, sc, late, late_twin,
     )

time: 240 us -> 216 us (0.900)
  waiting for transfers between devices: 60 us -> 46.2 us
  Pallas kernels: 111 us -> 99.6 us
    ppermute x5, waiting for transfers between devices: 23.2 us -> 9.81 us  [swap(): return lax.ppermute(v, ('ctx', 'wsh'), swap_pairs)]
    pallas_call x2, Pallas kernels: 15.6 us -> 11 us  [place_call(): pl.pallas_call(functools.partial(place_kernel, pieces, half, n_seq, rows...]
    pallas_call x1, Pallas kernels: 29.2 us -> 24.8 us  [ffn_call(): pl.pallas_call(functools.partial(ffn_kernel, per_shard), grid_spec=pltpu....]
    unnamed x74 -> x72, local copies, waits for them, and re-layouts: 6.09 us -> 5.13 us
  transfers between devices with their start and end apart: 40 -> 40, of which waited for: 15 -> 14; matrix products, arithmetic and copies ran while one was open for 6% -> 7% of each run, Pallas kernels for 29% -> 33%
where the time goes in v3:
time: 216 us; the launch traced here: 215 us
  Pallas kernels  99.6 us (46%)
  starting transfers between devices  46.6 us (22%)
  waiting for transfers between devices  46.2 us (21%)
  local copies, waits for them, and re-layouts  14.8 us (7%)
  other arithmetic  6.29 us (3%)
    pallas_call x1, Pallas kernels, ffn_call(): pl.pallas_call(functools.partial(ffn_kernel, per_shard), grid_spec=pltpu....  24.8 us
    pallas_call x4, Pallas kernels, attend_back_call(): pl.pallas_call(functools.partial(attend_back_kernel, base, first, has_dq)...  24.4 us
    ppermute x18, starting transfers between devices, partner(): lax.ppermute(v, 'ctx', [(s * half + p, s * half + (p ^ k)) for s in range...  18.5 us
    ppermute x18, waiting for transfers between devices, partner(): lax.ppermute(v, 'ctx', [(s * half + p, s * half + (p ^ k)) for s in range...  16.1 us
    ppermute x5, starting transfers between devices, swap(): return lax.ppermute(v, ('ctx', 'wsh'), swap_pairs)  16 us
    ppermute x5, waiting for transfers between devices, other_seq(): return lax.ppermute(v, ('seq', 'ctx'), pairs)  14.6 us
    pallas_call x2, Pallas kernels, attend_call(): pl.pallas_call(functools.partial(attend_kernel, bases, first), grid_spec=...  11.3 us
    pallas_call x2, Pallas kernels, place_call(): pl.pallas_call(functools.partial(place_kernel, pieces, half, n_seq, rows...  11 us
  transfers between devices with their start and end apart: 40, of which 14 were waited for; matrix products, arithmetic and copies ran while one was open for 7% of the time, Pallas kernels for 33%

profile of v3, /device:TPU:1, one launch (start us, length us, event | category | flops | bytes accessed | tf_op | source)
XLA Modules:
  0.0 215.3 jit_solution(3158541995594506038)
XLA Ops:
  0.7 5.7 %collective-permute-start.1 = (bf16[256,1024]{1,0:T(8,128)(2,1)}, bf16[256,1024]{1,0:T(8,128)(2,1)}, u32[]{:S(2)}, u32[]{:S(2)}) collective-permute-start(bf16[256,1024]{1,0:T(8,128)(2,1)} %bitcast.72), channel_id=1, source_target_pairs={{1,8},{3,10},{5,12},{7,14},{8,1},{10,3},{12,5},{14,7},{17,24},{19,... | collective-permute-start | bytes 1572872 | tf_op jit(solution)/shard_map/ppermute | solution.py:1037
  6.4 1.9 collective-permute-start
  8.4 0.7 tile.4
  9.1 0.7 tile.5
  9.9 0.7 broadcast_in_dim.23
  10.6 1.2 dynamic_slice.42
  11.8 1.3 constant_dynamic-slice_fusion.4
  13.6 5.6 %collective-permute-done = s32[1,16]{1,0:T(1,128)S(1)} collective-permute-done((s32[1,16]{1,0:T(1,128)}, s32[1,16]{1,0:T(1,128)S(1)}, u32[]{:S(2)}, u32[]{:S(2)}) %collective-permute-start) | collective-permute-done | bytes 96 | tf_op jit(solution)/shard_map/ppermute | solution.py:1037
  20.2 0.7 concatenate.34.sc
  21.1 1.1 broadcast_select_fusion.1.mine.x
  22.4 0.6 collective-permute-start.3
  23.1 1.9 collective-permute-start.8
  25.8 4.9 %qkv.1 = (bf16[512,1024]{1,0:T(8,128)(2,1)S(1)}, f32[512,768]{1,0:T(8,128)S(1)}, bf16[4,1024,128]{2,1,0:T(8,128)(2,1)S(1)}, bf16[512,512]{1,0:T(8,128)(2,1)S(1)}) custom-call(s32[24]{0:T(128)S(1)} %concatenate.34.sc, bf16[2,128,1024]{2,1,0:T(8,128)(2,1)S(1)} %bitcast.50, bf16[2,128,1024]{2,1,0:T(8,128)(2,1)S(1)} %bitcast.52, ...), custom_call_target="tpu_custom_call" | custom-call | flops 100000000 | bytes 1000000 | tf_op jit(solution)/shard_map/qkv/pallas_call | solution.py:167
  30.7 1.1 copy-done.9
  31.8 1.2 collective-permute-start.5
  33.1 3.7 %collective-permute-start.6 = (bf16[512,512]{1,0:T(8,128)(2,1)S(1)}, bf16[512,512]{1,0:T(8,128)(2,1)S(1)}, u32[]{:S(2)}, u32[]{:S(2)}) collective-permute-start(bf16[512,512]{1,0:T(8,128)(2,1)S(1)} %get-tuple-element.75.rest_0_.rest_1_.k.v), channel_id=1, source_target_pairs={{0,4},{2,6},{4,0},{6,2},{8,12},{10,14},{12,8},{14,10},{1,5},{3,7},... | collective-permute-start | bytes 1572872 | tf_op jit(solution)/shard_map/ppermute | solution.py:1043
  36.8 3.5 %attend.2.rest_6_ = f32[4,512,256]{2,1,0:T(8,128)S(1)} custom-call(s32[24]{0:T(128)S(1)} %concatenate.34.sc, bf16[4,1024,128]{2,1,0:T(8,128)(2,1)S(1)} %get-tuple-element.74.qm, bf16[512,512]{1,0:T(8,128)(2,1)S(1)} %get-tuple-element.75.rest_0_.rest_1_.k.v, bf16[512,512]{1,0:T(8,128)(2,1)S(1)} %get-tuple-element.75.rest_0_.rest_1_.k.v), custom_call_target="tpu_custom_call" | custom-call | flops 100000000 | bytes 1000000 | tf_op jit(solution)/shard_map/attend/pallas_call | solution.py:277
  40.5 0.5 collective-permute-start.9
  41.0 2.7 %constant_dynamic-slice_fusion.1 = (bf16[512,2304]{1,0:T(8,128)(2,1)S(1)}, bf16[512,2304]{1,0:T(8,128)(2,1)S(1)}) fusion(bf16[512,9216]{1,0:T(8,128)(2,1)} %wu_own.1, s32[]{:T(128)S(6)} %select_n.96, s32[]{:T(128)S(6)} %select_n.97), kind=kLoop, calls=%fused_computation.19 | loop fusion | bytes 9437192 | tf_op jit(solution)/shard_map/dynamic_slice | solution.py:1063
  43.7 2.7 %pad_maximum_fusion = bf16[512,4608]{1,0:T(8,128)(2,1)} fusion(bf16[512,2304]{1,0:T(8,128)(2,1)S(1)} %get-tuple-element.161, bf16[512,2304]{1,0:T(8,128)(2,1)S(1)} %get-tuple-element.160), kind=kLoop, calls=%fused_computation | loop fusion | flops 9437184 | bytes 9437184 | tf_op jit(solution)/shard_map/concatenate | solution.py:1115
  46.5 1.1 slice-done
  48.1 5.1 %hidden_back.1 = (f32[512,2304]{1,0:T(8,128)S(1)}, bf16[512,1024]{1,0:T(8,128)(2,1)S(1)}, bf16[16,512]{1,0:T(8,128)(2,1)S(1)}) custom-call(s32[24]{0:T(128)S(1)} %concatenate.34.sc, bf16[256,1024]{1,0:T(8,128)(2,1)S(1)} %broadcast_select_fusion.c_mine, bf16[128,1024]{1,0:T(8,128)(2,1)S(1)} %collective-permute-done.9.c_low, ...), custom_call_target="tpu_custom_call" | custom-call | flops 100000000 | bytes 1000000 | tf_op jit(solution)/shard_map/hidden_back/pallas_call | solution.py:372
  53.3 10.3 %collective-permute-done.7.rest_4_.rest_5_.k.v = bf16[512,512]{1,0:T(8,128)(2,1)S(1)} collective-permute-done((bf16[512,512]{1,0:T(8,128)(2,1)S(1)}, bf16[512,512]{1,0:T(8,128)(2,1)S(1)}, u32[]{:S(2)}, u32[]{:S(2)}) %collective-permute-start.7) | collective-permute-done | bytes 524320 | tf_op jit(solution)/shard_map/ppermute | solution.py:1043
  64.0 7.8 %attend.3.acc = f32[4,512,256]{2,1,0:T(8,128)S(1)} custom-call(s32[24]{0:T(128)S(1)} %concatenate.34.sc, bf16[4,1024,128]{2,1,0:T(8,128)(2,1)S(1)} %get-tuple-element.74.qm, bf16[512,512]{1,0:T(8,128)(2,1)S(1)} %collective-permute-done.5.rest_0_.rest_1_.k.v, ...), custom_call_target="tpu_custom_call", output_to_operand_aliasing={{}: (8, {})} | custom-call | flops 100000000 | bytes 1000000 | tf_op jit(solution)/shard_map/attend/pallas_call | solution.py:277
  71.9 2.4 %project.1 = (bf16[512,512]{1,0:T(8,128)(2,1)S(1)}, bf16[512,1024]{1,0:T(8,128)(2,1)S(1)}, f32[4,1,1024]{2,1,0:T(1,128)S(1)}) custom-call(s32[24]{0:T(128)S(1)} %concatenate.34.sc, f32[4,512,256]{2,1,0:T(8,128)S(1)} %attend.3.acc, bf16[512,1024]{1,0:T(8,128)(2,1)S(1)} %copy-done.2, bf16[8,16,1024]{2,1,0:T(8,128)(2,1)S(1)} %bitcast.58, ...), custom_call_target="tpu_custom_call" | custom-call | flops 100000000 | bytes 1000000 | tf_op jit(solution)/shard_map/project/pallas_call | solution.py:329
  74.5 2.5 %collective-permute-done.11.mix_b = bf16[512,1024]{1,0:T(8,128)(2,1)S(1)} collective-permute-done((bf16[512,1024]{1,0:T(8,128)(2,1)S(1)}, bf16[512,1024]{1,0:T(8,128)(2,1)S(1)}, u32[]{:S(2)}, u32[]{:S(2)}) %collective-permute-start.11) | collective-permute-done | bytes 1048608 | tf_op jit(solution)/shard_map/ppermute | solution.py:1040
  77.0 2.2 %copy-done.23 = bf16[512,4608]{1,0:T(8,128)(2,1)} copy-done((bf16[512,4608]{1,0:T(8,128)(2,1)}, bf16[512,4608]{1,0:T(8,128)(2,1)S(1)}, u32[]{:S(2)}) %copy-start.23) | copy-done | bytes 4718616
  79.2 24.8 %ffn.1 = (f32[256,1024]{1,0:T(8,128)S(1)}, bf16[256,1024]{1,0:T(8,128)(2,1)S(1)}, bf16[512,1024]{1,0:T(8,128)(2,1)S(1)}, bf16[1472,128]{1,0:T(8,128)(2,1)S(1)}) custom-call(s32[24]{0:T(128)S(1)} %concatenate.34.sc, bf16[256,1024]{1,0:T(8,128)(2,1)S(1)} %broadcast_select_fusion.1.mine.x, bf16[256,1024]{1,0:T(8,128)(2,1)S(1)} %collective-permute-done.2.other, ...), custom_call_target="tpu_custom_call" | custom-call | flops 1000000000 | bytes 2500000 | tf_op jit(solution)/shard_map/ffn/pallas_call | solution.py:506
  104.6 2.9 %collective-permute-done.13 = bf16[256,1024]{1,0:T(8,128)(2,1)S(1)} collective-permute-done((bf16[256,1024]{1,0:T(8,128)(2,1)S(1)}, bf16[256,1024]{1,0:T(8,128)(2,1)S(1)}, u32[]{:S(2)}, u32[]{:S(2)}) %collective-permute-start.13) | collective-permute-done | bytes 524320 | tf_op jit(solution)/shard_map/ppermute | solution.py:1040
  107.7 1.9 collective-permute-start.14
  109.6 5.7 %back_mix.1 = (f32[256,1024]{1,0:T(8,128)S(1)}, bf16[4,1024,128]{2,1,0:T(8,128)(2,1)S(1)}, f32[4,1,1024]{2,1,0:T(1,128)S(1)}, bf16[1472,128]{1,0:T(8,128)(2,1)S(1)}) custom-call(s32[24]{0:T(128)S(1)} %concatenate.34.sc, bf16[2,128,1024]{2,1,0:T(8,128)(2,1)S(1)} %bitcast.51, bf16[2,128,1024]{2,1,0:T(8,128)(2,1)S(1)} %bitcast.53, ...), custom_call_target="tpu_custom_call", output_to_operand_aliasing={{3}: (14, {})} | custom-call | flops 100000000 | bytes 1000000 | tf_op jit(solution)/shard_map/back_mix/pallas_call | solution.py:616
  115.8 0.7 collective-permute-start.17
  116.6 1.5 collective-permute-start.18
  118.1 6.1 %attend_back.4 = (f32[4,64,1024]{2,1,0:T(8,128)S(1)}, bf16[2,512,256]{2,1,0:T(8,128)(2,1)S(1)}) custom-call(s32[24]{0:T(128)S(1)} %concatenate.34.sc, bf16[4,1024,128]{2,1,0:T(8,128)(2,1)S(1)} %get-tuple-element.74.qm, bf16[4,1024,128]{2,1,0:T(8,128)(2,1)S(1)} %get-tuple-element.90.dom, bf16[512,512]{1,0:T(8,128)(2,1)S(1)} %collective-permute-done.5.rest_0_.rest_1_.k.v, ...), custom_call_target="tpu_custom_call" | custom-call | flops 100000000 | bytes 1000000 | tf_op jit(solution)/shard_map/attend_back/pallas_call | solution.py:717
  124.1 6.1 %attend_back.5 = (f32[4,64,1024]{2,1,0:T(8,128)S(1)}, bf16[2,512,256]{2,1,0:T(8,128)(2,1)S(1)}) custom-call(s32[24]{0:T(128)S(1)} %concatenate.34.sc, bf16[4,1024,128]{2,1,0:T(8,128)(2,1)S(1)} %get-tuple-element.74.qm, bf16[4,1024,128]{2,1,0:T(8,128)(2,1)S(1)} %get-tuple-element.90.dom, ...), custom_call_target="tpu_custom_call", output_to_operand_aliasing={{0}: (7, {})} | custom-call | flops 100000000 | bytes 1000000 | tf_op jit(solution)/shard_map/attend_back/pallas_call | solution.py:717
  130.3 1.0 collective-permute-start.20
  131.5 6.1 %attend_back.6 = (f32[4,64,1024]{2,1,0:T(8,128)S(1)}, bf16[2,512,256]{2,1,0:T(8,128)(2,1)S(1)}) custom-call(s32[24]{0:T(128)S(1)} %concatenate.34.sc, bf16[4,1024,128]{2,1,0:T(8,128)(2,1)S(1)} %get-tuple-element.74.qm, bf16[4,1024,128]{2,1,0:T(8,128)(2,1)S(1)} %get-tuple-element.90.dom, ...), custom_call_target="tpu_custom_call", output_to_operand_aliasing={{0}: (7, {})} | custom-call | flops 100000000 | bytes 1000000 | tf_op jit(solution)/shard_map/attend_back/pallas_call | solution.py:717
  137.7 1.6 collective-permute-start.21
  139.3 6.1 %attend_back.7 = (f32[4,64,1024]{2,1,0:T(8,128)S(1)}, f32[2,512,256]{2,1,0:T(8,128)S(1)}) custom-call(s32[24]{0:T(128)S(1)} %concatenate.34.sc, bf16[4,1024,128]{2,1,0:T(8,128)(2,1)S(1)} %get-tuple-element.74.qm, bf16[4,1024,128]{2,1,0:T(8,128)(2,1)S(1)} %get-tuple-element.90.dom, ...), custom_call_target="tpu_custom_call", output_to_operand_aliasing={{0}: (7, {})} | custom-call | flops 100000000 | bytes 1000000 | tf_op jit(solution)/shard_map/attend_back/pallas_call | solution.py:717
  145.4 9.9 %collective-permute-done.30 = bf16[368,128]{1,0:T(8,128)(2,1)S(1)} collective-permute-done((bf16[368,128]{1,0:T(8,128)(2,1)S(1)}, bf16[368,128]{1,0:T(8,128)(2,1)S(1)}, u32[]{:S(2)}, u32[]{:S(2)}) %collective-permute-start.30) | collective-permute-done | bytes 94240 | tf_op jit(solution)/shard_map/ppermute | solution.py:1052
  155.3 2.1 collective-permute-done.21.rest_2_
  157.5 1.0 collective-permute-start.31
  158.5 1.6 collective-permute-start.33
  160.1 6.5 %qkv_back.1 = (f32[256,1024]{1,0:T(8,128)S(1)}, bf16[256,1024]{1,0:T(8,128)(2,1)S(1)}, bf16[512,128]{1,0:T(8,128)(2,1)S(1)}) custom-call(s32[24]{0:T(128)S(1)} %concatenate.34.sc, f32[4,64,1024]{2,1,0:T(8,128)S(1)} %get-tuple-element.98.dq, f32[2,512,256]{2,1,0:T(8,128)S(1)} %get-tuple-element.99.dkv, ...), custom_call_target="tpu_custom_call" | custom-call | flops 100000000 | bytes 1000000 | tf_op jit(solution)/shard_map/qkv_back/pallas_call | solution.py:829
  166.7 1.3 collective-permute-done.33
  168.1 1.3 collective-permute-start.34
  169.4 2.1 collective-permute-start.22
  171.5 1.1 collective-permute-start.24
  172.6 1.6 collective-permute-start.26
  174.6 1.1 collective-permute-done.25
  175.6 0.9 collective-permute-done.26
  176.6 1.3 norm_back.1
  178.2 3.3 %collective-permute-start.29 = (bf16[128,128]{1,0:T(8,128)(2,1)S(1)}, bf16[128,128]{1,0:T(8,128)(2,1)S(1)}, u32[]{:S(2)}, u32[]{:S(2)}) collective-permute-start(bf16[128,128]{1,0:T(8,128)(2,1)S(1)} %add_convert_fusion.1), channel_id=1, source_target_pairs={{0,24},{2,26},{4,28},{6,30},{8,16},{10,18},{12,20},{14,22},{16,8},... | collective-permute-start | bytes 98312 | tf_op jit(solution)/shard_map/ppermute | solution.py:1052
  181.6 4.6 %collective-permute-done.28 = bf16[128,128]{1,0:T(8,128)(2,1)S(1)} collective-permute-done((bf16[128,128]{1,0:T(8,128)(2,1)S(1)}, bf16[128,128]{1,0:T(8,128)(2,1)S(1)}, u32[]{:S(2)}, u32[]{:S(2)}) %collective-permute-start.28) | collective-permute-done | bytes 32800 | tf_op jit(solution)/shard_map/ppermute | solution.py:1052
  186.3 2.8 %collective-permute-start.35 = (bf16[2,4,2,368,128]{4,3,2,1,0:T(8,128)(2,1)S(1)}, bf16[2,4,2,368,128]{4,3,2,1,0:T(8,128)(2,1)S(1)}, u32[]{:S(2)}, u32[]{:S(2)}) collective-permute-start(bf16[2,4,2,368,128]{4,3,2,1,0:T(8,128)(2,1)S(1)} %pad_maximum_fusion.1.own_core), channel_id=1, source_target_pairs={{0,1},{1,0},{2,3},{3,2},{4,5},{5,4},{6,7},{7,6},{8,9},{9,8},{10,11... | collective-permute-start | bytes 4521992 | tf_op jit(solution)/shard_map/ppermute | solution.py:1040
  189.1 1.0 collective-permute-start.36
  190.5 1.3 collective-permute-start.38
  191.8 4.5 %collective-permute-start.23 = (bf16[256,1024]{1,0:T(8,128)(2,1)}, bf16[256,1024]{1,0:T(8,128)(2,1)}, u32[]{:S(2)}, u32[]{:S(2)}) collective-permute-start(bf16[256,1024]{1,0:T(8,128)(2,1)} %get-tuple-element.109), channel_id=1, source_target_pairs={{1,8},{3,10},{5,12},{7,14},{8,1},{10,3},{12,5},{14,7},{17,24},{19,... | collective-permute-start | bytes 1572872 | tf_op jit(solution)/shard_map/ppermute | solution.py:1037
  196.3 7.3 %place.2 = (f32[8,2,16,4608]{3,2,1,0:T(8,128)}, f32[8,16,4608]{2,1,0:T(8,128)}, f32[8,16,1024]{2,1,0:T(8,128)}, f32[8,32,1024]{2,1,0:T(8,128)}, f32[8,16,1024]{2,1,0:T(8,128)}, /*index=5*/f32[8,16,1024]{2,1,0:T(8,128)}) custom-call(s32[24]{0:T(128)S(1)} %concatenate.34.sc, bf16[2,4,2,368,128]{4,3,2,1,0:T(8,128)(2,1)S(1)} %pad_maximum_fusion.1.own_core, ...), custom_call_target="tpu_custom_call" | custom-call | flops 10000000 | bytes 1000000 | tf_op jit(solution)/shard_map/place/pallas_call | solution.py:971
  203.8 1.2 home.2
  204.9 4.2 %collective-permute-done.23 = bf16[256,1024]{1,0:T(8,128)(2,1)} collective-permute-done((bf16[256,1024]{1,0:T(8,128)(2,1)}, bf16[256,1024]{1,0:T(8,128)(2,1)}, u32[]{:S(2)}, u32[]{:S(2)}) %collective-permute-start.23) | collective-permute-done | bytes 524320 | tf_op jit(solution)/shard_map/ppermute | solution.py:1037
  209.1 1.1 fusion.3
  210.2 1.2 home.3
  211.4 3.7 %place.3 = (f32[8,48,1024]{2,1,0:T(8,128)}, f32[8,16,1024]{2,1,0:T(8,128)}, f32[8,16,512]{2,1,0:T(8,128)}, f32[8,16,512]{2,1,0:T(8,128)}) custom-call(s32[24]{0:T(128)S(1)} %concatenate.34.sc, bf16[1,4,4,128,128]{4,3,2,1,0:T(8,128)(2,1)S(1)} %maximum_bitcast_fusion.own_core, bf16[1,4,4,128,128]{4,3,2,1,0:T(8,128)(2,1)} %collective-permute-done.39.twin), custom_call_target="tpu_custom_call" | custom-call | flops 10000000 | bytes 1000000 | tf_op jit(solution)/shard_map/place/pallas_call | solution.py:971
  (154 shorter events, 7.4 us)
Async XLA Ops:
  0.6 12.4 %copy-start.25 = (bf16[512,2048]{1,0:T(8,128)(2,1)S(1)}, bf16[512,2048]{1,0:T(8,128)(2,1)}, u32[]{:S(2)}) copy-start(bf16[512,2048]{1,0:T(8,128)(2,1)} %param.30) | copy-start | bytes 6291460
  0.7 20.4 %collective-permute-start.1 = (bf16[256,1024]{1,0:T(8,128)(2,1)}, bf16[256,1024]{1,0:T(8,128)(2,1)}, u32[]{:S(2)}, u32[]{:S(2)}) collective-permute-start(bf16[256,1024]{1,0:T(8,128)(2,1)} %bitcast.72), channel_id=1, source_target_pairs={{1,8},{3,10},{5,12},{7,14},{8,1},{10,3},{12,5},{14,7},{17,24},{19,... | collective-permute-start | bytes 1572872 | tf_op jit(solution)/shard_map/ppermute | solution.py:1037
  6.4 12.8 %collective-permute-start = (s32[1,16]{1,0:T(1,128)}, s32[1,16]{1,0:T(1,128)S(1)}, u32[]{:S(2)}, u32[]{:S(2)}) collective-permute-start(s32[1,16]{1,0:T(1,128)} %param.49), channel_id=1, source_target_pairs={{1,8},{3,10},{5,12},{7,14},{8,1},{10,3},{12,5},{14,7},{17,24},{19,... | collective-permute-start | bytes 200 | tf_op jit(solution)/shard_map/ppermute | solution.py:1037
  13.2 6.0 %copy-start.33 = (s32[1,16]{1,0:T(1,128)S(1)}, s32[1,16]{1,0:T(1,128)}, u32[]{:S(2)}) copy-start(s32[1,16]{1,0:T(1,128)} %param.49) | copy-start | bytes 196
  13.3 7.0 %copy-start.31 = (s32[4]{0:T(128)S(1)}, s32[4]{0:T(128)}, u32[]{:S(2)}) copy-start(s32[4]{0:T(128)} %param.48) | copy-start | bytes 52
  13.3 7.7 %copy-start.32 = (f32[32]{0:T(128)S(1)}, f32[32]{0:T(128)}, u32[]{:S(2)}) copy-start(f32[32]{0:T(128)} %constant.92.clone) | copy-start | bytes 388
  13.3 7.8 %copy-start.26 = (bf16[256,1,1024]{2,0,1:T(8,128)(2,1)S(1)}, bf16[256,1,1024]{2,0,1:T(8,128)(2,1)}, u32[]{:S(2)}) copy-start(bf16[256,1,1024]{2,0,1:T(8,128)(2,1)} %param.28) | copy-start | bytes 1572868
  13.6 9.5 %copy-start.27 = (bf16[256,1,1024]{2,0,1:T(8,128)(2,1)S(1)}, bf16[256,1,1024]{2,0,1:T(8,128)(2,1)}, u32[]{:S(2)}) copy-start(bf16[256,1,1024]{2,0,1:T(8,128)(2,1)} %param.29) | copy-start | bytes 1572868
  13.6 11.4 %copy-start.28 = (f32[128,32]{1,0:T(8,128)S(1)}, f32[128,32]{1,0:T(8,128)}, u32[]{:S(2)}) copy-start(f32[128,32]{1,0:T(8,128)} %constant.100) | copy-start | bytes 49156
  13.6 11.4 %copy-start.29 = (f32[128,32]{1,0:T(8,128)S(1)}, f32[128,32]{1,0:T(8,128)}, u32[]{:S(2)}) copy-start(f32[128,32]{1,0:T(8,128)} %constant.99) | copy-start | bytes 49156
  22.3 3.5 %collective-permute-start.2 = (bf16[256,1024]{1,0:T(8,128)(2,1)S(1)}, bf16[256,1024]{1,0:T(8,128)(2,1)S(1)}, u32[]{:S(2)}, u32[]{:S(2)}) collective-permute-start(bf16[256,1024]{1,0:T(8,128)(2,1)S(1)} %broadcast_select_fusion.1.mine.x), channel_id=1, source_target_pairs={{0,1},{1,0},{2,3},{3,2},{4,5},{5,4},{6,7},{7,6},{8,9},{9,8},{10,11... | collective-permute-start | bytes 1572872 | tf_op jit(solution)/shard_map/ppermute | solution.py:1040
  22.4 3.2 %collective-permute-start.3 = (bf16[512,512]{1,0:T(8,128)(2,1)S(1)}, bf16[512,512]{1,0:T(8,128)(2,1)S(1)}, u32[]{:S(2)}, u32[]{:S(2)}) collective-permute-start(bf16[512,512]{1,0:T(8,128)(2,1)S(1)} %get-tuple-element.169), channel_id=1, source_target_pairs={{0,1},{1,0},{2,3},{3,2},{4,5},{5,4},{6,7},{7,6},{8,9},{9,8},{10,11... | collective-permute-start | bytes 1572872 | tf_op jit(solution)/shard_map/ppermute | solution.py:1040
  23.0 2.8 %collective-permute-start.4 = (bf16[512,512]{1,0:T(8,128)(2,1)S(1)}, bf16[512,512]{1,0:T(8,128)(2,1)S(1)}, u32[]{:S(2)}, u32[]{:S(2)}) collective-permute-start(bf16[512,512]{1,0:T(8,128)(2,1)S(1)} %get-tuple-element.168), channel_id=1, source_target_pairs={{0,1},{1,0},{2,3},{3,2},{4,5},{5,4},{6,7},{7,6},{8,9},{9,8},{10,11... | collective-permute-start | bytes 1572872 | tf_op jit(solution)/shard_map/ppermute | solution.py:1040
  23.1 17.2 %collective-permute-start.8 = (bf16[256,1024]{1,0:T(8,128)(2,1)S(1)}, bf16[256,1024]{1,0:T(8,128)(2,1)S(1)}, u32[]{:S(2)}, u32[]{:S(2)}) collective-permute-start(bf16[256,1024]{1,0:T(8,128)(2,1)S(1)} %bitcast.73), channel_id=1, source_target_pairs={{1,8},{3,10},{5,12},{7,14},{8,1},{10,3},{12,5},{14,7},{17,24},{19,... | collective-permute-start | bytes 1572872 | tf_op jit(solution)/shard_map/ppermute | solution.py:1037
  25.6 5.1 %copy-start.5 = (bf16[512,512]{1,0:T(8,128)(2,1)}, bf16[512,512]{1,0:T(8,128)(2,1)S(1)}, u32[]{:S(2)}) copy-start(bf16[512,512]{1,0:T(8,128)(2,1)S(1)} %collective-permute-done.3.w_rec_q.rest_10_) | copy-start | bytes 1572868
  25.8 4.9 %copy-start.7 = (bf16[512,512]{1,0:T(8,128)(2,1)}, bf16[512,512]{1,0:T(8,128)(2,1)S(1)}, u32[]{:S(2)}) copy-start(bf16[512,512]{1,0:T(8,128)(2,1)S(1)} %collective-permute-done.4.w_rec_kv.rest_11_) | copy-start | bytes 1572868
  31.8 8.4 %copy-start.13 = (bf16[512,1024]{1,0:T(8,128)(2,1)}, bf16[512,1024]{1,0:T(8,128)(2,1)S(1)}, u32[]{:S(2)}) copy-start(bf16[512,1024]{1,0:T(8,128)(2,1)S(1)} %get-tuple-element.104.rest_8_) | copy-start | bytes 3145732
  31.8 21.4 %collective-permute-start.5 = (bf16[512,512]{1,0:T(8,128)(2,1)S(1)}, bf16[512,512]{1,0:T(8,128)(2,1)S(1)}, u32[]{:S(2)}, u32[]{:S(2)}) collective-permute-start(bf16[512,512]{1,0:T(8,128)(2,1)S(1)} %get-tuple-element.75.rest_0_.rest_1_.k.v), channel_id=1, source_target_pairs={{0,2},{2,0},{4,6},{6,4},{8,10},{10,8},{12,14},{14,12},{1,3},{3,1},... | collective-permute-start | bytes 1572872 | tf_op jit(solution)/shard_map/ppermute | solution.py:1043
  33.1 20.2 %collective-permute-start.6 = (bf16[512,512]{1,0:T(8,128)(2,1)S(1)}, bf16[512,512]{1,0:T(8,128)(2,1)S(1)}, u32[]{:S(2)}, u32[]{:S(2)}) collective-permute-start(bf16[512,512]{1,0:T(8,128)(2,1)S(1)} %get-tuple-element.75.rest_0_.rest_1_.k.v), channel_id=1, source_target_pairs={{0,4},{2,6},{4,0},{6,2},{8,12},{10,14},{12,8},{14,10},{1,5},{3,7},... | collective-permute-start | bytes 1572872 | tf_op jit(solution)/shard_map/ppermute | solution.py:1043
  36.8 26.7 %collective-permute-start.7 = (bf16[512,512]{1,0:T(8,128)(2,1)S(1)}, bf16[512,512]{1,0:T(8,128)(2,1)S(1)}, u32[]{:S(2)}, u32[]{:S(2)}) collective-permute-start(bf16[512,512]{1,0:T(8,128)(2,1)S(1)} %get-tuple-element.75.rest_0_.rest_1_.k.v), channel_id=1, source_target_pairs={{0,6},{2,4},{4,2},{6,0},{8,14},{10,12},{12,10},{14,8},{1,7},{3,5},... | collective-permute-start | bytes 1572872 | tf_op jit(solution)/shard_map/ppermute | solution.py:1043
  40.4 6.1 %collective-permute-start.10 = (bf16[128,1024]{1,0:T(8,128)(2,1)S(1)}, bf16[128,1024]{1,0:T(8,128)(2,1)S(1)}, u32[]{:S(2)}, u32[]{:S(2)}) collective-permute-start(bf16[128,1024]{1,0:T(8,128)(2,1)S(1)} %get-tuple-element.174), channel_id=1, source_target_pairs={{0,1},{1,0},{2,3},{3,2},{4,5},{5,4},{6,7},{7,6},{8,9},{9,8},{10,11... | collective-permute-start | bytes 786440 | tf_op jit(solution)/shard_map/ppermute | solution.py:1040
  40.5 6.0 %collective-permute-start.9 = (bf16[128,1024]{1,0:T(8,128)(2,1)S(1)}, bf16[128,1024]{1,0:T(8,128)(2,1)S(1)}, u32[]{:S(2)}, u32[]{:S(2)}) collective-permute-start(bf16[128,1024]{1,0:T(8,128)(2,1)S(1)} %get-tuple-element.175), channel_id=1, source_target_pairs={{0,1},{1,0},{2,3},{3,2},{4,5},{5,4},{6,7},{7,6},{8,9},{9,8},{10,11... | collective-permute-start | bytes 786440 | tf_op jit(solution)/shard_map/ppermute | solution.py:1040
  48.1 15.4 %copy-start.24 = (bf16[512,4608]{1,0:T(8,128)(2,1)S(1)}, bf16[512,4608]{1,0:T(8,128)(2,1)}, u32[]{:S(2)}) copy-start(bf16[512,4608]{1,0:T(8,128)(2,1)} %pad_maximum_fusion) | copy-start | bytes 14155780
  53.2 18.6 %copy-start = (f32[512,2304]{1,0:T(8,128)}, f32[512,2304]{1,0:T(8,128)S(1)}, u32[]{:S(2)}) copy-start(f32[512,2304]{1,0:T(8,128)S(1)} %get-tuple-element.78.dh_tile) | copy-start | bytes 14155780
  63.5 8.3 %copy-start.2 = (bf16[512,1024]{1,0:T(8,128)(2,1)S(1)}, bf16[512,1024]{1,0:T(8,128)(2,1)}, u32[]{:S(2)}) copy-start(bf16[512,1024]{1,0:T(8,128)(2,1)} %w_o.3) | copy-start | bytes 3145732
  63.5 8.3 %copy-start.17 = (bf16[8,1024,16]{1,2,0:T(8,128)(2,1)S(1)}, bf16[8,1024,16]{1,2,0:T(8,128)(2,1)}, u32[]{:S(2)}) copy-start(bf16[8,1024,16]{1,2,0:T(8,128)(2,1)} %param.42) | copy-start | bytes 786436
  63.5 8.4 %copy-start.18 = (bf16[8,16,1024]{2,1,0:T(8,128)(2,1)S(1)}, bf16[8,16,1024]{2,1,0:T(8,128)(2,1)}, u32[]{:S(2)}) copy-start(bf16[8,16,1024]{2,1,0:T(8,128)(2,1)} %b_o.3) | copy-start | bytes 786436
  63.5 13.5 %collective-permute-start.12 = (bf16[512,4608]{1,0:T(8,128)(2,1)S(1)}, bf16[512,4608]{1,0:T(8,128)(2,1)S(1)}, u32[]{:S(2)}, u32[]{:S(2)}) collective-permute-start(bf16[512,4608]{1,0:T(8,128)(2,1)S(1)} %copy-done.24), channel_id=1, source_target_pairs={{0,1},{1,0},{2,3},{3,2},{4,5},{5,4},{6,7},{7,6},{8,9},{9,8},{10,11... | collective-permute-start | bytes 14155784 | tf_op jit(solution)/shard_map/ppermute | solution.py:1040
  71.8 7.4 %copy-start.4 = (bf16[8,2,16,4608]{3,2,1,0:T(8,128)(2,1)S(1)}, bf16[8,2,16,4608]{3,2,1,0:T(8,128)(2,1)}, u32[]{:S(2)}) copy-start(bf16[8,2,16,4608]{3,2,1,0:T(8,128)(2,1)} %b_gu.1) | copy-start | bytes 7077892
  71.8 7.4 %copy-start.19 = (bf16[8,1024,32]{1,2,0:T(8,128)(2,1)S(1)}, bf16[8,1024,32]{1,2,0:T(8,128)(2,1)}, u32[]{:S(2)}) copy-start(bf16[8,1024,32]{1,2,0:T(8,128)(2,1)} %param.44) | copy-start | bytes 1572868
  74.3 2.7 %collective-permute-start.11 = (bf16[512,1024]{1,0:T(8,128)(2,1)S(1)}, bf16[512,1024]{1,0:T(8,128)(2,1)S(1)}, u32[]{:S(2)}, u32[]{:S(2)}) collective-permute-start(bf16[512,1024]{1,0:T(8,128)(2,1)S(1)} %get-tuple-element.81.mix_a), channel_id=1, source_target_pairs={{0,1},{1,0},{2,3},{3,2},{4,5},{5,4},{6,7},{7,6},{8,9},{9,8},{10,11... | collective-permute-start | bytes 3145736 | tf_op jit(solution)/shard_map/ppermute | solution.py:1040
  104.0 5.6 %collective-permute-start.15 = (bf16[512,1024]{1,0:T(8,128)(2,1)S(1)}, bf16[512,1024]{1,0:T(8,128)(2,1)S(1)}, u32[]{:S(2)}, u32[]{:S(2)}) collective-permute-start(bf16[512,1024]{1,0:T(8,128)(2,1)S(1)} %get-tuple-element.87.du_a), channel_id=1, source_target_pairs={{0,1},{1,0},{2,3},{3,2},{4,5},{5,4},{6,7},{7,6},{8,9},{9,8},{10,11... | collective-permute-start | bytes 3145736 | tf_op jit(solution)/shard_map/ppermute | solution.py:1040
  104.2 3.3 %collective-permute-start.13 = (bf16[256,1024]{1,0:T(8,128)(2,1)S(1)}, bf16[256,1024]{1,0:T(8,128)(2,1)S(1)}, u32[]{:S(2)}, u32[]{:S(2)}) collective-permute-start(bf16[256,1024]{1,0:T(8,128)(2,1)S(1)} %get-tuple-element.86), channel_id=1, source_target_pairs={{0,1},{1,0},{2,3},{3,2},{4,5},{5,4},{6,7},{7,6},{8,9},{9,8},{10,11... | collective-permute-start | bytes 1572872 | tf_op jit(solution)/shard_map/ppermute | solution.py:1040
  107.7 23.8 %collective-permute-start.14 = (bf16[256,1024]{1,0:T(8,128)(2,1)S(1)}, bf16[256,1024]{1,0:T(8,128)(2,1)S(1)}, u32[]{:S(2)}, u32[]{:S(2)}) collective-permute-start(bf16[256,1024]{1,0:T(8,128)(2,1)S(1)} %get-tuple-element.158), channel_id=1, source_target_pairs={{1,8},{3,10},{5,12},{7,14},{8,1},{10,3},{12,5},{14,7},{17,24},{19,... | collective-permute-start | bytes 1572872 | tf_op jit(solution)/shard_map/ppermute | solution.py:1037
  115.3 15.9 %collective-permute-start.16 = (bf16[368,128]{1,0:T(8,128)(2,1)S(1)}, bf16[368,128]{1,0:T(8,128)(2,1)S(1)}, u32[]{:S(2)}, u32[]{:S(2)}) collective-permute-start(bf16[368,128]{1,0:T(8,128)(2,1)S(1)} %get-tuple-element.176), channel_id=1, source_target_pairs={{0,2},{2,0},{4,6},{6,4},{8,10},{10,8},{12,14},{14,12},{1,3},{3,1},... | collective-permute-start | bytes 282632 | tf_op jit(solution)/shard_map/ppermute | solution.py:1043
  115.8 15.6 %collective-permute-start.17 = (bf16[368,128]{1,0:T(8,128)(2,1)S(1)}, bf16[368,128]{1,0:T(8,128)(2,1)S(1)}, u32[]{:S(2)}, u32[]{:S(2)}) collective-permute-start(bf16[368,128]{1,0:T(8,128)(2,1)S(1)} %get-tuple-element.178), channel_id=1, source_target_pairs={{0,4},{2,6},{4,0},{6,2},{8,12},{10,14},{12,8},{14,10},{1,5},{3,7},... | collective-permute-start | bytes 282632 | tf_op jit(solution)/shard_map/ppermute | solution.py:1043
  116.6 14.9 %collective-permute-start.18 = (bf16[368,128]{1,0:T(8,128)(2,1)S(1)}, bf16[368,128]{1,0:T(8,128)(2,1)S(1)}, u32[]{:S(2)}, u32[]{:S(2)}) collective-permute-start(bf16[368,128]{1,0:T(8,128)(2,1)S(1)} %get-tuple-element.177), channel_id=1, source_target_pairs={{0,6},{2,4},{4,2},{6,0},{8,14},{10,12},{12,10},{14,8},{1,7},{3,5},... | collective-permute-start | bytes 282632 | tf_op jit(solution)/shard_map/ppermute | solution.py:1043
  130.3 25.1 %collective-permute-start.20 = (bf16[2,512,256]{2,1,0:T(8,128)(2,1)S(1)}, bf16[2,512,256]{2,1,0:T(8,128)(2,1)S(1)}, u32[]{:S(2)}, u32[]{:S(2)}) collective-permute-start(bf16[2,512,256]{2,1,0:T(8,128)(2,1)S(1)} %get-tuple-element.101), channel_id=1, source_target_pairs={{0,4},{2,6},{4,0},{6,2},{8,12},{10,14},{12,8},{14,10},{1,5},{3,7},... | collective-permute-start | bytes 1572872 | tf_op jit(solution)/shard_map/ppermute | solution.py:1043
  131.2 24.1 %collective-permute-start.19 = (bf16[2,512,256]{2,1,0:T(8,128)(2,1)S(1)}, bf16[2,512,256]{2,1,0:T(8,128)(2,1)S(1)}, u32[]{:S(2)}, u32[]{:S(2)}) collective-permute-start(bf16[2,512,256]{2,1,0:T(8,128)(2,1)S(1)} %get-tuple-element.100), channel_id=1, source_target_pairs={{0,2},{2,0},{4,6},{6,4},{8,10},{10,8},{12,14},{14,12},{1,3},{3,1},... | collective-permute-start | bytes 1572872 | tf_op jit(solution)/shard_map/ppermute | solution.py:1043
  137.7 19.8 %collective-permute-start.21 = (bf16[2,512,256]{2,1,0:T(8,128)(2,1)S(1)}, bf16[2,512,256]{2,1,0:T(8,128)(2,1)S(1)}, u32[]{:S(2)}, u32[]{:S(2)}) collective-permute-start(bf16[2,512,256]{2,1,0:T(8,128)(2,1)S(1)} %get-tuple-element.102), channel_id=1, source_target_pairs={{0,6},{2,4},{4,2},{6,0},{8,14},{10,12},{12,10},{14,8},{1,7},{3,5},... | collective-permute-start | bytes 1572872 | tf_op jit(solution)/shard_map/ppermute | solution.py:1043
  139.2 16.1 %collective-permute-start.30 = (bf16[368,128]{1,0:T(8,128)(2,1)S(1)}, bf16[368,128]{1,0:T(8,128)(2,1)S(1)}, u32[]{:S(2)}, u32[]{:S(2)}) collective-permute-start(bf16[368,128]{1,0:T(8,128)(2,1)S(1)} %add_convert_fusion), channel_id=1, source_target_pairs={{0,8},{2,10},{4,12},{6,14},{8,0},{10,2},{12,4},{14,6},{16,24},{18,... | collective-permute-start | bytes 282632 | tf_op jit(solution)/shard_map/ppermute | solution.py:1052
  139.2 20.9 %copy-start.6 = (bf16[512,512]{1,0:T(8,128)(2,1)S(1)}, bf16[512,512]{1,0:T(8,128)(2,1)}, u32[]{:S(2)}) copy-start(bf16[512,512]{1,0:T(8,128)(2,1)} %copy-done.5) | copy-start | bytes 1572868
  139.2 20.9 %copy-start.8 = (bf16[512,512]{1,0:T(8,128)(2,1)S(1)}, bf16[512,512]{1,0:T(8,128)(2,1)}, u32[]{:S(2)}) copy-start(bf16[512,512]{1,0:T(8,128)(2,1)} %copy-done.7) | copy-start | bytes 1572868
  139.2 20.9 %copy-start.10 = (f32[512,768]{1,0:T(8,128)S(1)}, f32[512,768]{1,0:T(8,128)}, u32[]{:S(2)}) copy-start(f32[512,768]{1,0:T(8,128)} %copy-done.9) | copy-start | bytes 4718596
  139.2 20.9 %copy-start.14 = (bf16[512,1024]{1,0:T(8,128)(2,1)S(1)}, bf16[512,1024]{1,0:T(8,128)(2,1)}, u32[]{:S(2)}) copy-start(bf16[512,1024]{1,0:T(8,128)(2,1)} %copy-done.13) | copy-start | bytes 3145732
  139.3 20.9 %copy-start.16 = (bf16[8,16,1024]{2,1,0:T(8,128)(2,1)S(1)}, bf16[8,16,1024]{2,1,0:T(8,128)(2,1)}, u32[]{:S(2)}) copy-start(bf16[8,16,1024]{2,1,0:T(8,128)(2,1)} %rest_13_.1) | copy-start | bytes 786436
  139.3 20.9 %copy-start.22 = (bf16[8,16,512]{2,1,0:T(8,128)(2,1)S(1)}, bf16[8,16,512]{2,1,0:T(8,128)(2,1)}, u32[]{:S(2)}) copy-start(bf16[8,16,512]{2,1,0:T(8,128)(2,1)} %rest_15_.1) | copy-start | bytes 393220
  157.5 9.2 %collective-permute-start.31 = (bf16[2,368,128]{2,1,0:T(8,128)(2,1)S(1)}, bf16[2,368,128]{2,1,0:T(8,128)(2,1)S(1)}, u32[]{:S(2)}, u32[]{:S(2)}) collective-permute-start(bf16[2,368,128]{2,1,0:T(8,128)(2,1)S(1)} %pad_maximum_fusion.7), channel_id=1, source_target_pairs={{0,2},{2,0},{4,6},{6,4},{8,10},{10,8},{12,14},{14,12},{1,3},{3,1},... | collective-permute-start | bytes 565256 | tf_op jit(solution)/shard_map/ppermute | solution.py:1043
  158.5 8.2 %collective-permute-start.32 = (bf16[2,368,128]{2,1,0:T(8,128)(2,1)S(1)}, bf16[2,368,128]{2,1,0:T(8,128)(2,1)S(1)}, u32[]{:S(2)}, u32[]{:S(2)}) collective-permute-start(bf16[2,368,128]{2,1,0:T(8,128)(2,1)S(1)} %pad_maximum_fusion.7), channel_id=1, source_target_pairs={{0,4},{2,6},{4,0},{6,2},{8,12},{10,14},{12,8},{14,10},{1,5},{3,7},... | collective-permute-start | bytes 565256 | tf_op jit(solution)/shard_map/ppermute | solution.py:1043
  158.5 9.6 %collective-permute-start.33 = (bf16[2,368,128]{2,1,0:T(8,128)(2,1)S(1)}, bf16[2,368,128]{2,1,0:T(8,128)(2,1)S(1)}, u32[]{:S(2)}, u32[]{:S(2)}) collective-permute-start(bf16[2,368,128]{2,1,0:T(8,128)(2,1)S(1)} %pad_maximum_fusion.7), channel_id=1, source_target_pairs={{0,6},{2,4},{4,2},{6,0},{8,14},{10,12},{12,10},{14,8},{1,7},{3,5},... | collective-permute-start | bytes 565256 | tf_op jit(solution)/shard_map/ppermute | solution.py:1043
  168.1 18.0 %collective-permute-start.34 = (bf16[4,2,368,128]{3,2,1,0:T(8,128)(2,1)S(1)}, bf16[4,2,368,128]{3,2,1,0:T(8,128)(2,1)S(1)}, u32[]{:S(2)}, u32[]{:S(2)}) collective-permute-start(bf16[4,2,368,128]{3,2,1,0:T(8,128)(2,1)S(1)} %pad_maximum_fusion.4), channel_id=1, source_target_pairs={{0,16},{2,18},{4,20},{6,22},{8,24},{10,26},{12,28},{14,30},{16,0},... | collective-permute-start | bytes 2261000 | tf_op jit(solution)/shard_map/ppermute | solution.py:1052
  169.4 7.2 %collective-permute-start.22 = (bf16[256,1024]{1,0:T(8,128)(2,1)S(1)}, bf16[256,1024]{1,0:T(8,128)(2,1)S(1)}, u32[]{:S(2)}, u32[]{:S(2)}) collective-permute-start(bf16[256,1024]{1,0:T(8,128)(2,1)S(1)} %get-tuple-element.106), channel_id=1, source_target_pairs={{0,1},{1,0},{2,3},{3,2},{4,5},{5,4},{6,7},{7,6},{8,9},{9,8},{10,11... | collective-permute-start | bytes 1572872 | tf_op jit(solution)/shard_map/ppermute | solution.py:1040
  171.5 3.1 %collective-permute-start.24 = (bf16[128,128]{1,0:T(8,128)(2,1)S(1)}, bf16[128,128]{1,0:T(8,128)(2,1)S(1)}, u32[]{:S(2)}, u32[]{:S(2)}) collective-permute-start(bf16[128,128]{1,0:T(8,128)(2,1)S(1)} %get-tuple-element.181), channel_id=1, source_target_pairs={{0,2},{2,0},{4,6},{6,4},{8,10},{10,8},{12,14},{14,12},{1,3},{3,1},... | collective-permute-start | bytes 98312 | tf_op jit(solution)/shard_map/ppermute | solution.py:1043
  172.6 3.1 %collective-permute-start.25 = (bf16[128,128]{1,0:T(8,128)(2,1)S(1)}, bf16[128,128]{1,0:T(8,128)(2,1)S(1)}, u32[]{:S(2)}, u32[]{:S(2)}) collective-permute-start(bf16[128,128]{1,0:T(8,128)(2,1)S(1)} %get-tuple-element.183), channel_id=1, source_target_pairs={{0,4},{2,6},{4,0},{6,2},{8,12},{10,14},{12,8},{14,10},{1,5},{3,7},... | collective-permute-start | bytes 98312 | tf_op jit(solution)/shard_map/ppermute | solution.py:1043
  172.6 4.0 %collective-permute-start.26 = (bf16[128,128]{1,0:T(8,128)(2,1)S(1)}, bf16[128,128]{1,0:T(8,128)(2,1)S(1)}, u32[]{:S(2)}, u32[]{:S(2)}) collective-permute-start(bf16[128,128]{1,0:T(8,128)(2,1)S(1)} %get-tuple-element.182), channel_id=1, source_target_pairs={{0,6},{2,4},{4,2},{6,0},{8,14},{10,12},{12,10},{14,8},{1,7},{3,5},... | collective-permute-start | bytes 98312 | tf_op jit(solution)/shard_map/ppermute | solution.py:1043
  177.9 3.7 %collective-permute-start.27 = (bf16[128,128]{1,0:T(8,128)(2,1)S(1)}, bf16[128,128]{1,0:T(8,128)(2,1)S(1)}, u32[]{:S(2)}, u32[]{:S(2)}) collective-permute-start(bf16[128,128]{1,0:T(8,128)(2,1)S(1)} %add_convert_fusion.1), channel_id=1, source_target_pairs={{0,8},{2,10},{4,12},{6,14},{8,0},{10,2},{12,4},{14,6},{16,24},{18,... | collective-permute-start | bytes 98312 | tf_op jit(solution)/shard_map/ppermute | solution.py:1052
  177.9 8.2 %collective-permute-start.28 = (bf16[128,128]{1,0:T(8,128)(2,1)S(1)}, bf16[128,128]{1,0:T(8,128)(2,1)S(1)}, u32[]{:S(2)}, u32[]{:S(2)}) collective-permute-start(bf16[128,128]{1,0:T(8,128)(2,1)S(1)} %add_convert_fusion.1), channel_id=1, source_target_pairs={{0,16},{2,18},{4,20},{6,22},{8,24},{10,26},{12,28},{14,30},{16,0},... | collective-permute-start | bytes 98312 | tf_op jit(solution)/shard_map/ppermute | solution.py:1052
  178.2 8.0 %collective-permute-start.29 = (bf16[128,128]{1,0:T(8,128)(2,1)S(1)}, bf16[128,128]{1,0:T(8,128)(2,1)S(1)}, u32[]{:S(2)}, u32[]{:S(2)}) collective-permute-start(bf16[128,128]{1,0:T(8,128)(2,1)S(1)} %add_convert_fusion.1), channel_id=1, source_target_pairs={{0,24},{2,26},{4,28},{6,30},{8,16},{10,18},{12,20},{14,22},{16,8},... | collective-permute-start | bytes 98312 | tf_op jit(solution)/shard_map/ppermute | solution.py:1052
  186.3 9.9 %collective-permute-start.35 = (bf16[2,4,2,368,128]{4,3,2,1,0:T(8,128)(2,1)S(1)}, bf16[2,4,2,368,128]{4,3,2,1,0:T(8,128)(2,1)S(1)}, u32[]{:S(2)}, u32[]{:S(2)}) collective-permute-start(bf16[2,4,2,368,128]{4,3,2,1,0:T(8,128)(2,1)S(1)} %pad_maximum_fusion.1.own_core), channel_id=1, source_target_pairs={{0,1},{1,0},{2,3},{3,2},{4,5},{5,4},{6,7},{7,6},{8,9},{9,8},{10,11... | collective-permute-start | bytes 4521992 | tf_op jit(solution)/shard_map/ppermute | solution.py:1040
  189.1 14.4 %collective-permute-start.36 = (bf16[4,128,128]{2,1,0:T(8,128)(2,1)S(1)}, bf16[4,128,128]{2,1,0:T(8,128)(2,1)S(1)}, u32[]{:S(2)}, u32[]{:S(2)}) collective-permute-start(bf16[4,128,128]{2,1,0:T(8,128)(2,1)S(1)} %pad_maximum_fusion.8), channel_id=1, source_target_pairs={{0,2},{2,0},{4,6},{6,4},{8,10},{10,8},{12,14},{14,12},{1,3},{3,1},... | collective-permute-start | bytes 393224 | tf_op jit(solution)/shard_map/ppermute | solution.py:1043
  190.1 13.4 %collective-permute-start.37 = (bf16[4,128,128]{2,1,0:T(8,128)(2,1)S(1)}, bf16[4,128,128]{2,1,0:T(8,128)(2,1)S(1)}, u32[]{:S(2)}, u32[]{:S(2)}) collective-permute-start(bf16[4,128,128]{2,1,0:T(8,128)(2,1)S(1)} %pad_maximum_fusion.8), channel_id=1, source_target_pairs={{0,4},{2,6},{4,0},{6,2},{8,12},{10,14},{12,8},{14,10},{1,5},{3,7},... | collective-permute-start | bytes 393224 | tf_op jit(solution)/shard_map/ppermute | solution.py:1043
  190.5 13.1 %collective-permute-start.38 = (bf16[4,128,128]{2,1,0:T(8,128)(2,1)S(1)}, bf16[4,128,128]{2,1,0:T(8,128)(2,1)S(1)}, u32[]{:S(2)}, u32[]{:S(2)}) collective-permute-start(bf16[4,128,128]{2,1,0:T(8,128)(2,1)S(1)} %pad_maximum_fusion.8), channel_id=1, source_target_pairs={{0,6},{2,4},{4,2},{6,0},{8,14},{10,12},{12,10},{14,8},{1,7},{3,5},... | collective-permute-start | bytes 393224 | tf_op jit(solution)/shard_map/ppermute | solution.py:1043
  191.8 17.4 %collective-permute-start.23 = (bf16[256,1024]{1,0:T(8,128)(2,1)}, bf16[256,1024]{1,0:T(8,128)(2,1)}, u32[]{:S(2)}, u32[]{:S(2)}) collective-permute-start(bf16[256,1024]{1,0:T(8,128)(2,1)} %get-tuple-element.109), channel_id=1, source_target_pairs={{1,8},{3,10},{5,12},{7,14},{8,1},{10,3},{12,5},{14,7},{17,24},{19,... | collective-permute-start | bytes 1572872 | tf_op jit(solution)/shard_map/ppermute | solution.py:1037
  203.6 7.7 %collective-permute-start.39 = (bf16[1,4,4,128,128]{4,3,2,1,0:T(8,128)(2,1)S(1)}, bf16[1,4,4,128,128]{4,3,2,1,0:T(8,128)(2,1)}, u32[]{:S(2)}, u32[]{:S(2)}) collective-permute-start(bf16[1,4,4,128,128]{4,3,2,1,0:T(8,128)(2,1)S(1)} %maximum_bitcast_fusion.own_core), channel_id=1, source_target_pairs={{0,1},{1,0},{2,3},{3,2},{4,5},{5,4},{6,7},{7,6},{8,9},{9,8},{10,11... | collective-permute-start | bytes 1572872 | tf_op jit(solution)/shard_map/ppermute | solution.py:1040
  (12 other events, 40.3 us)
